TPU v7x, 128 devices: a whole 4x4x4 slice. The times are simulated.
128 devices in a mesh: batch: 2 (over x_lo), seq: 64 (over x_hi, z, y, core).
Axes of the slice: x: 4 (x_hi: 2, x_lo: 2; x = x_hi * 2 + x_lo), y: 4, z: 4, core: 2. Of those that a mesh axis runs over, the one named last changes fastest.
Arguments:
- tokens: bfloat16 [16384, 2048], P(('batch', 'seq')), may hold values from -8 to 8
- cotangent: bfloat16 [16384, 2048], P(('batch', 'seq')), may hold values from -6 to 6
- attn_gain: float32 [2048], replicated, may hold values from 0.1 to 1.9
- w_input: bfloat16 [2048, 2048], P(('batch', 'seq')), may hold values from -0.125 to 0.125
- w_forget: bfloat16 [2048, 2048], P(('batch', 'seq')), may hold values from -1 to 1
- w_outgate: bfloat16 [2048, 2048], P(('batch', 'seq')), may hold values from -0.125 to 0.125
- w_out: bfloat16 [2048, 2048], P(('batch', 'seq')), may hold values from -0.125 to 0.125
- norm_gain: float32 [2048], replicated, may hold values from 0.1 to 1.9
- mlp_gain: float32 [2048], replicated, may hold values from 0.1 to 1.9
- w_gate: bfloat16 [2048, 5632], P(('batch', 'seq')), may hold values from -0.125 to 0.125
- w_up: bfloat16 [2048, 5632], P(('batch', 'seq')), may hold values from -0.125 to 0.125
- w_down: bfloat16 [5632, 2048], P(('batch', 'seq')), may hold values from -0.078125 to 0.078125
- bound_table: float32 [24, 2048], replicated, may hold values from -4 to 4
- layer_idx: int32 [1], replicated, may hold values from 1 to 23
Outputs:
- result: bfloat16 [16384, 2048], P(('batch', 'seq'))
- grad_tokens: float32 [16384, 2048], P(('batch', 'seq'))
- grad_attn_gain: float32 [2048], replicated
- grad_w_input: float32 [2048, 2048], P(('batch', 'seq'))
- grad_w_forget: float32 [2048, 2048], P(('batch', 'seq'))
- grad_w_outgate: float32 [2048, 2048], P(('batch', 'seq'))
- grad_w_out: float32 [2048, 2048], P(('batch', 'seq'))
- grad_norm_gain: float32 [2048], replicated
- feedforward_gain_gradient: float32 [2048], replicated
- grad_w_gate: float32 [2048, 5632], P(('batch', 'seq'))
- grad_w_up: float32 [2048, 5632], P(('batch', 'seq'))
- grad_w_down: float32 [5632, 2048], P(('batch', 'seq'))
- grad_bound_table: float32 [24, 2048], replicated
All inputs are finite; a program needn't handle non-finite values.
Results may differ from a plain program's by a relative error of at most 0.009.
Values may be sent and summed in bfloat16 or wider, within the bound.
A program may use at most 704 MiB of HBM per device.

v0:
```python
import jax
import jax.numpy as jnp
from jax import lax
from jax.sharding import PartitionSpec as P

EPS = 1e-06


def entering(x, axis, combine, identity, reverse):
    devices, mine = (lax.axis_size(axis), lax.axis_index(axis))
    everything = jax.tree.map(lambda part: lax.all_gather(part, axis), x)
    start = jax.tree.map(
        lambda part, zero: jnp.broadcast_to(jnp.asarray(zero, part.dtype), part.shape), x, identity
    )

    def lap(k, before):
        at = devices - 1 - k if reverse else k
        reached = at > mine if reverse else at < mine
        new = combine(before, jax.tree.map(lambda part: part[at], everything))
        return jax.tree.map(lambda a, b: jnp.where(reached, a, b), new, before)

    return lax.fori_loop(0, devices, lap, start)


def norm_parts(field):
    rms_scale = lax.rsqrt(jnp.mean(field * field, axis=-1, keepdims=True) + EPS)
    return (field * rms_scale, rms_scale)


def norm_back(grad_normed, normed, rms_scale):
    return rms_scale * (
        grad_normed - normed * jnp.mean(grad_normed * normed, axis=-1, keepdims=True)
    )


def chain_link(earlier, later):
    return (earlier[0] * later[0], later[0] * earlier[1] + later[1])


def silu_slope(field):
    sigmoid_v = jax.nn.sigmoid(field)
    return sigmoid_v * (1.0 + field * (1.0 - sigmoid_v))


def bound_value(bound_table, layer_idx):
    probabilities = jax.nn.softmax(bound_table, axis=0)
    levels = jnp.arange(bound_table.shape[0], dtype=jnp.int32)[:, None]
    keep_mask = jnp.where((levels >= 1) & (levels <= layer_idx[0]), 1.0, 0.0).astype(jnp.float32)
    return jnp.sum(probabilities * keep_mask, axis=0)


def mat_dot(left_side, right_side):
    return jnp.dot(left_side, right_side, preferred_element_type=jnp.float32)


def dot_trans(left_side, right_side):
    return lax.dot_general(
        left_side, right_side, (((1,), (1,)), ((), ())), preferred_element_type=jnp.float32
    )


def dot_left(left_side, right_side):
    return lax.dot_general(
        left_side, right_side, (((0,), (0,)), ((), ())), preferred_element_type=jnp.float32
    )


def on_device(
    tokens,
    cotangent,
    attn_gain,
    w_input,
    w_forget,
    w_outgate,
    w_out,
    norm_gain,
    mlp_gain,
    w_gate,
    w_up,
    w_down,
    bound_table,
    layer_idx,
):
    model_width = tokens.shape[1]
    inner_hidden_width = w_gate.shape[1]
    gathered = (
        lax.all_gather(w_input, ("batch", "seq"), axis=0, tiled=True),
        lax.all_gather(w_forget, ("batch", "seq"), axis=0, tiled=True),
        lax.all_gather(w_outgate, ("batch", "seq"), axis=0, tiled=True),
        lax.all_gather(w_out, ("batch", "seq"), axis=0, tiled=True),
        lax.all_gather(w_gate, ("batch", "seq"), axis=0, tiled=True),
        lax.all_gather(w_up, ("batch", "seq"), axis=0, tiled=True),
        lax.all_gather(w_down, ("batch", "seq"), axis=0, tiled=True),
    )
    big_input, big_forget, big_outgate, big_out, big_gate, big_up, big_down = gathered
    residual_in = tokens.astype(jnp.float32)
    first_norm, first_scale = norm_parts(residual_in)
    first_in = (first_norm * attn_gain).astype(jnp.bfloat16)
    proj_in = mat_dot(first_in, big_input)
    proj_forget = mat_dot(first_in, big_forget)
    proj_gate = mat_dot(first_in, big_outgate)
    lower_bound = bound_value(bound_table, layer_idx)
    sigmoid_f = jax.nn.sigmoid(proj_forget)
    forget = lower_bound + (1.0 - lower_bound) * sigmoid_f
    act_in = jax.nn.silu(proj_in)
    inputs = act_in * (1.0 - forget)
    decay_run, local_run = lax.associative_scan(chain_link, (forget, inputs), axis=0)
    identity = (jnp.ones((model_width,), jnp.float32), jnp.zeros((model_width,), jnp.float32))
    before = entering((decay_run[-1], local_run[-1]), "seq", chain_link, identity, False)
    carry_in = before[1]
    states = local_run + decay_run * carry_in
    state_norm, state_scale = norm_parts(states)
    act_gate = jax.nn.silu(proj_gate)
    gated = (state_norm * norm_gain * act_gate).astype(jnp.bfloat16)
    residual_mid = residual_in + mat_dot(gated, big_out)
    second_norm, second_scale = norm_parts(residual_mid)
    second_in = (second_norm * mlp_gain).astype(jnp.bfloat16)
    gate_proj = mat_dot(second_in, big_gate)
    up_proj = mat_dot(second_in, big_up)
    act_mlp = jax.nn.silu(gate_proj)
    hidden = (act_mlp * up_proj).astype(jnp.bfloat16)
    result = (residual_mid + mat_dot(hidden, big_down)).astype(jnp.bfloat16)
    again = (
        lax.all_gather(w_input, ("batch", "seq"), axis=0, tiled=True),
        lax.all_gather(w_forget, ("batch", "seq"), axis=0, tiled=True),
        lax.all_gather(w_outgate, ("batch", "seq"), axis=0, tiled=True),
        lax.all_gather(w_out, ("batch", "seq"), axis=0, tiled=True),
        lax.all_gather(w_gate, ("batch", "seq"), axis=0, tiled=True),
        lax.all_gather(w_up, ("batch", "seq"), axis=0, tiled=True),
        lax.all_gather(w_down, ("batch", "seq"), axis=0, tiled=True),
    )
    big_input, big_forget, big_outgate, big_out, big_gate, big_up, big_down = again
    grad_result = cotangent.astype(jnp.float32)
    grad_hidden = dot_trans(cotangent, big_down)
    grad_gate = (grad_hidden * up_proj * silu_slope(gate_proj)).astype(jnp.bfloat16)
    grad_up = (grad_hidden * act_mlp).astype(jnp.bfloat16)
    grad_second = dot_trans(grad_gate, big_gate) + dot_trans(grad_up, big_up)
    feedforward_gain_gradient = jnp.sum(grad_second * second_norm, axis=0)
    grad_mixed = grad_result + norm_back(grad_second * mlp_gain, second_norm, second_scale)
    grad_branch = grad_mixed.astype(jnp.bfloat16)
    grad_gated = dot_trans(grad_branch, big_out)
    grad_norm_gain = jnp.sum(grad_gated * state_norm * act_gate, axis=0)
    grad_proj_gate = (grad_gated * state_norm * norm_gain * silu_slope(proj_gate)).astype(
        jnp.bfloat16
    )
    grad_states = norm_back(grad_gated * norm_gain * act_gate, state_norm, state_scale)
    next_forget = jnp.concatenate((forget[1:], jnp.ones((1, model_width), jnp.float32)), axis=0)
    back_decay, back_local = lax.associative_scan(
        chain_link, (next_forget, grad_states), reverse=True, axis=0
    )
    after = entering((decay_run[-1], forget[0] * back_local[0]), "seq", chain_link, identity, True)
    grad_inputs = back_local + back_decay * after[1]
    prev_states = jnp.concatenate((carry_in[None, :], states[:-1]), axis=0)
    grad_forget = grad_inputs * (prev_states - act_in)
    grad_proj_in = (grad_inputs * (1.0 - forget) * silu_slope(proj_in)).astype(jnp.bfloat16)
    grad_proj_forget = (grad_forget * (1.0 - lower_bound) * sigmoid_f * (1.0 - sigmoid_f)).astype(
        jnp.bfloat16
    )
    grad_lower = jnp.sum(grad_forget * (1.0 - sigmoid_f), axis=0)
    unused, pullback = jax.vjp(lambda table: bound_value(table, layer_idx), bound_table)
    grad_table = pullback(grad_lower)[0]
    grad_first = (
        dot_trans(grad_proj_in, big_input)
        + dot_trans(grad_proj_forget, big_forget)
        + dot_trans(grad_proj_gate, big_outgate)
    )
    grad_attn_gain = jnp.sum(grad_first * first_norm, axis=0)
    grad_tokens = grad_mixed + norm_back(grad_first * attn_gain, first_norm, first_scale)
    grad_mixer = jnp.concatenate((grad_proj_in, grad_proj_forget, grad_proj_gate), axis=1)
    grad_ffn_in = jnp.concatenate((grad_gate, grad_up), axis=1)

    def column_part(left_side, right_side):
        return dot_left(left_side, right_side)

    summed = lax.psum_scatter(
        jnp.concatenate(
            (
                column_part(first_in, grad_mixer),
                column_part(gated, grad_branch),
                column_part(second_in, grad_ffn_in),
            ),
            axis=1,
        ),
        ("batch", "seq"),
        scatter_dimension=0,
        tiled=True,
    )
    grad_w_down = lax.psum_scatter(
        dot_left(hidden, cotangent), ("batch", "seq"), scatter_dimension=0, tiled=True
    )
    totals = lax.psum(
        (grad_attn_gain, grad_norm_gain, feedforward_gain_gradient, grad_table), ("batch", "seq")
    )
    width_two = 2 * model_width
    width_three = 3 * model_width
    width_four = 4 * model_width
    grad_w_input = summed[:, :model_width]
    grad_w_forget = summed[:, model_width:width_two]
    grad_w_outgate = summed[:, width_two:width_three]
    grad_w_out = summed[:, width_three:width_four]
    grad_w_gate = summed[:, width_four : width_four + inner_hidden_width]
    grad_w_up = summed[:, width_four + inner_hidden_width :]
    return (
        result,
        grad_tokens,
        totals[0],
        grad_w_input,
        grad_w_forget,
        grad_w_outgate,
        grad_w_out,
        totals[1],
        totals[2],
        grad_w_gate,
        grad_w_up,
        grad_w_down,
        totals[3],
    )


def solution(mesh):
    return jax.shard_map(
        on_device,
        mesh=mesh,
        in_specs=(
            P(("batch", "seq"), None),
            P(("batch", "seq"), None),
            P(),
            P(("batch", "seq"), None),
            P(("batch", "seq"), None),
            P(("batch", "seq"), None),
            P(("batch", "seq"), None),
            P(),
            P(),
            P(("batch", "seq"), None),
            P(("batch", "seq"), None),
            P(("batch", "seq"), None),
            P(),
            P(),
        ),
        out_specs=(
            P(("batch", "seq"), None),
            P(("batch", "seq"), None),
            P(),
            P(("batch", "seq"), None),
            P(("batch", "seq"), None),
            P(("batch", "seq"), None),
            P(("batch", "seq"), None),
            P(),
            P(),
            P(("batch", "seq"), None),
            P(("batch", "seq"), None),
            P(("batch", "seq"), None),
            P(),
        ),
        check_vma=False,
    )
```

profile of v0, /device:TPU:1, one launch (start us, length us, event | category | flops | bytes accessed | tf_op | source)
XLA Modules:
  0.0 3447.4 jit_solution(5994467230520173235)
XLA Ops:
  17.5 198.3 %all-gather.14.cloned.1.call-done = bf16[2048,2048]{1,0:T(8,128)(2,1)} async-done(((bf16[16,2048]{1,0:T(8,128)(2,1)}), bf16[2048,2048]{1,0:T(8,128)(2,1)}) %all-gather.14.cloned.1.call-update) | async-done | bytes 8388624 | tf_op jit(solution)/shard_map/all_gather | solution.py:88
  220.8 198.4 %all-gather.12.cloned.1.call-done = bf16[2048,2048]{1,0:T(8,128)(2,1)} async-done(((bf16[16,2048]{1,0:T(8,128)(2,1)}), bf16[2048,2048]{1,0:T(8,128)(2,1)}) %all-gather.12.cloned.1.call-update) | async-done | bytes 8388624 | tf_op jit(solution)/shard_map/all_gather | solution.py:87
  488.3 95.3 %all-gather = f32[64,1,2048]{2,1,0:T(1,128)S(1)} all-gather(f32[1,1,2048]{2,1,0:T(1,128)S(1)} %add_bitcast_fusion.1), channel_id=1, replica_groups=mesh['batch'=2,'seq'=64] {'seq'}, dimensions={0}, use_global_device_ids=true | all-gather | bytes 532480 | tf_op jit(solution)/shard_map/all_gather | solution.py:11
  592.0 90.3 %all-gather.1 = f32[64,1,2048]{2,1,0:T(1,128)S(1)} all-gather(f32[1,1,2048]{2,1,0:T(1,128)S(1)} %add_bitcast_fusion), channel_id=1, replica_groups=mesh['batch'=2,'seq'=64] {'seq'}, dimensions={0}, use_global_device_ids=true | all-gather | bytes 532480 | tf_op jit(solution)/shard_map/all_gather | solution.py:11
  704.8 59.9 %while.30 = (s32[]{:T(128)}, f32[2048]{0:T(1024)S(1)}, s32[]{:T(128)}, f32[64,2048]{1,0:T(8,128)}, f32[64,2048]{1,0:T(8,128)}, /*index=5*/s32[]{:T(128)}, s32[]{:T(128)}) while((s32[]{:T(128)}, f32[2048]{0:T(1024)S(1)}, s32[]{:T(128)}, f32[64,2048]{1,0:T(8,128)}, f32[64,2048]{1,0:T(8,128)}, /*index=5*/s32[]{:T(128)}, ...), condition=%wide.region_5.6_spmd.clone, body=%wide.region_4.5_spmd.clone.sunk | while | flops 8196 | bytes 65645 | solution.py:22
  773.7 52.3 %all-gather.18.cloned.1.call-done = bf16[2048,2048]{1,0:T(8,128)(2,1)} async-done(((bf16[16,2048]{1,0:T(8,128)(2,1)}), bf16[2048,2048]{1,0:T(8,128)(2,1)}) %all-gather.18.cloned.1.call-update) | async-done | bytes 8388624 | tf_op jit(solution)/shard_map/all_gather | solution.py:90
  830.9 222.7 %all-gather.24.cloned.1.call-done = bf16[128,44,2048]{2,1,0:T(8,128)(2,1)} async-done(((bf16[1,44,2048]{2,1,0:T(8,128)(2,1)}), bf16[128,44,2048]{2,1,0:T(8,128)(2,1)}) %all-gather.24.cloned.1.call-update) | async-done | bytes 23068688 | tf_op jit(solution)/shard_map/all_gather | solution.py:93
  1053.6 29.8 reshape.101
  1083.4 195.2 %all-gather.22.cloned.1.call-done = bf16[2048,5632]{1,0:T(8,128)(2,1)} async-done(((bf16[16,5632]{1,0:T(8,128)(2,1)}), bf16[2048,5632]{1,0:T(8,128)(2,1)}) %all-gather.22.cloned.1.call-update) | async-done | bytes 23068688 | tf_op jit(solution)/shard_map/all_gather | solution.py:92
  1278.6 12.4 fusion.79
  1290.9 212.5 %all-gather.20.cloned.1.call-done = bf16[2048,5632]{1,0:T(8,128)(2,1)} async-done(((bf16[16,5632]{1,0:T(8,128)(2,1)}), bf16[2048,5632]{1,0:T(8,128)(2,1)}) %all-gather.20.cloned.1.call-update) | async-done | bytes 23068688 | tf_op jit(solution)/shard_map/all_gather | solution.py:91
  1503.4 12.3 fusion.78
  1515.7 15.6 multiply_convert_fusion
  1531.4 13.1 fusion.80
  1544.5 14.1 multiply_reduce_fusion.1
  1560.3 9.0 multiply_reduce_fusion.2
  1628.1 8.5 slice.577
  1693.5 9.5 fusion.34
  1703.1 33.4 fusion.1
  1737.6 9.0 rev.8
  1746.5 94.6 %all-gather.3 = f32[64,1,2048]{2,1,0:T(1,128)S(1)} all-gather(f32[1,1,2048]{2,1,0:T(1,128)S(1)} %fusion.57), channel_id=1, replica_groups=mesh['batch'=2,'seq'=64] {'seq'}, dimensions={0}, use_global_device_ids=true | all-gather | bytes 532480 | tf_op jit(solution)/shard_map/all_gather | solution.py:11
  1842.1 60.3 %while.31 = (s32[]{:T(128)}, f32[2048]{0:T(1024)S(1)}, s32[]{:T(128)}, f32[64,2048]{1,0:T(8,128)}, f32[64,2048]{1,0:T(8,128)}, /*index=5*/s32[]{:T(128)}, s32[]{:T(128)}, s32[]{:T(128)}, s32[]{:T(128)}) while((s32[]{:T(128)}, f32[2048]{0:T(1024)S(1)}, s32[]{:T(128)}, f32[64,2048]{1,0:T(8,128)}, f32[64,2048]{1,0:T(8,128)}, ...), condition=%wide.region_11.12_spmd.clone, body=%wide.region_10.11_spmd.clone.sunk | while | flops 8200 | bytes 65707 | solution.py:22
  1912.5 8.9 rev.9
  1925.2 20.6 fusion.10
  1945.8 102.0 %pad_maximum_fusion = f32[2048,19456]{1,0:T(8,128)} fusion(f32[2048,11264]{1,0:T(8,128)} %fusion.1, f32[2048,2048]{1,0:T(8,128)} %fusion.34, f32[2048,6144]{1,0:T(8,128)} %fusion.10), kind=kLoop, calls=%fused_computation.6 | loop fusion | flops 79691776 | bytes 318767104 | tf_op jit(solution)/shard_map/concatenate | solution.py:176
  2049.3 18.5 fusion.82
  2067.8 542.7 %fusion = f32[48,2048]{1,0:T(8,128)S(1)} fusion(f32[5632,2048]{1,0:T(8,128)} %fusion.82), kind=kCustom, calls=%all-reduce-scatter | all-reduce-scatter fusion | flops 12582913 | bytes 46530560
  2631.2 11.7 fusion.9
  2667.7 613.9 %all-reduce.60 = (f32[2048]{0:T(1024)}, f32[2048]{0:T(1024)}, f32[2048]{0:T(1024)}) all-reduce(f32[2048]{0:T(1024)S(1)} %get-tuple-element.281, f32[2048]{0:T(1024)S(1)} %copy-done.53, f32[2048]{0:T(1024)S(1)} %copy-done.42), channel_id=1, replica_groups=mesh['batch'=2,'seq'=64] {'batch','seq'}, use_global_device_ids=true, to_apply=%region_14.15 | all-reduce | flops 6144 | bytes 49152 | tf_op jit(solution)/shard_map/psum | solution.py:191
  3304.9 8.5 collective-permute-done.1
  3320.1 30.7 concatenate.116
  3356.5 82.4 %all-reduce.63.cloned.1.call-done = f32[24,2048]{1,0:T(8,128)} async-done(((f32[24,2048]{1,0:T(8,128)}), f32[24,2048]{1,0:T(8,128)}) %all-reduce.63.cloned.1.call-update) | async-done | bytes 196624 | tf_op jit(solution)/shard_map/psum | solution.py:191
  (673 shorter events, 460.5 us)
Async XLA Ops:
  7.2 208.6 %all-gather.14.cloned.1.call-start = ((), (), s32[]{:S(2)}) async-start(), calls=%async_computation.2 | async-start | bytes 8454144 | tf_op jit(solution)/shard_map/all_gather | solution.py:88
  7.9 411.3 %all-gather.12.cloned.1.call-start = ((), (), s32[]{:S(2)}) async-start(), calls=%async_computation.1 | async-start | bytes 8454144 | tf_op jit(solution)/shard_map/all_gather | solution.py:87
  8.7 758.7 %all-gather.16.cloned.1.call-start = ((), (), s32[]{:S(2)}) async-start(), calls=%async_computation.3 | async-start | bytes 8454144 | tf_op jit(solution)/shard_map/all_gather | solution.py:89
  9.4 816.6 %all-gather.18.cloned.1.call-start = ((), (), s32[]{:S(2)}) async-start(), calls=%async_computation.4 | async-start | bytes 8454144 | tf_op jit(solution)/shard_map/all_gather | solution.py:90
  10.0 1043.6 %all-gather.24.cloned.1.call-start = ((), (), s32[]{:S(2)}) async-start(), calls=%async_computation.9 | async-start | bytes 25362432 | tf_op jit(solution)/shard_map/all_gather | solution.py:93
  10.6 1268.0 %all-gather.22.cloned.1.call-start = ((), (), s32[]{:S(2)}) async-start(), calls=%async_computation.6 | async-start | bytes 23248896 | tf_op jit(solution)/shard_map/all_gather | solution.py:92
  11.1 1492.3 %all-gather.20.cloned.1.call-start = ((), (), s32[]{:S(2)}) async-start(), calls=%async_computation.5 | async-start | bytes 23248896 | tf_op jit(solution)/shard_map/all_gather | solution.py:91
  11.9 3340.7 %reduce-scatter.4.cloned.1.call-start = ((), (), s32[]{:S(2)}) async-start(), calls=%async_computation.7 | async-start | bytes 160628736 | tf_op jit(solution)/shard_map/reduce_scatter | solution.py:175
  17.4 401.8 %copy-start.48 = (f32[128]{0:T(128)}, f32[128]{0:T(128)S(1)}, u32[]{:S(2)}) copy-start(f32[128]{0:T(128)S(1)} %add_rsqrt_fusion.2) | copy-start | bytes 1540
  17.5 401.7 %copy-start.43 = (f32[2048]{0:T(1024)}, f32[2048]{0:T(1024)S(1)}, u32[]{:S(2)}) copy-start(f32[2048]{0:T(1024)S(1)} %broadcast_subtract_fusion) | copy-start | bytes 24580
  17.5 401.7 %copy-start.2 = (bf16[128,2048]{1,0:T(8,128)(2,1)S(1)}, bf16[128,2048]{1,0:T(8,128)(2,1)}, u32[]{:S(2)}) copy-start(bf16[128,2048]{1,0:T(8,128)(2,1)} %param.18) | copy-start | bytes 1572868
  17.5 401.7 %copy-start.33 = (f32[2048]{0:T(1024)S(1)}, f32[2048]{0:T(1024)}, u32[]{:S(2)}) copy-start(f32[2048]{0:T(1024)} %param.20) | copy-start | bytes 24580
  485.2 282.2 %copy-start.52 = (f32[2048]{0:T(1024)S(1)}, f32[2048]{0:T(1024)}, u32[]{:S(2)}) copy-start(f32[2048]{0:T(1024)} %param.25) | copy-start | bytes 24580
  830.7 727.8 %copy-start = (f32[128,2048]{1,0:T(8,128)}, f32[128,2048]{1,0:T(8,128)S(1)}, u32[]{:S(2)}) copy-start(f32[128,2048]{1,0:T(8,128)S(1)} %get-tuple-element.391) | copy-start | bytes 3145732
  2047.8 1391.0 %all-reduce.63.cloned.1.call-start = ((), (), s32[]{:S(2)}) async-start(), calls=%async_computation.8 | async-start | bytes 393216 | tf_op jit(solution)/shard_map/psum | solution.py:191
  2067.8 555.7 %copy-start.11 = (f32[24,2048]{1,0:T(8,128)S(1)}, f32[24,2048]{1,0:T(8,128)}, u32[]{:S(2)}) copy-start(f32[24,2048]{1,0:T(8,128)} %param.30) | copy-start | bytes 589828
  2067.8 555.7 %copy-start.37 = (f32[2048]{0:T(1024)S(1)}, f32[2048]{0:T(1024)}, u32[]{:S(2)}) copy-start(f32[2048]{0:T(1024)} %copy-done.36) | copy-start | bytes 24580
  2067.8 555.7 %copy-start.41 = (f32[2048]{0:T(1024)S(1)}, f32[2048]{0:T(1024)}, u32[]{:S(2)}) copy-start(f32[2048]{0:T(1024)} %get-tuple-element.306) | copy-start | bytes 24580
  2067.8 555.7 %copy-start.55 = (f32[24]{0:T(128)S(1)}, f32[24]{0:T(128)}, u32[]{:S(2)}) copy-start(f32[24]{0:T(128)} %copy-done.54) | copy-start | bytes 292
  2067.8 563.4 %copy-start.1 = (f32[128,2048]{1,0:T(8,128)S(1)}, f32[128,2048]{1,0:T(8,128)}, u32[]{:S(2)}) copy-start(f32[128,2048]{1,0:T(8,128)} %copy-done) | copy-start | bytes 3145732
  2611.2 670.4 %collective-permute-start.9 = (f32[48,2048]{1,0:T(8,128)S(1)}, f32[48,2048]{1,0:T(8,128)}, u32[]{:S(2)}, u32[]{:S(2)}) collective-permute-start(f32[48,2048]{1,0:T(8,128)S(1)} %fusion), channel_id=1, source_target_pairs={{0,10},{1,11},{2,12},{3,13},{4,14},{5,15},{6,16},{7,17},{8,18},{9,... | collective-permute-start | bytes 1179656
  2613.3 671.4 %collective-permute-start.8 = (f32[48,2048]{1,0:T(8,128)S(1)}, f32[48,2048]{1,0:T(8,128)}, u32[]{:S(2)}, u32[]{:S(2)}) collective-permute-start(f32[48,2048]{1,0:T(8,128)S(1)} %fusion), channel_id=1, source_target_pairs={{0,9},{1,10},{2,11},{3,12},{4,13},{5,14},{6,15},{7,16},{8,17},{9,1... | collective-permute-start | bytes 1179656
  2615.3 672.1 %collective-permute-start.7 = (f32[48,2048]{1,0:T(8,128)S(1)}, f32[48,2048]{1,0:T(8,128)}, u32[]{:S(2)}, u32[]{:S(2)}) collective-permute-start(f32[48,2048]{1,0:T(8,128)S(1)} %fusion), channel_id=1, source_target_pairs={{0,8},{1,9},{2,10},{3,11},{4,12},{5,13},{6,14},{7,15},{8,16},{9,17... | collective-permute-start | bytes 1179656
  2617.4 674.3 %collective-permute-start.6 = (f32[48,2048]{1,0:T(8,128)S(1)}, f32[48,2048]{1,0:T(8,128)}, u32[]{:S(2)}, u32[]{:S(2)}) collective-permute-start(f32[48,2048]{1,0:T(8,128)S(1)} %fusion), channel_id=1, source_target_pairs={{0,7},{1,8},{2,9},{3,10},{4,11},{5,12},{6,13},{7,14},{8,15},{9,16}... | collective-permute-start | bytes 1179656
  2623.7 32.5 collective-permute-start.10
  2656.1 641.4 %copy-start.8 = (f32[128,2048]{1,0:T(8,128)S(1)}, f32[128,2048]{1,0:T(8,128)}, u32[]{:S(2)}) copy-start(f32[128,2048]{1,0:T(8,128)} %copy-done.7) | copy-start | bytes 3145732
  2656.2 638.5 %collective-permute-start.5 = (f32[48,2048]{1,0:T(8,128)S(1)}, f32[48,2048]{1,0:T(8,128)S(1)}, u32[]{:S(2)}, u32[]{:S(2)}) collective-permute-start(f32[48,2048]{1,0:T(8,128)S(1)} %fusion), channel_id=1, source_target_pairs={{0,6},{1,7},{2,8},{3,9},{4,10},{5,11},{6,12},{7,13},{8,14},{9,15},... | collective-permute-start | bytes 1179656
  3281.7 17.2 collective-permute-start.4
  3284.7 14.1 collective-permute-start.3
  3287.4 17.5 collective-permute-start.2
  3291.8 21.6 collective-permute-start.1
  3294.6 25.5 collective-permute-start
  (46 other events, 1846.5 us)
Sparse Core Ops, SparseCore 0:
  9.7 206.0 all-gather.13
  217.5 201.5 all-gather.11
  420.9 201.7 all-gather.15
  624.2 201.6 all-gather.17
  827.5 226.0 all-gather.23
  1055.2 223.3 all-gather.21
  1280.3 223.1 all-gather.19
  2048.0 1170.1 reduce-scatter.3
  3223.4 215.4 all-reduce.62
where the time goes:
time: 3470 us; the launch traced here: 3450 us
  blocking collectives  1440 us (41%)
  waiting for transfers between devices  1190 us (34%)
  local copies, waits for them, and re-layouts  375 us (11%)
  matrix products  208 us (6%)
  other arithmetic  176 us (5%)
  starting transfers between devices  43.6 us (1%)
    psum x1, blocking collectives, on_device(): lax.psum((grad_attn_gain, grad_norm_gain, feedforward_gain_gradient, grad...  614 us
    unnamed x1, blocking collectives  543 us
    all_gather x3, blocking collectives, entering(): everything = jax.tree.map(lambda part: lax.all_gather(part, axis), x)  280 us
    all_gather x1, waiting for transfers between devices, on_device(): lax.all_gather(w_down, ('batch', 'seq'), axis=0, tiled=True)  223 us
    all_gather x1, waiting for transfers between devices, on_device(): lax.all_gather(w_gate, ('batch', 'seq'), axis=0, tiled=True)  213 us
    all_gather x1, waiting for transfers between devices, on_device(): lax.all_gather(w_input, ('batch', 'seq'), axis=0, tiled=True)  198 us
    all_gather x1, waiting for transfers between devices, on_device(): lax.all_gather(w_forget, ('batch', 'seq'), axis=0, tiled=True)  198 us
    all_gather x1, waiting for transfers between devices, on_device(): lax.all_gather(w_up, ('batch', 'seq'), axis=0, tiled=True)  195 us
  transfers between devices with their start and end apart: 20, of which 10 were waited for; matrix products, arithmetic and copies ran while one was open for 25% of the time, Pallas kernels for 0%

commit v1 on v0

v1 whole, which is shorter than its diff:
```python
import functools

import jax
import jax.numpy as jnp
from jax import lax
from jax.experimental import pallas as pl
from jax.experimental.pallas import tpu as pltpu
from jax.sharding import Mesh, PartitionSpec as P

EPS = 1e-06
BF = jnp.bfloat16
F32 = jnp.float32
AXES = ("xlo", "xhi", "z", "y", "core")
MESH = pl.DeviceIdType.MESH
ANY = pl.BlockSpec(memory_space=pl.ANY)
VMEM = pl.BlockSpec(memory_space=pltpu.VMEM)
STEPS = (1, 3, 2)
GROUP = [(a, b) for a in range(4) for b in range(2) if a or b]
CHAIN = [(a, b) for a in range(2) for b in range(4) if a or b]
PLANE = [(a, b) for a in range(4) for b in range(4) if a or b]
HIGH = lax.Precision.HIGHEST


def ax(name):
    return lax.axis_index(name)


def ring(axis, s):
    if axis == "x":
        x = lax.rem(ax("xhi") * 2 + ax("xlo") + s, 4)
        return {"xhi": lax.div(x, 2), "xlo": lax.rem(x, 2)}
    return {axis: lax.rem(ax(axis) + s, 4)}


def sibling():
    return {"core": 1 - ax("core")}


def in_group(s, t):
    return {"y": lax.rem(ax("y") + s, 4), "core": lax.rem(ax("core") + t, 2)}


def in_chain(s, t):
    return {"xhi": lax.rem(ax("xhi") + s, 2), "z": lax.rem(ax("z") + t, 4)}


def in_plane(s, t):
    return {**ring("x", s), **ring("z", t)}


def place():
    return ax("xlo") * 8 + ax("xhi") * 4 + ax("z"), ax("y") * 2 + ax("core")


def device(p, g):
    return {
        "xlo": lax.div(p, 8),
        "xhi": lax.rem(lax.div(p, 4), 2),
        "z": lax.rem(p, 4),
        "y": lax.div(g, 2),
        "core": lax.rem(g, 2),
    }


class Copies:
    def __init__(self, send, recv, near):
        self.sems = (send, recv, near)
        self.count = 0
        self.locals = 0
        self.open = []

    def remote(self, src, dst, dev):
        i = self.count
        self.count += 1
        return pltpu.make_async_remote_copy(
            src_ref=src,
            dst_ref=dst,
            send_sem=self.sems[0].at[i],
            recv_sem=self.sems[1].at[i],
            device_id=dev,
            device_id_type=MESH,
        )

    def send(self, src, dst, dev):
        copy = self.remote(src, dst, dev)
        copy.start()
        self.open.append(copy)
        return copy

    def local(self, src, dst):
        copy = pltpu.make_async_copy(src, dst, self.sems[2].at[self.locals])
        self.locals += 1
        copy.start()
        return copy

    def finish(self):
        for copy in self.open:
            copy.wait_send()


def greet(peers, shuffle=None):
    bar = pltpu.get_barrier_semaphore()
    for dev in peers:
        pl.semaphore_signal(bar, inc=1, device_id=dev, device_id_type=MESH)
    count = len(peers)
    if shuffle is not None:
        source, from_me, to_me = shuffle

        @pl.when(jnp.logical_not(from_me))
        def _():
            pl.semaphore_signal(bar, inc=1, device_id=source, device_id_type=MESH)

        count = count + jnp.where(to_me, 0, 1)
    pl.semaphore_wait(bar, count)


def rings():
    return [ring("x", s) for s in STEPS] + [ring("z", s) for s in STEPS]


def ys():
    return [ring("y", s) for s in STEPS] + [sibling()]


def run(chains, order):
    for i in order:
        next(chains[i], None)
    for chain in chains:
        for _ in chain:
            pass


def rows_of(i, n=16):
    return pl.ds(pl.multiple_of(i * n, n), n)


def group_gather(cp, src, full):
    g = place()[1]
    own = cp.local(src, full.at[g])
    moved = {s: cp.send(src, full.at[g], ring("y", s)) for s in STEPS}
    near = [cp.send(src, full.at[g], sibling())]
    yield
    for s in STEPS:
        moved[s].wait_recv()
        k = 2 * lax.rem(ax("y") + 4 - s, 4) + ax("core")
        near.append(cp.send(full.at[k], full.at[k], sibling()))
    yield
    for copy in near:
        copy.wait_recv()
    own.wait()


def group_sum(cp, part, mine, near, far, out):
    c = ax("core")
    block = {s: 2 * lax.rem(ax("y") + s, 4) for s in range(4)}
    sent = {s: cp.send(part.at[block[s] + 1 - c], near.at[s], sibling()) for s in (2, 1, 3, 0)}
    own = {s: cp.local(part.at[block[s] + c], mine.at[s]) for s in (2, 1, 3, 0)}
    yield
    moved = {}
    for s in (2, 1, 3):
        own[s].wait()
        sent[s].wait_recv()

        def add(i, carry, s=s):
            r = rows_of(i)
            mine[s, r, :] = (mine[s, r, :].astype(F32) + near[s, r, :].astype(F32)).astype(BF)
            return carry

        lax.fori_loop(0, mine.shape[1] // 16, add, 0)
        moved[s] = cp.send(mine.at[s], far.at[s - 1], ring("y", s))
    own[0].wait()
    sent[0].wait_recv()
    yield
    for s in (1, 3, 2):
        moved[s].wait_recv()

    def total(r):
        acc = mine[0, r, :].astype(F32) + near[0, r, :].astype(F32)
        for s in range(3):
            acc = acc + far[s, r, :].astype(F32)
        return acc

    out.append(total)


def group_sum_scratch(rows, width):
    return [
        pltpu.VMEM((4, rows, width), BF),
        pltpu.VMEM((4, rows, width), BF),
        pltpu.VMEM((3, rows, width), BF),
    ]


def plane_gather(cp, buf, halves):
    me = (ax("xlo"), ax("xhi"), ax("z"))

    def view(h, *at):
        return buf.at[at + halves[h]]

    first = []
    for s in STEPS:
        first.append(cp.send(view(0, *me), view(0, *me), ring("z", s)))
        first.append(cp.send(view(1, *me), view(1, *me), ring("x", s)))
    yield
    for copy in first:
        copy.wait_recv()
    column = view(0, me[0], me[1], pl.ds(0, 4))
    row = view(1, pl.ds(0, 2), pl.ds(0, 2), me[2])
    wide = {}
    for s in (1, 3):
        wide["x", s] = cp.send(column, column, ring("x", s))
        wide["z", s] = cp.send(row, row, ring("z", s))
    yield
    last = []
    for s in (1, 3):
        back = ring("x", 4 - s)
        wide["x", s].wait_recv()
        v = view(0, back["xlo"], back["xhi"], pl.ds(0 if s == 1 else 2, 2))
        last.append(cp.send(v, v, ring("x", s)))
        back = ring("z", 4 - s)
        wide["z", s].wait_recv()
        v = view(1, 0 if s == 1 else 1, pl.ds(0, 2), back["z"])
        last.append(cp.send(v, v, ring("z", s)))
    yield
    for copy in last:
        copy.wait_recv()


def half_shapes(halves):
    return [tuple(d.size for d in h) for h in halves]


def plane_sum_scratch(halves):
    a, b = half_shapes(halves)
    return [
        pltpu.VMEM((4,) + a, BF),
        pltpu.VMEM((3, 4) + a, BF),
        pltpu.VMEM((3,) + a, BF),
        pltpu.VMEM((2, 2) + b, BF),
        pltpu.VMEM((3, 2, 2) + b, BF),
        pltpu.VMEM((3,) + b, BF),
    ]


def plane_sum(cp, part, halves, own_a, far_a, last_a, own_b, far_b, last_b, out):
    me = (ax("xlo"), ax("xhi"), ax("z"))
    shape_a, shape_b = half_shapes(halves)

    def view(h, *at):
        return part.at[at + halves[h]]

    near_a = cp.local(view(0, me[0], me[1], pl.ds(0, 4)), own_a)
    near_b = cp.local(view(1, pl.ds(0, 2), pl.ds(0, 2), me[2]), own_b)
    first_a, first_b = [], []
    for j, s in enumerate(STEPS):
        d = ring("x", s)
        first_a.append(cp.send(view(0, d["xlo"], d["xhi"], pl.ds(0, 4)), far_a.at[j], d))
        d = ring("z", s)
        first_b.append(cp.send(view(1, pl.ds(0, 2), pl.ds(0, 2), d["z"]), far_b.at[j], d))
    yield
    near_a.wait()
    for copy in first_a:
        copy.wait_recv()
    for k in range(4):

        def add(i, carry, k=k):
            r = rows_of(i)
            acc = own_a[k, r, :].astype(F32)
            for j in range(3):
                acc = acc + far_a[j, k, r, :].astype(F32)
            own_a[k, r, :] = acc.astype(BF)
            return carry

        lax.fori_loop(0, shape_a[0] // 16, add, 0)
    second = []
    for j, s in enumerate(STEPS):
        d = ring("z", s)
        second.append(cp.send(own_a.at[d["z"]], last_a.at[j], d))
    near_b.wait()
    for copy in first_b:
        copy.wait_recv()
    for k in range(4):

        def add(i, carry, k=k):
            r = rows_of(i)
            acc = own_b[k // 2, k % 2, r, :].astype(F32)
            for j in range(3):
                acc = acc + far_b[j, k // 2, k % 2, r, :].astype(F32)
            own_b[k // 2, k % 2, r, :] = acc.astype(BF)
            return carry

        lax.fori_loop(0, shape_b[0] // 16, add, 0)
    for j, s in enumerate(STEPS):
        d = ring("x", s)
        second.append(cp.send(own_b.at[d["xlo"], d["xhi"]], last_b.at[j], d))
    yield
    for copy in second:
        copy.wait_recv()

    def end_a(i, carry):
        r = rows_of(i)
        acc = own_a[me[2], r, :].astype(F32)
        for j in range(3):
            acc = acc + last_a[j, r, :].astype(F32)
        at = rows_of(i) if halves[0][0].start == 0 else pl.ds(halves[0][0].start + i * 16, 16)
        out[at, halves[0][1]] = acc.astype(BF)
        return carry

    lax.fori_loop(0, shape_a[0] // 16, end_a, 0)

    def end_b(i, carry):
        r = rows_of(i)
        acc = own_b[me[0], me[1], r, :].astype(F32)
        for j in range(3):
            acc = acc + last_b[j, r, :].astype(F32)
        at = pl.ds(pl.multiple_of(halves[1][0].start + i * 16, 16), 16)
        out[at, halves[1][1]] = acc.astype(BF)
        return carry

    lax.fori_loop(0, shape_b[0] // 16, end_b, 0)


def by_rows(rows, width):
    h = rows // 2
    return ((pl.ds(0, h), pl.ds(0, width)), (pl.ds(h, h), pl.ds(0, width)))


def by_columns(rows, width):
    h = width // 2
    return ((pl.ds(0, rows), pl.ds(0, h)), (pl.ds(0, rows), pl.ds(h, h)))


def call(body, name, ident, out_shape, in_specs, out_specs, scratch, sems, near, **kw):
    return pl.pallas_call(
        body,
        name=name,
        out_shape=out_shape,
        in_specs=in_specs,
        out_specs=out_specs,
        scratch_shapes=list(scratch)
        + [
            pltpu.SemaphoreType.DMA((sems,)),
            pltpu.SemaphoreType.DMA((sems,)),
            pltpu.SemaphoreType.DMA((near,)),
        ],
        compiler_params=pltpu.CompilerParams(
            collective_id=ident, has_side_effects=True, vmem_limit_bytes=56 << 20
        ),
        **kw,
    )


def gather_body(
    tok, gain, w_in, w_f, w_og, w_o, gu, dn, cot, b3, bo, bgu, bdn, fi, gf, first, send, recv, near
):
    cp = Copies(send, recv, near)
    p, g = place()
    d = p * 8 + g
    to_p, to_g = lax.rem(d, 16), lax.div(d, 16)
    from_d = 16 * g + p
    target = device(to_p, to_g)
    source = device(lax.div(from_d, 8), lax.rem(from_d, 8))
    same = to_p * 8 + to_g == d
    greet(rings() + [in_group(*st) for st in GROUP], (source, from_d == d, same))
    me = (ax("xlo"), ax("xhi"), ax("z"))
    mine16 = pl.ds(pl.multiple_of(g * 16, 16), 16)
    shards = (w_in, w_f, w_og)
    third = w_in.shape[1] // 8
    locals_ = []
    arrive3, arrive_gu = [], []
    for j, w in enumerate(shards):
        to = b3.at[me + (mine16, pl.ds(j * third, third))]
        for st in GROUP:
            q = in_group(*st)
            k = q["y"] * 2 + q["core"]
            arrive3.append(cp.send(w.at[:, pl.ds(pl.multiple_of(k * third, 128), third)], to, q))
        locals_.append(cp.local(w.at[:, pl.ds(pl.multiple_of(g * third, 128), third)], to))

    shuffles = []
    for src, buf in ((w_o, bo), (dn, bdn)):
        at = (lax.div(to_p, 8), lax.rem(lax.div(to_p, 4), 2), lax.rem(to_p, 4))
        copy = cp.remote(src, buf.at[at], target)
        home = pltpu.make_async_copy(src, buf.at[at], cp.sems[2].at[cp.locals])
        cp.locals += 1

        @pl.when(same)
        def _(home=home):
            home.start()

        @pl.when(jnp.logical_not(same))
        def _(copy=copy):
            copy.start()

        shuffles.append((copy, home))
    to = bgu.at[me + (mine16,)]
    for st in GROUP:
        q = in_group(*st)
        arrive_gu.append(cp.send(gu.at[q["y"] * 2 + q["core"]], to, q))
    locals_.append(cp.local(gu.at[g], to))

    def norm(i, carry):
        r = rows_of(i)
        x = tok[r, :].astype(F32)
        s = lax.rsqrt(jnp.mean(x * x, axis=-1, keepdims=True) + EPS)
        first[r, :] = (x * s * gain[...]).astype(BF)
        return carry

    lax.fori_loop(0, tok.shape[0] // 16, norm, 0)
    chain_fi = group_gather(cp, first, fi)
    next(chain_fi)
    chain_g = group_gather(cp, cot, gf)
    next(chain_g)
    for copy in arrive3 + arrive_gu:
        copy.wait_recv()
    for copy in locals_:
        copy.wait()

    for copy, home in shuffles:

        @pl.when(same)
        def _(home=home):
            home.wait()

        @pl.when(jnp.logical_not(same))
        def _(copy=copy):
            copy.wait()

    rows = b3.shape[3]
    chains = [
        plane_gather(cp, b3, by_rows(rows, b3.shape[4])),
        plane_gather(cp, bo, by_columns(16, bo.shape[4])),
        plane_gather(cp, bgu, by_rows(rows, bgu.shape[4])),
        plane_gather(cp, bdn, by_columns(bdn.shape[3], bdn.shape[4])),
        chain_fi,
        chain_g,
    ]
    run(chains, (0, 1, 2, 3, 0, 1, 2, 3, 4, 0, 1, 5, 2, 3))
    cp.finish()


def silu_slope(v, s):
    return s * (1.0 + v * (1.0 - s))


def row_sums(x):
    ones = jnp.ones((8, x.shape[1]), F32)
    return lax.dot_general(
        ones, x, (((1,), (1,)), ((), ())), precision=HIGH, preferred_element_type=F32
    )[0:1]


def as_column(row, width):
    t = jnp.transpose(jnp.broadcast_to(row, (128, 128)))
    return jnp.concatenate([t] * (width // 128), axis=1)


def chunk_rows(s):
    return pl.ds(pl.multiple_of(s * 128, 128), 128)


def wide(ref, r):
    return jnp.concatenate([ref[j, r, :] for j in range(ref.shape[0])], axis=1)


def put(ref, r, value):
    for j in range(ref.shape[0]):
        ref[j, r, :] = value[:, 128 * j : 128 * (j + 1)]


def share(cp, src, dst, index, peers):
    copies = [cp.send(src, dst.at[index], dev) for dev in peers]
    dst[pl.ds(index, 1)] = src[...][None]
    return copies


def scan_body(
    proj, lb, gain, gated, states, forget, tot, links, carry, prod, entry, mine, rowsum, rows8, send, recv, near
):
    cp = Copies(send, recv, near)
    tiles, rows = states.shape[:2]
    w = 128 * tiles
    steps = rows // 8
    peers_chain = [in_chain(*st) for st in CHAIN]
    peers_group = [in_group(*st) for st in GROUP]
    greet(peers_chain + peers_group)
    low = lb[...]

    def gates(i, c):
        r = rows_of(i, 32)
        f = low + (1.0 - low) * jax.nn.sigmoid(proj[r, w : 2 * w])
        v = proj[r, 0:w]
        put(forget, r, f)
        put(states, r, v * jax.nn.sigmoid(v) * (1.0 - f))
        return c

    lax.fori_loop(0, 8 * steps // 32, gates, 0)

    def step(t, c):
        at = pl.ds(t, 8, stride=steps)
        new = []
        for j, (h, a) in enumerate(c):
            f = forget[j, at, :]
            h = f * h + states[j, at, :]
            a = a * f
            states[j, at, :] = h
            prod[j, at, :] = a
            new.append((h, a))
        return tuple(new)

    start = ((jnp.zeros((8, 128), F32), jnp.ones((8, 128), F32)),) * tiles
    ends = lax.fori_loop(0, steps, step, start, unroll=8)
    h = jnp.concatenate([e[0] for e in ends], axis=1)
    a = jnp.concatenate([e[1] for e in ends], axis=1)
    c = jnp.zeros((1, w), F32)
    q = jnp.ones((1, w), F32)
    cs, qs = [], []
    for s in range(8):
        cs.append(c)
        qs.append(q)
        c = a[s : s + 1] * c + h[s : s + 1]
        q = a[s : s + 1] * q
    mine[...] = jnp.concatenate([q, c, jnp.zeros((6, w), F32)], axis=0)
    k = ax("xhi") * 4 + ax("z")
    for copy in share(cp, mine, links, k, peers_chain):
        copy.wait_recv()
    come = jnp.zeros((1, w), F32)
    for j in range(8):
        new = links[j, 0:1, :] * come + links[j, 1:2, :]
        come = jnp.where(j < k, new, come)
    carry[...] = jnp.broadcast_to(come, (8, w))
    entry[...] = jnp.concatenate(qs, axis=0) * come + jnp.concatenate(cs, axis=0)

    def finish(s, c):
        r = chunk_rows(s)
        st = wide(states, r) + wide(prod, r) * entry[pl.ds(s, 1), :]
        put(states, r, st)
        rowsum[pl.ds(s, 1), :] = row_sums(st * st)
        return c

    lax.fori_loop(0, 8, finish, 0)
    for copy in share(cp, rowsum, rows8, place()[1], peers_group):
        copy.wait_recv()
    total = rows8[0]
    for j in range(1, 8):
        total = total + rows8[j]
    tot[...] = lax.rsqrt(total / (8.0 * w) + EPS)

    def gate(s, c):
        r = chunk_rows(s)
        v = proj[r, 2 * w : 3 * w]
        n = wide(states, r) * as_column(tot[pl.ds(s, 1), :], w)
        gated[r, :] = (n * gain[...] * (v * jax.nn.sigmoid(v))).astype(BF)
        return c

    lax.fori_loop(0, 8, gate, 0)
    cp.finish()


def middle_body(part, tok, gain, mid, full, own, near_, far, block, send, recv, near):
    cp = Copies(send, recv, near)
    greet(ys())
    sums = []
    run([group_sum(cp, part, own, near_, far, sums)], ())

    def norm(i, carry):
        r = rows_of(i)
        x = tok[r, :].astype(F32) + sums[0](r)
        mid[r, :] = x
        s = lax.rsqrt(jnp.mean(x * x, axis=-1, keepdims=True) + EPS)
        block[r, :] = (x * s * gain[...]).astype(BF)
        return carry

    lax.fori_loop(0, mid.shape[0] // 16, norm, 0)
    run([group_gather(cp, block, full)], ())
    cp.finish()


def turn_body(
    part, part_r, mid, cot, gain, result, mixed, full, sums_out, own, near_, far, own_r, near_r, far_r, block, send, recv, near
):
    cp = Copies(send, recv, near)
    greet(ys())
    sums, sums_r = [], []
    chain = group_sum(cp, part, own, near_, far, sums)
    chain_r = group_sum(cp, part_r, own_r, near_r, far_r, sums_r)
    run([chain, chain_r], (0, 0, 1, 1, 0))
    sums_out[...] = jnp.zeros_like(sums_out)

    def back(i, carry):
        r = rows_of(i)
        x = mid[r, :]
        s = lax.rsqrt(jnp.mean(x * x, axis=-1, keepdims=True) + EPS)
        n = x * s
        dy = sums[0](r)
        sums_out[0:1, :] = sums_out[0:1, :] + jnp.sum(dy * n, axis=0, keepdims=True)
        dy = dy * gain[...]
        v = cot[r, :].astype(F32) + s * (dy - n * jnp.mean(dy * n, axis=-1, keepdims=True))
        mixed[r, :] = v
        block[r, :] = v.astype(BF)
        result[r, :] = (x + sums_r[0](r)).astype(BF)
        return carry

    lax.fori_loop(0, mid.shape[0] // 16, back, 0)
    run([group_gather(cp, block, full)], ())
    cp.finish()


def back_body(
    gg, proj, states, forget, tot, links, carry, lb, gain, grads, sums_out, gs, prod, entry, mine, rowsum, rows8, far, send, recv, near
):
    cp = Copies(send, recv, near)
    tiles, rows = states.shape[:2]
    w = 128 * tiles
    steps = rows // 8
    peers_chain = [in_chain(*st) for st in CHAIN]
    peers_group = [in_group(*st) for st in GROUP]
    greet(peers_chain + peers_group)
    low = lb[...]
    sums_out[...] = jnp.zeros_like(sums_out)

    def through(s, c):
        r = chunk_rows(s)
        v = proj[r, 2 * w : 3 * w]
        sig = jax.nn.sigmoid(v)
        n = wide(states, r) * as_column(tot[pl.ds(s, 1), :], w)
        dy = gg[r, :]
        sums_out[0:1, :] = sums_out[0:1, :] + jnp.sum(dy * n * (v * sig), axis=0, keepdims=True)
        grads[r, 2 * w : 3 * w] = (dy * n * gain[...] * silu_slope(v, sig)).astype(BF)
        dy = dy * gain[...] * (v * sig)
        put(gs, r, dy)
        rowsum[pl.ds(s, 1), :] = row_sums(dy * n)
        return c

    lax.fori_loop(0, 8, through, 0)
    for copy in share(cp, rowsum, rows8, place()[1], peers_group):
        copy.wait_recv()
    total = rows8[0]
    for j in range(1, 8):
        total = total + rows8[j]
    def norm(s, c):
        r = chunk_rows(s)
        t = as_column(tot[pl.ds(s, 1), :], w)
        m = as_column(rowsum[pl.ds(s, 1), :], w)
        put(gs, r, t * (wide(gs, r) - wide(states, r) * t * m))
        return c

    cp.finish()
    cp.open = []
    rowsum[...] = total / (8.0 * w)
    lax.fori_loop(0, 8, norm, 0)

    def step(i, c):
        at = pl.ds(steps - 1 - i, 8, stride=steps)
        new = []
        for j, (h, a) in enumerate(c):
            f = forget[j, at, :]
            v = gs[j, at, :] + h
            gs[j, at, :] = v
            prod[j, at, :] = a
            new.append((f * v, a * f))
        return tuple(new)

    start = ((jnp.zeros((8, 128), F32), jnp.ones((8, 128), F32)),) * tiles
    ends = lax.fori_loop(0, steps, step, start, unroll=8)
    h = jnp.concatenate([e[0] for e in ends], axis=1)
    a = jnp.concatenate([e[1] for e in ends], axis=1)
    c = jnp.zeros((1, w), F32)
    q = jnp.ones((1, w), F32)
    cs, qs = [None] * 8, [None] * 8
    for s in range(7, -1, -1):
        cs[s] = c
        qs[s] = q
        c = a[s : s + 1] * c + h[s : s + 1]
        q = a[s : s + 1] * q
    mine[...] = jnp.broadcast_to(c, (8, w))
    k = ax("xhi") * 4 + ax("z")
    for copy in share(cp, mine, far, k, peers_chain):
        copy.wait_recv()
    come = jnp.zeros((1, w), F32)
    for j in range(7, -1, -1):
        new = links[j, 0:1, :] * come + far[j, 0:1, :]
        come = jnp.where(j > k, new, come)
    entry[...] = jnp.concatenate(qs, axis=0) * come + jnp.concatenate(cs, axis=0)

    def last(s, c):
        r = chunk_rows(s)
        v = wide(gs, r) + wide(prod, r) * entry[pl.ds(s, 1), :]
        st = wide(states, r)
        above = pl.ds(jnp.maximum(s * 128 - 1, 0), 1)
        before = jnp.where(s == 0, carry[0:1, :], wide(states, above))
        top = lax.broadcasted_iota(jnp.int32, (128, w), 0) == 0
        prev = jnp.where(top, before, pltpu.roll(st, 1, 0))
        x = proj[r, 0:w]
        sx = jax.nn.sigmoid(x)
        f = wide(forget, r)
        sf = jax.nn.sigmoid(proj[r, w : 2 * w])
        gf = v * (prev - x * sx)
        grads[r, 0:w] = (v * (1.0 - f) * silu_slope(x, sx)).astype(BF)
        grads[r, w : 2 * w] = (gf * (1.0 - low) * sf * (1.0 - sf)).astype(BF)
        sums_out[1:2, :] = sums_out[1:2, :] + jnp.sum(gf * (1.0 - sf), axis=0, keepdims=True)
        return c

    lax.fori_loop(0, 8, last, 0)
    cp.finish()


def sum_body(*refs):
    (part, tok, mixed, gain, ffn_sums, mix_sums, d3, do, dgu, ddn) = refs[:10]
    (gtok, r3, rgu, ro, rdn, totals) = refs[10:16]
    scratch = list(refs[16:-3])
    cp = Copies(*refs[-3:])
    own, near_, far = scratch[:3]
    plane = [scratch[3 + 6 * i : 9 + 6 * i] for i in range(4)]
    o3, ogu, oo, od, va, ga, ta, gb, tb = scratch[27:]
    p, g = place()
    d = p * 8 + g
    from_d = 16 * g + p
    same = from_d == d
    target = device(lax.div(from_d, 8), lax.rem(from_d, 8))
    source = device(lax.rem(d, 16), lax.div(d, 16))
    greet(
        [in_plane(*st) for st in PLANE] + [in_group(*st) for st in GROUP],
        (source, lax.rem(d, 16) * 8 + lax.div(d, 16) == d, same),
    )
    sums = []
    rows = d3.shape[3]
    chain = group_sum(cp, part, own, near_, far, sums)
    chains = [
        plane_sum(cp, dgu, by_rows(rows, dgu.shape[4]), *plane[0], ogu),
        plane_sum(cp, ddn, by_columns(ddn.shape[3], ddn.shape[4]), *plane[1], od),
        plane_sum(cp, d3, by_rows(rows, d3.shape[4]), *plane[2], o3),
        plane_sum(cp, do, by_columns(16, do.shape[4]), *plane[3], oo),
    ]
    next(chain)
    for c in chains:
        next(c)
    next(chain)
    for _ in chain:
        pass
    va[...] = jnp.zeros_like(va)

    def back(i, carry):
        r = rows_of(i)
        x = tok[r, :].astype(F32)
        s = lax.rsqrt(jnp.mean(x * x, axis=-1, keepdims=True) + EPS)
        n = x * s
        dy = sums[0](r)
        va[0:1, :] = va[0:1, :] + jnp.sum(dy * n, axis=0, keepdims=True)
        dy = dy * gain[...]
        gtok[r, :] = mixed[r, :] + s * (dy - n * jnp.mean(dy * n, axis=-1, keepdims=True))
        return carry

    lax.fori_loop(0, gtok.shape[0] // 16, back, 0)
    va[1:2, :] = ffn_sums[0:1, :]
    w = ga.shape[2]
    small = []
    for st in GROUP:
        q = in_group(*st)
        k = q["y"] * 2 + q["core"]
        small.append(cp.send(va.at[:, pl.ds(pl.multiple_of(k * w, 128), w)], ga.at[g], q))
    ga[pl.ds(g, 1)] = va[:, pl.ds(pl.multiple_of(g * w, 128), w)][None]
    for c in chains:
        next(c)
    for copy in small:
        copy.wait_recv()
    acc = ga[0]
    for j in range(1, 8):
        acc = acc + ga[j]
    ta[...] = acc
    ta[2:4, :] = mix_sums[0:2, :]
    for copy in share(cp, ta, gb, p, [in_plane(*st) for st in PLANE]):
        copy.wait_recv()
    acc = gb[0]
    for j in range(1, 16):
        acc = acc + gb[j]
    tb[...] = acc
    small = share(cp, tb, totals, g, [in_group(*st) for st in GROUP])
    for c in chains:
        for _ in c:
            pass
    arrive = []
    near_copies = []
    for src, dst in ((ogu, rgu), (o3, r3)):
        for st in GROUP:
            q = in_group(*st)
            k = q["y"] * 2 + q["core"]
            at = pl.ds(pl.multiple_of(k * 16, 16), 16)
            arrive.append(cp.send(src.at[at, :], dst.at[g], q))
        near_copies.append(cp.local(src.at[pl.ds(pl.multiple_of(g * 16, 16), 16), :], dst.at[g]))
    shuffles = []
    for src, dst in ((oo, ro), (od, rdn)):
        copy = cp.remote(src, dst, target)
        home = pltpu.make_async_copy(src, dst, cp.sems[2].at[cp.locals])
        cp.locals += 1

        @pl.when(same)
        def _(home=home):
            home.start()

        @pl.when(jnp.logical_not(same))
        def _(copy=copy):
            copy.start()

        shuffles.append((copy, home))
    for copy in small + arrive:
        copy.wait_recv()
    for copy in near_copies:
        copy.wait()
    for copy, home in shuffles:

        @pl.when(same)
        def _(home=home):
            home.wait()

        @pl.when(jnp.logical_not(same))
        def _(copy=copy):
            copy.wait()

    cp.finish()


def bound_value(bound_table, layer_idx):
    probabilities = jax.nn.softmax(bound_table, axis=0)
    levels = jnp.arange(bound_table.shape[0], dtype=jnp.int32)[:, None]
    keep = jnp.where((levels >= 1) & (levels <= layer_idx[0]), 1.0, 0.0).astype(F32)
    return jnp.sum(probabilities * keep, axis=0)


def dot(a, b, dims):
    return lax.dot_general(a, b, (dims, ((), ())), preferred_element_type=F32)


NN = ((1,), (0,))
NT = ((1,), (1,))
TN = ((0,), (0,))


def on_device(
    tokens, cotangent, attn_gain, w_input, w_forget, w_outgate, w_out, norm_gain, mlp_gain, w_gate, w_up, w_down, bound_table, layer_idx
):
    n, width = tokens.shape
    rows = w_input.shape[0]
    hidden_width = w_gate.shape[1]
    down = w_down.shape[0]
    padded = -(-down // 16) * 16
    unit = 16 * padded
    w = width // 8
    shape = jax.ShapeDtypeStruct

    def spread(m):
        m = jnp.pad(m.reshape(rows, 128, down), ((0, 0), (0, 0), (0, padded - down)))
        return m.reshape(rows, 8, unit).transpose(1, 0, 2)

    gu = jnp.concatenate([spread(w_gate), spread(w_up)], axis=2)
    dn = jnp.pad(w_down, ((0, padded - down), (0, 0)))
    gains = attn_gain[None, :]
    b3, bo, bgu, bdn, fi, gf = call(
        gather_body,
        "gather",
        0,
        [
            shape((2, 2, 4, 8 * rows, 3 * w), BF),
            shape((2, 2, 4, rows, width), BF),
            shape((2, 2, 4, 8 * rows, 2 * unit), BF),
            shape((2, 2, 4, padded, width), BF),
            shape((8, n, width), BF),
            shape((8, n, width), BF),
        ],
        [VMEM, VMEM] + [ANY] * 7,
        [ANY] * 6,
        [pltpu.VMEM((n, width), BF)],
        110,
        10,
    )(tokens, gains, w_input, w_forget, w_outgate, w_out, gu, dn, cotangent)
    big3 = b3.reshape(width, 3 * w)
    big_out = bo.reshape(w, width)
    big_gu = bgu.reshape(width, 2 * unit)
    big_down = bdn.reshape(unit, width)
    first_full = fi.reshape(8 * n, width)
    g_full = gf.reshape(8 * n, width)

    group = ax("y") * 2 + ax("core")
    lower = bound_value(lax.dynamic_slice_in_dim(bound_table, group * w, w, 1), layer_idx)[None, :]
    mixer_gain = lax.dynamic_slice_in_dim(norm_gain, group * w, w, 0)[None, :]
    proj = dot(first_full, big3, NN)
    gated, states, forget, tot, links, carry = call(
        scan_body,
        "scan",
        1,
        [
            shape((8 * n, w), BF),
            shape((w // 128, 8 * n, 128), F32),
            shape((w // 128, 8 * n, 128), F32),
            shape((8, n), F32),
            shape((8, 8, w), F32),
            shape((8, w), F32),
        ],
        [VMEM] * 3,
        [VMEM] * 6,
        [
            pltpu.VMEM((w // 128, 8 * n, 128), F32),
            pltpu.VMEM((8, w), F32),
            pltpu.VMEM((8, w), F32),
            pltpu.VMEM((8, n), F32),
            pltpu.VMEM((8, 8, n), F32),
        ],
        16,
        2,
    )(proj, lower, mixer_gain)
    mid_part = dot(gated, big_out, NN).astype(BF).reshape(8, n, width)
    sum_scratch = group_sum_scratch(n, width)
    mid, si = call(
        middle_body,
        "middle",
        2,
        [shape((n, width), F32), shape((8, n, width), BF)],
        [ANY, VMEM, VMEM],
        [VMEM, ANY],
        sum_scratch + [pltpu.VMEM((n, width), BF)],
        20,
        8,
    )(mid_part, tokens, mlp_gain[None, :])
    second_full = si.reshape(8 * n, width)
    gate_up = dot(second_full, big_gu, NN)
    gate_proj, up_proj = gate_up[:, :unit], gate_up[:, unit:]
    sig = jax.nn.sigmoid(gate_proj)
    act = gate_proj * sig
    hidden = (act * up_proj).astype(BF)
    result_part = dot(hidden, big_down, NN).astype(BF).reshape(8, n, width)

    grad_hidden = dot(g_full, big_down, NT)
    grad_gate = (grad_hidden * up_proj * silu_slope(gate_proj, sig)).astype(BF)
    grad_up = (grad_hidden * act).astype(BF)
    grad_gu = jnp.concatenate([grad_gate, grad_up], axis=1)
    second_part = dot(grad_gu, big_gu, NT).astype(BF).reshape(8, n, width)
    result, mixed, gb, ffn_sums = call(
        turn_body,
        "turn",
        3,
        [
            shape((n, width), BF),
            shape((n, width), F32),
            shape((8, n, width), BF),
            shape((8, width), F32),
        ],
        [ANY, ANY, VMEM, VMEM, VMEM],
        [VMEM, VMEM, ANY, VMEM],
        sum_scratch + sum_scratch + [pltpu.VMEM((n, width), BF)],
        32,
        12,
    )(second_part, result_part, mid, cotangent, mlp_gain[None, :])
    branch_full = gb.reshape(8 * n, width)
    grad_gated = dot(branch_full, big_out, NT)
    grads3, mix_sums = call(
        back_body,
        "back",
        4,
        [shape((8 * n, 3 * w), BF), shape((8, w), F32)],
        [VMEM] * 9,
        [VMEM] * 2,
        [
            pltpu.VMEM((w // 128, 8 * n, 128), F32),
            pltpu.VMEM((w // 128, 8 * n, 128), F32),
            pltpu.VMEM((8, w), F32),
            pltpu.VMEM((8, w), F32),
            pltpu.VMEM((8, n), F32),
            pltpu.VMEM((8, 8, n), F32),
            pltpu.VMEM((8, 8, w), F32),
        ],
        16,
        2,
    )(grad_gated, proj, states, forget, tot, links, carry, lower, mixer_gain)
    first_part = dot(grads3, big3, NT).astype(BF).reshape(8, n, width)

    d3 = dot(first_full, grads3, TN).astype(BF).reshape(2, 2, 4, 8 * rows, 3 * w)
    do = dot(gated, branch_full, TN).astype(BF).reshape(2, 2, 4, rows, width)
    dgu = dot(second_full, grad_gu, TN).astype(BF).reshape(2, 2, 4, 8 * rows, 2 * unit)
    ddn = dot(hidden, g_full, TN).astype(BF).reshape(2, 2, 4, padded, width)
    plane_scratch = (
        plane_sum_scratch(by_rows(8 * rows, 2 * unit))
        + plane_sum_scratch(by_columns(padded, width))
        + plane_sum_scratch(by_rows(8 * rows, 3 * w))
        + plane_sum_scratch(by_columns(rows, width))
    )
    grad_tokens, r3, rgu, ro, rdn, totals = call(
        sum_body,
        "sums",
        5,
        [
            shape((n, width), F32),
            shape((8, rows, 3 * w), BF),
            shape((8, rows, 2 * unit), BF),
            shape((rows, width), BF),
            shape((padded, width), BF),
            shape((8, 8, w), F32),
        ],
        [ANY, VMEM, VMEM, VMEM, VMEM, VMEM] + [ANY] * 4,
        [VMEM, VMEM, VMEM, VMEM, VMEM, VMEM],
        sum_scratch
        + plane_scratch
        + [
            pltpu.VMEM((8 * rows, 3 * w), BF),
            pltpu.VMEM((8 * rows, 2 * unit), BF),
            pltpu.VMEM((rows, width), BF),
            pltpu.VMEM((padded, width), BF),
            pltpu.VMEM((8, width), F32),
            pltpu.VMEM((8, 8, w), F32),
            pltpu.VMEM((8, w), F32),
            pltpu.VMEM((16, 8, w), F32),
            pltpu.VMEM((8, w), F32),
        ],
        110,
        18,
    )(first_part, tokens, mixed, gains, ffn_sums, mix_sums, d3, do, dgu, ddn)

    def join(m):
        m = m.transpose(1, 0, 2)
        return m.reshape(rows, 8 * m.shape[2]).astype(F32)

    def unspread(m):
        m = m.transpose(1, 0, 2).reshape(rows, 128, padded)[:, :, :down]
        return m.reshape(rows, hidden_width).astype(F32)

    sums = totals.transpose(1, 0, 2).reshape(8, width)
    pullback = jax.vjp(lambda table: bound_value(table, layer_idx), bound_table)[1]
    return (
        result,
        grad_tokens,
        sums[0],
        join(r3[:, :, :w]),
        join(r3[:, :, w : 2 * w]),
        join(r3[:, :, 2 * w :]),
        ro.astype(F32),
        sums[2],
        sums[1],
        unspread(rgu[:, :, :unit]),
        unspread(rgu[:, :, unit:]),
        rdn[:down].astype(F32),
        pullback(sums[3])[0],
    )


def solution(mesh):
    split = Mesh(mesh.devices.reshape(2, 2, 4, 4, 2), AXES)
    cut = P(AXES, None)
    return jax.shard_map(
        on_device,
        mesh=split,
        in_specs=(cut, cut, P(), cut, cut, cut, cut, P(), P(), cut, cut, cut, P(), P()),
        out_specs=(cut, cut, P(), cut, cut, cut, cut, P(), P(), cut, cut, cut, P()),
        check_vma=False,
    )
```

time: 3470 us -> 530 us (0.15)
  blocking collectives: 1440 us -> 0 us
  waiting for transfers between devices: 1190 us -> 0 us
  Pallas kernels: 0 us -> 418 us
  local copies, waits for them, and re-layouts: 375 us -> 18.8 us
  other arithmetic: 176 us -> 7.18 us
  matrix products: 208 us -> 76.7 us
  starting transfers between devices: 43.6 us -> 0 us
    all_gather x7 -> x0, waiting for transfers between devices: 1080 us -> none  [the longest x1 223 us: on_device(): lax.all_gather(w_down, ('batch', 'seq'), axis=0, tiled=True)]
    psum x1 -> x0, blocking collectives: 614 us -> none  [on_device(): lax.psum((grad_attn_gain, grad_norm_gain, feedforward_gain_gradient, grad...]
    unnamed x1 -> x0, blocking collectives: 543 us -> none
    pallas_call x0 -> x6, Pallas kernels: none -> 418 us  [the longest x1 123 us: on_device(): call(sum_body, 'sums', 5, [shape((n, width), F32), shape((8, rows, 3 * w)...]
    all_gather x3 -> x0, blocking collectives: 280 us -> none  [entering(): everything = jax.tree.map(lambda part: lax.all_gather(part, axis), x)]
    dot_general x18 -> x12, matrix products: 208 us -> 76.7 us  [dot(): return lax.dot_general(a, b, (dims, ((), ())), preferred_element_type=F32)]
    concatenate x23 -> x1, other arithmetic: 118 us -> 0.77 us  [on_device(): gu = jnp.concatenate([spread(w_gate), spread(w_up)], axis=2)]
    dynamic_slice x128 -> x1, local copies, waits for them, and re-layouts: 114 us -> 1.41 us  [on_device(): mixer_gain = lax.dynamic_slice_in_dim(norm_gain, group * w, w, 0)[None, :]]
  transfers between devices with their start and end apart: 20 -> 0, of which waited for: 10 -> 0; matrix products, arithmetic and copies ran while one was open for 25% -> 0% of each run, Pallas kernels for 0% -> 0%
where the time goes in v1:
time: 530 us; the launch traced here: 523 us
  Pallas kernels  418 us (79%)
  matrix products  76.7 us (14%)
  local copies, waits for them, and re-layouts  18.8 us (4%)
  other arithmetic  7.18 us (1%)
    pallas_call x1, Pallas kernels, on_device(): call(sum_body, 'sums', 5, [shape((n, width), F32), shape((8, rows, 3 * w)...  123 us
    pallas_call x1, Pallas kernels, on_device(): call(gather_body, 'gather', 0, [shape((2, 2, 4, 8 * rows, 3 * w), BF), sh...  106 us
    pallas_call x1, Pallas kernels, on_device(): call(turn_body, 'turn', 3, [shape((n, width), BF), shape((n, width), F32)...  83.8 us
    dot_general x12, matrix products, dot(): return lax.dot_general(a, b, (dims, ((), ())), preferred_element_type=F32)  76.7 us
    pallas_call x1, Pallas kernels, on_device(): call(middle_body, 'middle', 2, [shape((n, width), F32), shape((8, n, widt...  61.1 us
    pallas_call x1, Pallas kernels, on_device(): call(back_body, 'back', 4, [shape((8 * n, 3 * w), BF), shape((8, w), F32)...  22.2 us
    pallas_call x1, Pallas kernels, on_device(): call(scan_body, 'scan', 1, [shape((8 * n, w), BF), shape((w // 128, 8 * n...  21.5 us

profile of v1, /device:TPU:1, one launch (start us, length us, event | category | flops | bytes accessed | tf_op | source)
XLA Modules:
  0.0 522.6 jit_solution(10809429077563104240)
XLA Ops:
  2.8 1.4 multiply_reduce_fusion
  4.2 2.4 reshape.143
  7.3 2.4 reshape.145
  10.4 0.8 pad_maximum_fusion.3.gu
  11.9 106.1 %gather.1 = (bf16[2,2,4,128,768]{4,3,2,1,0:T(8,128)(2,1)}, bf16[2,2,4,16,2048]{4,3,2,1,0:T(8,128)(2,1)}, bf16[2,2,4,128,1536]{4,3,2,1,0:T(8,128)(2,1)}, bf16[2,2...) custom-call(bf16[128,2048]{1,0:T(8,128)(2,1)} %refs_1_.1, ...), custom_call_target="tpu_custom_call" | custom-call | tf_op jit(solution)/shard_map/gather/pallas_call | solution.py:857
  118.0 8.3 %fusion.10.proj = f32[1024,768]{1,0:T(8,128)} fusion(bf16[1024,2048]{1,0:T(8,128)(2,1)} %bitcast.102, bf16[2048,768]{1,0:T(8,128)(2,1)} %bitcast.108), kind=kOutput, calls=%fused_computation.42 | convolution fusion | flops 3221225472 | bytes 10485760 | tf_op jit(solution)/shard_map/dot_general | solution.py:830
  126.3 1.4 dynamic_slice.7
  127.7 21.5 %scan.1 = (bf16[1024,256]{1,0:T(8,128)(2,1)}, f32[2,1024,128]{2,1,0:T(8,128)}, f32[2,1024,128]{2,1,0:T(8,128)}, f32[8,128]{1,0:T(8,128)}, f32[8,8,256]{2,1,0:T(8,128)}, /*index=5*/f32[8,256]{1,0:T(8,128)}) custom-call(f32[1024,768]{1,0:T(8,128)} %fusion.10.proj, f32[1,256]{1,0:T(1,128)} %bitcast.89, f32[1,256]{1,0:T(1,128)} %bitcast.91), custom_call_target="tpu_custom_call" | custom-call | tf_op jit(solution)/shard_map/scan/pallas_call | solution.py:886
  149.2 4.5 convolution_convert_fusion.2
  153.7 61.1 %middle.1 = (f32[128,2048]{1,0:T(8,128)}, bf16[8,128,2048]{2,1,0:T(8,128)(2,1)}) custom-call(bf16[8,128,2048]{2,1,0:T(8,128)(2,1)} %bitcast.69, bf16[128,2048]{1,0:T(8,128)(2,1)} %refs_1_.1, f32[1,2048]{1,0:T(1,128)} %bitcast.86), custom_call_target="tpu_custom_call" | custom-call | tf_op jit(solution)/shard_map/middle/pallas_call | solution.py:912
  214.8 10.6 %fusion.11 = f32[1024,1536]{0,1:T(8,128)} fusion(bf16[1024,2048]{1,0:T(8,128)(2,1)} %bitcast.104, bf16[2048,1536]{1,0:T(8,128)(2,1)S(1)} %bitcast.98), kind=kOutput, calls=%fused_computation.43 | convolution fusion | flops 6442450944 | bytes 16777216 | tf_op jit(solution)/shard_map/dot_general | solution.py:830
  225.5 6.9 %multiply_convert_fusion.2 = (bf16[1024,768]{0,1:T(8,128)(2,1)S(1)}, bf16[1024,768]{0,1:T(8,128)(2,1)S(1)}, bf16[1024,768]{0,1:T(8,128)(2,1)S(1)}) fusion(f32[1024,1536]{0,1:T(8,128)} %fusion.11, bf16[1024,2048]{1,0:T(8,128)(2,1)S(1)} %bitcast.100, bf16[768,2048]{1,0:T(8,128)(2,1)S(1)} %bitcast.110), kind=kOutput, calls=%fused_computation.10 | convolution fusion | flops 3233021952 | bytes 18350080 | tf_op jit(solution)/shard_map/dot_general | solution.py:830
  232.4 9.6 %convolution_convert_fusion = bf16[2048,1536]{1,0:T(8,128)(2,1)} fusion(bf16[1024,2048]{1,0:T(8,128)(2,1)S(1)} %bitcast.105, bf16[1024,768]{0,1:T(8,128)(2,1)S(1)} %get-tuple-element.66, bf16[1024,768]{0,1:T(8,128)(2,1)S(1)} %get-tuple-element.65), kind=kOutput, calls=%fused_computation | convolution fusion | flops 6451888128 | bytes 13631488 | tf_op jit(solution)/shard_map/dot_general | solution.py:830
  242.0 8.4 %convolution_convert_fusion.1 = bf16[1024,2048]{1,0:T(8,128)(2,1)} fusion(bf16[2048,1536]{1,0:T(8,128)(2,1)S(1)} %bitcast.99, bf16[1024,768]{0,1:T(8,128)(2,1)S(1)} %get-tuple-element.66, bf16[1024,768]{0,1:T(8,128)(2,1)S(1)} %get-tuple-element.65), kind=kOutput, calls=%fused_computation.1 | convolution fusion | flops 6450839552 | bytes 13631488 | tf_op jit(solution)/shard_map/dot_general | solution.py:830
  250.3 5.1 convolution_convert_fusion.4
  255.5 83.8 %turn.1 = (bf16[128,2048]{1,0:T(8,128)(2,1)}, f32[128,2048]{1,0:T(8,128)}, bf16[8,128,2048]{2,1,0:T(8,128)(2,1)}, f32[8,2048]{1,0:T(8,128)}) custom-call(bf16[8,128,2048]{2,1,0:T(8,128)(2,1)} %bitcast.71, bf16[8,128,2048]{2,1,0:T(8,128)(2,1)} %bitcast.72, f32[128,2048]{1,0:T(8,128)} %get-tuple-element.47.mid, bf16[128,2048]{1,0:T(8,128)(2,1)} %cot.3, ...), custom_call_target="tpu_custom_call" | custom-call | tf_op jit(solution)/shard_map/turn/pallas_call | solution.py:936
  339.3 4.6 convolution_convert_fusion.7
  343.9 2.3 fusion.12.gg
  346.2 22.2 %back.1 = (bf16[1024,768]{1,0:T(8,128)(2,1)}, f32[8,256]{1,0:T(8,128)}) custom-call(f32[1024,256]{1,0:T(8,128)} %fusion.12.gg, f32[1024,768]{1,0:T(8,128)} %fusion.10.proj, f32[2,1024,128]{2,1,0:T(8,128)} %get-tuple-element.50.states, f32[2,1024,128]{2,1,0:T(8,128)} %get-tuple-element.51.forget, f32[8,128]{1,0:T(8,128)} %get-tuple-element.52.tot, ...), custom_call_target="tpu_custom_call" | custom-call | tf_op jit(solution)/shard_map/back/pallas_call | solution.py:954
  368.5 6.6 %convolution_convert_fusion.6 = bf16[2048,768]{1,0:T(8,128)(2,1)} fusion(bf16[1024,2048]{1,0:T(8,128)(2,1)S(1)} %bitcast.103, bf16[1024,768]{1,0:T(8,128)(2,1)} %get-tuple-element.55), kind=kOutput, calls=%fused_computation.6 | convolution fusion | flops 3222798336 | bytes 8912896 | tf_op jit(solution)/shard_map/dot_general | solution.py:830
  375.0 5.0 convolution_convert_fusion.3
  380.1 4.8 convolution_convert_fusion.5
  384.9 123.3 %sums.1 = (f32[128,2048]{1,0:T(8,128)}, bf16[8,16,768]{2,1,0:T(8,128)(2,1)}, bf16[8,16,1536]{2,1,0:T(8,128)(2,1)}, bf16[16,2048]{1,0:T(8,128)(2,1)}, bf16[48,2048]{1,0:T(8,128)(2,1)}, /*index=5*/f32[8,8,256]{2,1,0:T(8,128)}) custom-call(bf16[8,128,2048]{2,1,0:T(8,128)(2,1)} %bitcast.73, bf16[128,2048]{1,0:T(8,128)(2,1)} %refs_1_.1, ...), custom_call_target="tpu_custom_call" | custom-call | tf_op jit(solution)/shard_map/sums/pallas_call | solution.py:985
  508.2 1.6 fusion.9
  510.0 0.8 fusion.2
  510.8 1.0 slice_bitcast_fusion
  512.7 1.3 reshape.168
  514.9 1.3 reshape.169
  518.2 0.8 slice_convert_fusion.2
  519.0 1.5 convert_element_type.103
  520.5 0.8 copy.47
  521.3 1.0 copy.48
  (65 shorter events, 7.4 us)
Async XLA Ops:
  4.2 7.0 %copy-start.5 = (bf16[44,2048]{1,0:T(8,128)(2,1)S(1)}, bf16[44,2048]{1,0:T(8,128)(2,1)}, u32[]{:S(2)}) copy-start(bf16[44,2048]{1,0:T(8,128)(2,1)} %param.25) | copy-start | bytes 540676
  126.3 22.9 %copy-start.3 = (bf16[2,2,4,16,2048]{4,3,2,1,0:T(8,128)(2,1)S(1)}, bf16[2,2,4,16,2048]{4,3,2,1,0:T(8,128)(2,1)}, u32[]{:S(2)}) copy-start(bf16[2,2,4,16,2048]{4,3,2,1,0:T(8,128)(2,1)} %get-tuple-element.44) | copy-start | bytes 3145732
  149.2 65.6 %slice-start = ((s8[6291456]{0:T(1024)(128)(4,1)}), s8[4194304]{0:T(1024)(128)(4,1)S(1)}, s32[]{:S(2)}) async-start(s8[6291456]{0:T(1024)(128)(4,1)} %bitcast.96), calls=%async_computation | async-start | bytes 8388608
  149.2 65.6 %slice-start.1 = ((s8[6291456]{0:T(1024)(128)(4,1)}), s8[2097152]{0:T(1024)(128)(4,1)S(1)}, s32[]{:S(2)}) async-start(s8[6291456]{0:T(1024)(128)(4,1)} %bitcast.96), calls=%async_computation.1 | async-start | bytes 4194304
  214.8 10.6 %copy-start.8 = (bf16[8,128,2048]{2,1,0:T(8,128)(2,1)S(1)}, bf16[8,128,2048]{2,1,0:T(8,128)(2,1)}, u32[]{:S(2)}) copy-start(bf16[8,128,2048]{2,1,0:T(8,128)(2,1)} %get-tuple-element.39) | copy-start | bytes 12582916
  214.8 10.6 %copy-start.14 = (bf16[2,2,4,48,2048]{4,3,2,1,0:T(8,128)(2,1)S(1)}, bf16[2,2,4,48,2048]{4,3,2,1,0:T(8,128)(2,1)}, u32[]{:S(2)}) copy-start(bf16[2,2,4,48,2048]{4,3,2,1,0:T(8,128)(2,1)} %get-tuple-element.40) | copy-start | bytes 9437188
  225.4 7.0 %copy-start.11 = (bf16[8,128,2048]{2,1,0:T(8,128)(2,1)S(1)}, bf16[8,128,2048]{2,1,0:T(8,128)(2,1)}, u32[]{:S(2)}) copy-start(bf16[8,128,2048]{2,1,0:T(8,128)(2,1)} %get-tuple-element.45) | copy-start | bytes 12582916
  232.4 18.0 %copy-start.16 = (bf16[1024,768]{0,1:T(8,128)(2,1)}, bf16[1024,768]{0,1:T(8,128)(2,1)S(1)}, u32[]{:S(2)}) copy-start(bf16[1024,768]{0,1:T(8,128)(2,1)S(1)} %get-tuple-element.67) | copy-start | bytes 4718596
  255.5 83.8 %copy-start.1 = (bf16[1024,256]{1,0:T(8,128)(2,1)S(1)}, bf16[1024,256]{1,0:T(8,128)(2,1)}, u32[]{:S(2)}) copy-start(bf16[1024,256]{1,0:T(8,128)(2,1)} %get-tuple-element.43) | copy-start | bytes 1572868
  339.3 4.6 copy-start.12
  346.2 22.2 %copy-start.10 = (bf16[8,128,2048]{2,1,0:T(8,128)(2,1)S(1)}, bf16[8,128,2048]{2,1,0:T(8,128)(2,1)}, u32[]{:S(2)}) copy-start(bf16[8,128,2048]{2,1,0:T(8,128)(2,1)} %get-tuple-element.41) | copy-start | bytes 12582916
  368.4 6.6 %copy-start.13 = (bf16[2,2,4,128,768]{4,3,2,1,0:T(8,128)(2,1)S(1)}, bf16[2,2,4,128,768]{4,3,2,1,0:T(8,128)(2,1)}, u32[]{:S(2)}) copy-start(bf16[2,2,4,128,768]{4,3,2,1,0:T(8,128)(2,1)} %get-tuple-element.42) | copy-start | bytes 9437188
  368.4 6.6 %copy-start.15 = (bf16[1024,768]{1,0:T(8,128)(2,1)S(1)}, bf16[1024,768]{1,0:T(8,128)(2,1)}, u32[]{:S(2)}) copy-start(bf16[1024,768]{1,0:T(8,128)(2,1)} %get-tuple-element.55) | copy-start | bytes 4718596
  375.0 5.1 copy-start.9
  375.0 5.0 copy-start.17
  384.9 124.9 %copy-start = (f32[24,2048]{1,0:T(8,128)S(1)}, f32[24,2048]{1,0:T(8,128)}, u32[]{:S(2)}) copy-start(f32[24,2048]{1,0:T(8,128)} %param.26) | copy-start | bytes 589828
  512.7 3.5 copy-start.7
  512.7 5.5 %copy-start.6 = (bf16[48,2048]{1,0:T(8,128)(2,1)S(1)}, bf16[48,2048]{1,0:T(8,128)(2,1)}, u32[]{:S(2)}) copy-start(bf16[48,2048]{1,0:T(8,128)(2,1)} %get-tuple-element.64) | copy-start | bytes 589828
  514.0 6.5 %copy-start.4 = (bf16[128,2048]{1,0:T(8,128)(2,1)S(1)}, bf16[128,2048]{1,0:T(8,128)(2,1)}, u32[]{:S(2)}) copy-start(bf16[128,2048]{1,0:T(8,128)(2,1)} %get-tuple-element.92) | copy-start | bytes 1572868
  514.7 6.6 %copy-start.2 = (f32[128,2048]{1,0:T(8,128)S(1)}, f32[128,2048]{1,0:T(8,128)}, u32[]{:S(2)}) copy-start(f32[128,2048]{1,0:T(8,128)} %get-tuple-element.93) | copy-start | bytes 3145732

commit v2 on v1

--- a/solution.py
+++ b/solution.py
@@ -93,6 +93,12 @@
         copy.start()
         return copy
 
+    def sent(self, copies):
+        for copy in copies:
+            copy.wait_send()
+        gone = {id(copy) for copy in copies}
+        self.open = [copy for copy in self.open if id(copy) not in gone]
+
     def finish(self):
         for copy in self.open:
             copy.wait_send()
@@ -112,6 +118,61 @@
 
         count = count + jnp.where(to_me, 0, 1)
     pl.semaphore_wait(bar, count)
+
+
+def to_group(cp, source, dst):
+    g = place()[1]
+    there = dst(g)
+    copies = []
+    for st in GROUP:
+        q = in_group(*st)
+        copies.append(cp.send(source(q["y"] * 2 + q["core"]), there, q))
+    return copies, cp.local(source(g), there)
+
+
+def settle(copies, home):
+    for copy in copies:
+        copy.wait_recv()
+    home.wait()
+
+
+class Shuffle:
+    def __init__(self, outward):
+        p, g = place()
+        self.d = p * 8 + g
+        row = 16 * g + p
+        there = (lax.rem(self.d, 16), lax.div(self.d, 16))
+        here = (lax.div(row, 8), lax.rem(row, 8))
+        to, come = (there, here) if outward else (here, there)
+        self.to = to
+        self.target, self.source = device(*to), device(*come)
+        self.to_me = to[0] * 8 + to[1] == self.d
+        self.from_me = come[0] * 8 + come[1] == self.d
+        self.greeting = (self.source, self.from_me, self.to_me)
+
+    def start(self, cp, src, dst):
+        copy = cp.remote(src, dst, self.target)
+        home = pltpu.make_async_copy(src, dst, cp.sems[2].at[cp.locals])
+        cp.locals += 1
+
+        @pl.when(self.to_me)
+        def _():
+            home.start()
+
+        @pl.when(jnp.logical_not(self.to_me))
+        def _():
+            copy.start()
+
+        return copy, home
+
+    def wait(self, pair):
+        @pl.when(self.to_me)
+        def _():
+            pair[1].wait()
+
+        @pl.when(jnp.logical_not(self.to_me))
+        def _():
+            pair[0].wait()
 
 
 def rings():
@@ -191,17 +252,21 @@
     ]
 
 
-def plane_gather(cp, buf, halves):
+def plane_gather(cp, buf, halves, block=None):
     me = (ax("xlo"), ax("xhi"), ax("z"))
+    home = None if block is None else cp.local(block, buf.at[me])
 
     def view(h, *at):
         return buf.at[at + halves[h]]
 
+    mine = [view(h, *me) if block is None else block.at[halves[h]] for h in range(2)]
     first = []
     for s in STEPS:
-        first.append(cp.send(view(0, *me), view(0, *me), ring("z", s)))
-        first.append(cp.send(view(1, *me), view(1, *me), ring("x", s)))
+        first.append(cp.send(mine[0], view(0, *me), ring("z", s)))
+        first.append(cp.send(mine[1], view(1, *me), ring("x", s)))
     yield
+    if home is not None:
+        home.wait()
     for copy in first:
         copy.wait_recv()
     column = view(0, me[0], me[1], pl.ds(0, 4))
@@ -350,53 +415,26 @@
     )
 
 
-def gather_body(
-    tok, gain, w_in, w_f, w_og, w_o, gu, dn, cot, b3, bo, bgu, bdn, fi, gf, first, send, recv, near
-):
+def gather_body(tok, gain, w_in, w_f, w_og, w_o, b3, bo, fi, first, send, recv, near):
     cp = Copies(send, recv, near)
-    p, g = place()
-    d = p * 8 + g
-    to_p, to_g = lax.rem(d, 16), lax.div(d, 16)
-    from_d = 16 * g + p
-    target = device(to_p, to_g)
-    source = device(lax.div(from_d, 8), lax.rem(from_d, 8))
-    same = to_p * 8 + to_g == d
-    greet(rings() + [in_group(*st) for st in GROUP], (source, from_d == d, same))
+    g = place()[1]
+    shuffle = Shuffle(True)
+    greet(rings() + [in_group(*st) for st in GROUP], shuffle.greeting)
     me = (ax("xlo"), ax("xhi"), ax("z"))
-    mine16 = pl.ds(pl.multiple_of(g * 16, 16), 16)
-    shards = (w_in, w_f, w_og)
     third = w_in.shape[1] // 8
-    locals_ = []
-    arrive3, arrive_gu = [], []
-    for j, w in enumerate(shards):
-        to = b3.at[me + (mine16, pl.ds(j * third, third))]
-        for st in GROUP:
-            q = in_group(*st)
-            k = q["y"] * 2 + q["core"]
-            arrive3.append(cp.send(w.at[:, pl.ds(pl.multiple_of(k * third, 128), third)], to, q))
-        locals_.append(cp.local(w.at[:, pl.ds(pl.multiple_of(g * third, 128), third)], to))
-
-    shuffles = []
-    for src, buf in ((w_o, bo), (dn, bdn)):
-        at = (lax.div(to_p, 8), lax.rem(lax.div(to_p, 4), 2), lax.rem(to_p, 4))
-        copy = cp.remote(src, buf.at[at], target)
-        home = pltpu.make_async_copy(src, buf.at[at], cp.sems[2].at[cp.locals])
-        cp.locals += 1
-
-        @pl.when(same)
-        def _(home=home):
-            home.start()
-
-        @pl.when(jnp.logical_not(same))
-        def _(copy=copy):
-            copy.start()
-
-        shuffles.append((copy, home))
-    to = bgu.at[me + (mine16,)]
-    for st in GROUP:
-        q = in_group(*st)
-        arrive_gu.append(cp.send(gu.at[q["y"] * 2 + q["core"]], to, q))
-    locals_.append(cp.local(gu.at[g], to))
+    arrive = []
+    for j, w in enumerate((w_in, w_f, w_og)):
+        arrive.append(
+            to_group(
+                cp,
+                lambda k, w=w: w.at[:, pl.ds(pl.multiple_of(k * third, 128), third)],
+                lambda k, j=j: b3.at[me + (rows_of(k), pl.ds(j * third, third))],
+            )
+        )
+    q = shuffle.to[0]
+    moved = shuffle.start(
+        cp, w_o, bo.at[lax.div(q, 8), lax.rem(lax.div(q, 4), 2), lax.rem(q, 4)]
+    )
 
     def norm(i, carry):
         r = rows_of(i)
@@ -406,35 +444,17 @@
         return carry
 
     lax.fori_loop(0, tok.shape[0] // 16, norm, 0)
-    chain_fi = group_gather(cp, first, fi)
-    next(chain_fi)
-    chain_g = group_gather(cp, cot, gf)
-    next(chain_g)
-    for copy in arrive3 + arrive_gu:
-        copy.wait_recv()
-    for copy in locals_:
-        copy.wait()
-
-    for copy, home in shuffles:
-
-        @pl.when(same)
-        def _(home=home):
-            home.wait()
-
-        @pl.when(jnp.logical_not(same))
-        def _(copy=copy):
-            copy.wait()
-
-    rows = b3.shape[3]
+    chain = group_gather(cp, first, fi)
+    next(chain)
+    for pair in arrive:
+        settle(*pair)
+    shuffle.wait(moved)
     chains = [
-        plane_gather(cp, b3, by_rows(rows, b3.shape[4])),
-        plane_gather(cp, bo, by_columns(16, bo.shape[4])),
-        plane_gather(cp, bgu, by_rows(rows, bgu.shape[4])),
-        plane_gather(cp, bdn, by_columns(bdn.shape[3], bdn.shape[4])),
-        chain_fi,
-        chain_g,
+        plane_gather(cp, b3, by_rows(*b3.shape[3:])),
+        plane_gather(cp, bo, by_columns(*bo.shape[3:])),
+        chain,
     ]
-    run(chains, (0, 1, 2, 3, 0, 1, 2, 3, 4, 0, 1, 5, 2, 3))
+    run(chains, (0, 1, 0, 1, 0, 1, 2))
     cp.finish()
 
 
@@ -474,15 +494,20 @@
 
 
 def scan_body(
-    proj, lb, gain, gated, states, forget, tot, links, carry, prod, entry, mine, rowsum, rows8, send, recv, near
+    proj, lb, gain, gu, dn, cot, gated, states, forget, tot, links, carry, gf, block_gu, block_dn, prod, entry, mine, rowsum, rows8, send, recv, near
 ):
     cp = Copies(send, recv, near)
+    shuffle = Shuffle(True)
     tiles, rows = states.shape[:2]
     w = 128 * tiles
     steps = rows // 8
     peers_chain = [in_chain(*st) for st in CHAIN]
     peers_group = [in_group(*st) for st in GROUP]
-    greet(peers_chain + peers_group)
+    greet(peers_chain + peers_group, shuffle.greeting)
+    arrive = to_group(cp, lambda k: gu.at[k], lambda k: block_gu.at[rows_of(k), :])
+    moved = shuffle.start(cp, dn, block_dn)
+    chain = group_gather(cp, cot, gf)
+    next(chain)
     low = lb[...]
 
     def gates(i, c):
@@ -553,14 +578,26 @@
         return c
 
     lax.fori_loop(0, 8, gate, 0)
+    settle(*arrive)
+    shuffle.wait(moved)
+    for _ in chain:
+        pass
     cp.finish()
 
 
-def middle_body(part, tok, gain, mid, full, own, near_, far, block, send, recv, near):
+def middle_body(
+    part, tok, gain, block_gu, block_dn, mid, full, bgu, bdn, own, near_, far, block, send, recv, near
+):
     cp = Copies(send, recv, near)
-    greet(ys())
+    greet(ys() + rings())
     sums = []
-    run([group_sum(cp, part, own, near_, far, sums)], ())
+    chains = [
+        group_sum(cp, part, own, near_, far, sums),
+        plane_gather(cp, bgu, by_rows(*bgu.shape[3:]), block_gu),
+        plane_gather(cp, bdn, by_columns(*bdn.shape[3:]), block_dn),
+    ]
+    for i in (0, 1, 2, 0, 1, 2, 0):
+        next(chains[i], None)
 
     def norm(i, carry):
         r = rows_of(i)
@@ -571,19 +608,33 @@
         return carry
 
     lax.fori_loop(0, mid.shape[0] // 16, norm, 0)
-    run([group_gather(cp, block, full)], ())
+    chains[0] = group_gather(cp, block, full)
+    run(chains, (0, 1, 2, 0))
     cp.finish()
 
 
 def turn_body(
-    part, part_r, mid, cot, gain, result, mixed, full, sums_out, own, near_, far, own_r, near_r, far_r, block, send, recv, near
+    part, part_r, mid, cot, gain, dgu, ddn, result, mixed, full, sums_out, block_gu, block_dn, own, near_, far, own_r, near_r, far_r, block, *rest
 ):
-    cp = Copies(send, recv, near)
-    greet(ys())
+    cp = Copies(*rest[-3:])
+    greet(ys() + rings())
     sums, sums_r = [], []
     chain = group_sum(cp, part, own, near_, far, sums)
     chain_r = group_sum(cp, part_r, own_r, near_r, far_r, sums_r)
-    run([chain, chain_r], (0, 0, 1, 1, 0))
+    planes = [
+        plane_sum(cp, dgu, by_rows(*dgu.shape[3:]), *rest[:6], block_gu),
+        plane_sum(cp, ddn, by_columns(*ddn.shape[3:]), *rest[6:12], block_dn),
+    ]
+    next(chain)
+    next(planes[0])
+    next(planes[1])
+    next(chain)
+    next(chain_r)
+    next(chain_r)
+    for _ in chain:
+        pass
+    for _ in chain_r:
+        pass
     sums_out[...] = jnp.zeros_like(sums_out)
 
     def back(i, carry):
@@ -601,20 +652,23 @@
         return carry
 
     lax.fori_loop(0, mid.shape[0] // 16, back, 0)
-    run([group_gather(cp, block, full)], ())
+    run([group_gather(cp, block, full)] + planes, (0, 1, 2, 0))
     cp.finish()
 
 
 def back_body(
-    gg, proj, states, forget, tot, links, carry, lb, gain, grads, sums_out, gs, prod, entry, mine, rowsum, rows8, far, send, recv, near
+    gg, proj, states, forget, tot, links, carry, lb, gain, block_gu, block_dn, grads, sums_out, rgu, rdn, gs, prod, entry, mine, rowsum, rows8, far, send, recv, near
 ):
     cp = Copies(send, recv, near)
+    shuffle = Shuffle(False)
     tiles, rows = states.shape[:2]
     w = 128 * tiles
     steps = rows // 8
     peers_chain = [in_chain(*st) for st in CHAIN]
     peers_group = [in_group(*st) for st in GROUP]
-    greet(peers_chain + peers_group)
+    greet(peers_chain + peers_group, shuffle.greeting)
+    arrive = to_group(cp, lambda k: block_gu.at[rows_of(k), :], lambda k: rgu.at[k])
+    moved = shuffle.start(cp, block_dn, rdn)
     low = lb[...]
     sums_out[...] = jnp.zeros_like(sums_out)
 
@@ -632,7 +686,8 @@
         return c
 
     lax.fori_loop(0, 8, through, 0)
-    for copy in share(cp, rowsum, rows8, place()[1], peers_group):
+    small = share(cp, rowsum, rows8, place()[1], peers_group)
+    for copy in small:
         copy.wait_recv()
     total = rows8[0]
     for j in range(1, 8):
@@ -644,8 +699,7 @@
         put(gs, r, t * (wide(gs, r) - wide(states, r) * t * m))
         return c
 
-    cp.finish()
-    cp.open = []
+    cp.sent(small)
     rowsum[...] = total / (8.0 * w)
     lax.fori_loop(0, 8, norm, 0)
 
@@ -701,40 +755,35 @@
         return c
 
     lax.fori_loop(0, 8, last, 0)
+    settle(*arrive)
+    shuffle.wait(moved)
     cp.finish()
 
 
 def sum_body(*refs):
-    (part, tok, mixed, gain, ffn_sums, mix_sums, d3, do, dgu, ddn) = refs[:10]
-    (gtok, r3, rgu, ro, rdn, totals) = refs[10:16]
-    scratch = list(refs[16:-3])
+    (part, tok, mixed, gain, ffn_sums, mix_sums, d3, do) = refs[:8]
+    (gtok, r3, ro, totals) = refs[8:12]
+    scratch = list(refs[12:-3])
     cp = Copies(*refs[-3:])
     own, near_, far = scratch[:3]
-    plane = [scratch[3 + 6 * i : 9 + 6 * i] for i in range(4)]
-    o3, ogu, oo, od, va, ga, ta, gb, tb = scratch[27:]
+    o3, oo, va, ga, ta, gb, tb = scratch[15:]
     p, g = place()
-    d = p * 8 + g
-    from_d = 16 * g + p
-    same = from_d == d
-    target = device(lax.div(from_d, 8), lax.rem(from_d, 8))
-    source = device(lax.rem(d, 16), lax.div(d, 16))
+    shuffle = Shuffle(False)
     greet(
-        [in_plane(*st) for st in PLANE] + [in_group(*st) for st in GROUP],
-        (source, lax.rem(d, 16) * 8 + lax.div(d, 16) == d, same),
+        [in_plane(*st) for st in PLANE] + [in_group(*st) for st in GROUP], shuffle.greeting
     )
     sums = []
-    rows = d3.shape[3]
     chain = group_sum(cp, part, own, near_, far, sums)
     chains = [
-        plane_sum(cp, dgu, by_rows(rows, dgu.shape[4]), *plane[0], ogu),
-        plane_sum(cp, ddn, by_columns(ddn.shape[3], ddn.shape[4]), *plane[1], od),
-        plane_sum(cp, d3, by_rows(rows, d3.shape[4]), *plane[2], o3),
-        plane_sum(cp, do, by_columns(16, do.shape[4]), *plane[3], oo),
+        plane_sum(cp, d3, by_rows(*d3.shape[3:]), *scratch[3:9], o3),
+        plane_sum(cp, do, by_columns(*do.shape[3:]), *scratch[9:15], oo),
     ]
     next(chain)
     for c in chains:
         next(c)
     next(chain)
+    for c in chains:
+        next(c)
     for _ in chain:
         pass
     va[...] = jnp.zeros_like(va)
@@ -759,8 +808,6 @@
         k = q["y"] * 2 + q["core"]
         small.append(cp.send(va.at[:, pl.ds(pl.multiple_of(k * w, 128), w)], ga.at[g], q))
     ga[pl.ds(g, 1)] = va[:, pl.ds(pl.multiple_of(g * w, 128), w)][None]
-    for c in chains:
-        next(c)
     for copy in small:
         copy.wait_recv()
     acc = ga[0]
@@ -778,44 +825,12 @@
     for c in chains:
         for _ in c:
             pass
-    arrive = []
-    near_copies = []
-    for src, dst in ((ogu, rgu), (o3, r3)):
-        for st in GROUP:
-            q = in_group(*st)
-            k = q["y"] * 2 + q["core"]
-            at = pl.ds(pl.multiple_of(k * 16, 16), 16)
-            arrive.append(cp.send(src.at[at, :], dst.at[g], q))
-        near_copies.append(cp.local(src.at[pl.ds(pl.multiple_of(g * 16, 16), 16), :], dst.at[g]))
-    shuffles = []
-    for src, dst in ((oo, ro), (od, rdn)):
-        copy = cp.remote(src, dst, target)
-        home = pltpu.make_async_copy(src, dst, cp.sems[2].at[cp.locals])
-        cp.locals += 1
-
-        @pl.when(same)
-        def _(home=home):
-            home.start()
-
-        @pl.when(jnp.logical_not(same))
-        def _(copy=copy):
-            copy.start()
-
-        shuffles.append((copy, home))
-    for copy in small + arrive:
-        copy.wait_recv()
-    for copy in near_copies:
-        copy.wait()
-    for copy, home in shuffles:
-
-        @pl.when(same)
-        def _(home=home):
-            home.wait()
-
-        @pl.when(jnp.logical_not(same))
-        def _(copy=copy):
-            copy.wait()
-
+    arrive = to_group(cp, lambda k: o3.at[rows_of(k), :], lambda k: r3.at[k])
+    moved = shuffle.start(cp, oo, ro)
+    for copy in small:
+        copy.wait_recv()
+    settle(*arrive)
+    shuffle.wait(moved)
     cp.finish()
 
 
@@ -854,36 +869,30 @@
     gu = jnp.concatenate([spread(w_gate), spread(w_up)], axis=2)
     dn = jnp.pad(w_down, ((0, padded - down), (0, 0)))
     gains = attn_gain[None, :]
-    b3, bo, bgu, bdn, fi, gf = call(
+    b3, bo, fi = call(
         gather_body,
         "gather",
         0,
         [
             shape((2, 2, 4, 8 * rows, 3 * w), BF),
             shape((2, 2, 4, rows, width), BF),
-            shape((2, 2, 4, 8 * rows, 2 * unit), BF),
-            shape((2, 2, 4, padded, width), BF),
-            shape((8, n, width), BF),
             shape((8, n, width), BF),
         ],
-        [VMEM, VMEM] + [ANY] * 7,
-        [ANY] * 6,
+        [VMEM, VMEM] + [ANY] * 4,
+        [ANY] * 3,
         [pltpu.VMEM((n, width), BF)],
-        110,
-        10,
-    )(tokens, gains, w_input, w_forget, w_outgate, w_out, gu, dn, cotangent)
+        64,
+        8,
+    )(tokens, gains, w_input, w_forget, w_outgate, w_out)
     big3 = b3.reshape(width, 3 * w)
     big_out = bo.reshape(w, width)
-    big_gu = bgu.reshape(width, 2 * unit)
-    big_down = bdn.reshape(unit, width)
     first_full = fi.reshape(8 * n, width)
-    g_full = gf.reshape(8 * n, width)
 
     group = ax("y") * 2 + ax("core")
     lower = bound_value(lax.dynamic_slice_in_dim(bound_table, group * w, w, 1), layer_idx)[None, :]
     mixer_gain = lax.dynamic_slice_in_dim(norm_gain, group * w, w, 0)[None, :]
     proj = dot(first_full, big3, NN)
-    gated, states, forget, tot, links, carry = call(
+    gated, states, forget, tot, links, carry, gf, block_gu, block_dn = call(
         scan_body,
         "scan",
         1,
@@ -894,9 +903,12 @@
             shape((8, n), F32),
             shape((8, 8, w), F32),
             shape((8, w), F32),
+            shape((8, n, width), BF),
+            shape((8 * rows, 2 * unit), BF),
+            shape((padded, width), BF),
         ],
-        [VMEM] * 3,
-        [VMEM] * 6,
+        [VMEM] * 3 + [ANY] * 3,
+        [VMEM] * 6 + [ANY] * 3,
         [
             pltpu.VMEM((w // 128, 8 * n, 128), F32),
             pltpu.VMEM((8, w), F32),
@@ -904,22 +916,30 @@
             pltpu.VMEM((8, n), F32),
             pltpu.VMEM((8, 8, n), F32),
         ],
-        16,
-        2,
-    )(proj, lower, mixer_gain)
+        32,
+        4,
+    )(proj, lower, mixer_gain, gu, dn, cotangent)
+    g_full = gf.reshape(8 * n, width)
     mid_part = dot(gated, big_out, NN).astype(BF).reshape(8, n, width)
     sum_scratch = group_sum_scratch(n, width)
-    mid, si = call(
+    mid, si, bgu, bdn = call(
         middle_body,
         "middle",
         2,
-        [shape((n, width), F32), shape((8, n, width), BF)],
-        [ANY, VMEM, VMEM],
-        [VMEM, ANY],
+        [
+            shape((n, width), F32),
+            shape((8, n, width), BF),
+            shape((2, 2, 4, 8 * rows, 2 * unit), BF),
+            shape((2, 2, 4, padded, width), BF),
+        ],
+        [ANY, VMEM, VMEM, ANY, ANY],
+        [VMEM, ANY, ANY, ANY],
         sum_scratch + [pltpu.VMEM((n, width), BF)],
-        20,
-        8,
-    )(mid_part, tokens, mlp_gain[None, :])
+        48,
+        10,
+    )(mid_part, tokens, mlp_gain[None, :], block_gu, block_dn)
+    big_gu = bgu.reshape(width, 2 * unit)
+    big_down = bdn.reshape(unit, width)
     second_full = si.reshape(8 * n, width)
     gate_up = dot(second_full, big_gu, NN)
     gate_proj, up_proj = gate_up[:, :unit], gate_up[:, unit:]
@@ -933,7 +953,9 @@
     grad_up = (grad_hidden * act).astype(BF)
     grad_gu = jnp.concatenate([grad_gate, grad_up], axis=1)
     second_part = dot(grad_gu, big_gu, NT).astype(BF).reshape(8, n, width)
-    result, mixed, gb, ffn_sums = call(
+    dgu = dot(second_full, grad_gu, TN).astype(BF).reshape(2, 2, 4, 8 * rows, 2 * unit)
+    ddn = dot(hidden, g_full, TN).astype(BF).reshape(2, 2, 4, padded, width)
+    result, mixed, gb, ffn_sums, block_dgu, block_ddn = call(
         turn_body,
         "turn",
         3,
@@ -942,22 +964,33 @@
             shape((n, width), F32),
             shape((8, n, width), BF),
             shape((8, width), F32),
+            shape((8 * rows, 2 * unit), BF),
+            shape((padded, width), BF),
         ],
-        [ANY, ANY, VMEM, VMEM, VMEM],
-        [VMEM, VMEM, ANY, VMEM],
-        sum_scratch + sum_scratch + [pltpu.VMEM((n, width), BF)],
-        32,
-        12,
-    )(second_part, result_part, mid, cotangent, mlp_gain[None, :])
+        [ANY, ANY, VMEM, VMEM, VMEM, ANY, ANY],
+        [VMEM, VMEM, ANY, VMEM, VMEM, VMEM],
+        sum_scratch
+        + sum_scratch
+        + [pltpu.VMEM((n, width), BF)]
+        + plane_sum_scratch(by_rows(8 * rows, 2 * unit))
+        + plane_sum_scratch(by_columns(padded, width)),
+        56,
+        16,
+    )(second_part, result_part, mid, cotangent, mlp_gain[None, :], dgu, ddn)
     branch_full = gb.reshape(8 * n, width)
     grad_gated = dot(branch_full, big_out, NT)
-    grads3, mix_sums = call(
+    grads3, mix_sums, rgu, rdn = call(
         back_body,
         "back",
         4,
-        [shape((8 * n, 3 * w), BF), shape((8, w), F32)],
-        [VMEM] * 9,
-        [VMEM] * 2,
+        [
+            shape((8 * n, 3 * w), BF),
+            shape((8, w), F32),
+            shape((8, rows, 2 * unit), BF),
+            shape((padded, width), BF),
+        ],
+        [VMEM] * 9 + [ANY] * 2,
+        [VMEM] * 2 + [ANY] * 2,
         [
             pltpu.VMEM((w // 128, 8 * n, 128), F32),
             pltpu.VMEM((w // 128, 8 * n, 128), F32),
@@ -967,51 +1000,40 @@
             pltpu.VMEM((8, 8, n), F32),
             pltpu.VMEM((8, 8, w), F32),
         ],
-        16,
-        2,
-    )(grad_gated, proj, states, forget, tot, links, carry, lower, mixer_gain)
+        24,
+        4,
+    )(grad_gated, proj, states, forget, tot, links, carry, lower, mixer_gain, block_dgu, block_ddn)
     first_part = dot(grads3, big3, NT).astype(BF).reshape(8, n, width)
 
     d3 = dot(first_full, grads3, TN).astype(BF).reshape(2, 2, 4, 8 * rows, 3 * w)
     do = dot(gated, branch_full, TN).astype(BF).reshape(2, 2, 4, rows, width)
-    dgu = dot(second_full, grad_gu, TN).astype(BF).reshape(2, 2, 4, 8 * rows, 2 * unit)
-    ddn = dot(hidden, g_full, TN).astype(BF).reshape(2, 2, 4, padded, width)
-    plane_scratch = (
-        plane_sum_scratch(by_rows(8 * rows, 2 * unit))
-        + plane_sum_scratch(by_columns(padded, width))
-        + plane_sum_scratch(by_rows(8 * rows, 3 * w))
-        + plane_sum_scratch(by_columns(rows, width))
-    )
-    grad_tokens, r3, rgu, ro, rdn, totals = call(
+    grad_tokens, r3, ro, totals = call(
         sum_body,
         "sums",
         5,
         [
             shape((n, width), F32),
             shape((8, rows, 3 * w), BF),
-            shape((8, rows, 2 * unit), BF),
             shape((rows, width), BF),
-            shape((padded, width), BF),
             shape((8, 8, w), F32),
         ],
-        [ANY, VMEM, VMEM, VMEM, VMEM, VMEM] + [ANY] * 4,
-        [VMEM, VMEM, VMEM, VMEM, VMEM, VMEM],
+        [ANY, VMEM, VMEM, VMEM, VMEM, VMEM] + [ANY] * 2,
+        [VMEM, VMEM, VMEM, VMEM],
         sum_scratch
-        + plane_scratch
+        + plane_sum_scratch(by_rows(8 * rows, 3 * w))
+        + plane_sum_scratch(by_columns(rows, width))
         + [
             pltpu.VMEM((8 * rows, 3 * w), BF),
-            pltpu.VMEM((8 * rows, 2 * unit), BF),
             pltpu.VMEM((rows, width), BF),
-            pltpu.VMEM((padded, width), BF),
             pltpu.VMEM((8, width), F32),
             pltpu.VMEM((8, 8, w), F32),
             pltpu.VMEM((8, w), F32),
             pltpu.VMEM((16, 8, w), F32),
             pltpu.VMEM((8, w), F32),
         ],
-        110,
-        18,
-    )(first_part, tokens, mixed, gains, ffn_sums, mix_sums, d3, do, dgu, ddn)
+        80,
+        16,
+    )(first_part, tokens, mixed, gains, ffn_sums, mix_sums, d3, do)
 
     def join(m):
         m = m.transpose(1, 0, 2)

time: 530 us -> 431 us (0.81)
  Pallas kernels: 418 us -> 323 us
    pallas_call x1, Pallas kernels: 123 us -> 51.2 us  [on_device(): call(sum_body, 'sums', 5, [shape((n, width), F32), shape((8, rows, 3 * w)...]
    pallas_call x1, Pallas kernels: 106 us -> 44 us  [on_device(): call(gather_body, 'gather', 0, [shape((2, 2, 4, 8 * rows, 3 * w), BF), sh...]
    pallas_call x1, Pallas kernels: 21.5 us -> 49.1 us  [on_device(): call(scan_body, 'scan', 1, [shape((8 * n, w), BF), shape((w // 128, 8 * n...]
    pallas_call x1, Pallas kernels: 22.2 us -> 31.3 us  [on_device(): call(back_body, 'back', 4, [shape((8 * n, 3 * w), BF), shape((8, w), F32)...]
where the time goes in v2:
time: 431 us; the launch traced here: 423 us
  Pallas kernels  323 us (75%)
  matrix products  74.2 us (17%)
  local copies, waits for them, and re-layouts  15.8 us (4%)
  other arithmetic  8.09 us (2%)
    pallas_call x1, Pallas kernels, on_device(): call(turn_body, 'turn', 3, [shape((n, width), BF), shape((n, width), F32)...  85.4 us
    dot_general x12, matrix products, dot(): return lax.dot_general(a, b, (dims, ((), ())), preferred_element_type=F32)  74.2 us
    pallas_call x1, Pallas kernels, on_device(): call(middle_body, 'middle', 2, [shape((n, width), F32), shape((8, n, widt...  62.2 us
    pallas_call x1, Pallas kernels, on_device(): call(sum_body, 'sums', 5, [shape((n, width), F32), shape((8, rows, 3 * w)...  51.2 us
    pallas_call x1, Pallas kernels, on_device(): call(scan_body, 'scan', 1, [shape((8 * n, w), BF), shape((w // 128, 8 * n...  49.1 us
    pallas_call x1, Pallas kernels, on_device(): call(gather_body, 'gather', 0, [shape((2, 2, 4, 8 * rows, 3 * w), BF), sh...  44 us
    pallas_call x1, Pallas kernels, on_device(): call(back_body, 'back', 4, [shape((8 * n, 3 * w), BF), shape((8, w), F32)...  31.3 us

profile of v2, /device:TPU:1, one launch (start us, length us, event | category | flops | bytes accessed | tf_op | source)
XLA Modules:
  0.0 423.4 jit_solution(1177186577732605890)
XLA Ops:
  2.8 1.4 multiply_reduce_fusion
  4.2 1.3 dynamic_slice.7
  5.6 44.0 %gather.1 = (bf16[2,2,4,128,768]{4,3,2,1,0:T(8,128)(2,1)}, bf16[2,2,4,16,2048]{4,3,2,1,0:T(8,128)(2,1)}, bf16[8,128,2048]{2,1,0:T(8,128)(2,1)}) custom-call(bf16[128,2048]{1,0:T(8,128)(2,1)} %refs_1_.1, f32[1,2048]{1,0:T(1,128)} %bitcast.86, bf16[16,2048]{1,0:T(8,128)(2,1)} %w_in.1, bf16[16,2048]{1,0:T(8,128)(2,1)} %w_f.1, bf16[16,2048]{1,0:T(8,128)(2,1)} %w_og.1, ...), custom_call_target="tpu_custom_call" | custom-call | tf_op jit(solution)/shard_map/gather/pallas_call | solution.py:872
  49.6 8.3 %fusion.10.proj = f32[1024,768]{1,0:T(8,128)} fusion(bf16[1024,2048]{1,0:T(8,128)(2,1)} %bitcast.100, bf16[2048,768]{1,0:T(8,128)(2,1)} %bitcast.108), kind=kOutput, calls=%fused_computation.42 | convolution fusion | flops 3221225472 | bytes 10485760 | tf_op jit(solution)/shard_map/dot_general | solution.py:845
  58.0 1.5 reshape.145
  60.1 1.5 reshape.147
  62.3 0.8 pad_maximum_fusion.3.gu
  63.8 49.1 %scan.1 = (bf16[1024,256]{1,0:T(8,128)(2,1)}, f32[2,1024,128]{2,1,0:T(8,128)}, f32[2,1024,128]{2,1,0:T(8,128)}, f32[8,128]{1,0:T(8,128)}, f32[8,8,256]{2,1,0:T(8...) custom-call(f32[1024,768]{1,0:T(8,128)} %fusion.10.proj, ...), custom_call_target="tpu_custom_call" | custom-call | tf_op jit(solution)/shard_map/scan/pallas_call | solution.py:895
  112.9 4.3 %convolution_convert_fusion.2 = bf16[1024,2048]{1,0:T(8,128)(2,1)} fusion(bf16[1024,256]{1,0:T(8,128)(2,1)} %get-tuple-element.46, bf16[256,2048]{1,0:T(8,128)(2,1)S(1)} %bitcast.77), kind=kOutput, calls=%fused_computation.2 | convolution fusion | flops 1075838976 | bytes 5767168 | tf_op jit(solution)/shard_map/dot_general | solution.py:845
  117.2 62.2 %middle.1 = (f32[128,2048]{1,0:T(8,128)}, bf16[8,128,2048]{2,1,0:T(8,128)(2,1)}, bf16[2,2,4,128,1536]{4,3,2,1,0:T(8,128)(2,1)}, bf16[2,2,4,48,2048]{4,3,2,1,0:T(8,128)(2,1)}) custom-call(bf16[8,128,2048]{2,1,0:T(8,128)(2,1)} %bitcast.69, bf16[128,2048]{1,0:T(8,128)(2,1)} %refs_1_.1, f32[1,2048]{1,0:T(1,128)} %bitcast.84, ...), custom_call_target="tpu_custom_call" | custom-call | tf_op jit(solution)/shard_map/middle/pallas_call | solution.py:925
  179.4 10.5 %fusion.11 = f32[1024,1536]{0,1:T(8,128)S(1)} fusion(bf16[1024,2048]{1,0:T(8,128)(2,1)} %bitcast.104, bf16[2048,1536]{1,0:T(8,128)(2,1)} %bitcast.96), kind=kOutput, calls=%fused_computation.43 | convolution fusion | flops 6442450944 | bytes 16777216 | tf_op jit(solution)/shard_map/dot_general | solution.py:845
  189.9 4.6 %multiply_convert_fusion.2 = (bf16[1024,768]{0,1:T(8,128)(2,1)S(1)}, bf16[1024,768]{0,1:T(8,128)(2,1)S(1)}, bf16[1024,768]{0,1:T(8,128)(2,1)S(1)}) fusion(f32[1024,1536]{0,1:T(8,128)S(1)} %fusion.11, bf16[1024,2048]{1,0:T(8,128)(2,1)S(1)} %bitcast.102, bf16[768,2048]{1,0:T(8,128)(2,1)S(1)} %bitcast.110), kind=kOutput, calls=%fused_computation.10 | convolution fusion | flops 3233021952 | bytes 18350080 | tf_op jit(solution)/shard_map/dot_general | solution.py:845
  194.5 4.8 %convolution_convert_fusion.6 = bf16[768,2048]{1,0:T(8,128)(2,1)} fusion(bf16[1024,768]{0,1:T(8,128)(2,1)S(1)} %get-tuple-element.75, bf16[1024,2048]{1,0:T(8,128)(2,1)S(1)} %bitcast.103), kind=kOutput, calls=%fused_computation.6 | convolution fusion | flops 3222798336 | bytes 8912896 | tf_op jit(solution)/shard_map/dot_general | solution.py:845
  199.4 9.7 %convolution_convert_fusion = bf16[2048,1536]{1,0:T(8,128)(2,1)} fusion(bf16[1024,2048]{1,0:T(8,128)(2,1)S(1)} %bitcast.105, bf16[1024,768]{0,1:T(8,128)(2,1)S(1)} %get-tuple-element.74, bf16[1024,768]{0,1:T(8,128)(2,1)S(1)} %get-tuple-element.73), kind=kOutput, calls=%fused_computation | convolution fusion | flops 6451888128 | bytes 13631488 | tf_op jit(solution)/shard_map/dot_general | solution.py:845
  209.1 5.1 %convolution_convert_fusion.4 = bf16[1024,2048]{1,0:T(8,128)(2,1)} fusion(bf16[1024,768]{0,1:T(8,128)(2,1)S(1)} %get-tuple-element.75, bf16[768,2048]{1,0:T(8,128)(2,1)S(1)} %bitcast.111), kind=kOutput, calls=%fused_computation.4 | convolution fusion | flops 3223322624 | bytes 8912896 | tf_op jit(solution)/shard_map/dot_general | solution.py:845
  214.2 8.4 %convolution_convert_fusion.1 = bf16[1024,2048]{1,0:T(8,128)(2,1)} fusion(bf16[2048,1536]{1,0:T(8,128)(2,1)S(1)} %bitcast.99, bf16[1024,768]{0,1:T(8,128)(2,1)S(1)} %get-tuple-element.74, bf16[1024,768]{0,1:T(8,128)(2,1)S(1)} %get-tuple-element.73), kind=kOutput, calls=%fused_computation.1 | convolution fusion | flops 6450839552 | bytes 13631488 | tf_op jit(solution)/shard_map/dot_general | solution.py:845
  222.5 85.4 %turn.1 = (bf16[128,2048]{1,0:T(8,128)(2,1)}, f32[128,2048]{1,0:T(8,128)}, bf16[8,128,2048]{2,1,0:T(8,128)(2,1)}, f32[8,2048]{1,0:T(8,128)}, bf16[128,1536]{1,0:T(8,128)(2,1)}, /*index=5*/bf16[48,2048]{1,0:T(8,128)(2,1)}) custom-call(bf16[8,128,2048]{2,1,0:T(8,128)(2,1)} %bitcast.73, bf16[8,128,2048]{2,1,0:T(8,128)(2,1)} %bitcast.72, ...), custom_call_target="tpu_custom_call" | custom-call | tf_op jit(solution)/shard_map/turn/pallas_call | solution.py:958
  308.0 4.6 %convolution_convert_fusion.7 = bf16[256,2048]{1,0:T(8,128)(2,1)} fusion(bf16[1024,256]{1,0:T(8,128)(2,1)S(1)} %copy-done.1, bf16[1024,2048]{1,0:T(8,128)(2,1)} %bitcast.106), kind=kOutput, calls=%fused_computation.13 | convolution fusion | flops 1074266112 | bytes 5767168 | tf_op jit(solution)/shard_map/dot_general | solution.py:845
  312.6 2.3 fusion.12.gg
  314.9 31.3 %back.1 = (bf16[1024,768]{1,0:T(8,128)(2,1)}, f32[8,256]{1,0:T(8,128)}, bf16[8,16,1536]{2,1,0:T(8,128)(2,1)}, bf16[48,2048]{1,0:T(8,128)(2,1)}) custom-call(f32[1024,256]{1,0:T(8,128)} %fusion.12.gg, f32[1024,768]{1,0:T(8,128)} %fusion.10.proj, f32[2,1024,128]{2,1,0:T(8,128)} %get-tuple-element.56.states, f32[2,1024,128]{2,1,0:T(8,128)} %get-tuple-element.57.forget, ...), custom_call_target="tpu_custom_call" | custom-call | tf_op jit(solution)/shard_map/back/pallas_call | solution.py:982
  346.2 6.6 %convolution_convert_fusion.5 = bf16[2048,768]{1,0:T(8,128)(2,1)} fusion(bf16[1024,2048]{1,0:T(8,128)(2,1)S(1)} %bitcast.101, bf16[1024,768]{1,0:T(8,128)(2,1)} %get-tuple-element.63), kind=kOutput, calls=%fused_computation.5 | convolution fusion | flops 3222798336 | bytes 8912896 | tf_op jit(solution)/shard_map/dot_general | solution.py:845
  352.8 5.0 %convolution_convert_fusion.3 = bf16[1024,2048]{1,0:T(8,128)(2,1)} fusion(bf16[1024,768]{1,0:T(8,128)(2,1)S(1)} %copy-done.16, bf16[2048,768]{1,0:T(8,128)(2,1)S(1)} %bitcast.109), kind=kOutput, calls=%fused_computation.3 | convolution fusion | flops 3223322624 | bytes 8912896 | tf_op jit(solution)/shard_map/dot_general | solution.py:845
  357.8 51.2 %sums.1 = (f32[128,2048]{1,0:T(8,128)}, bf16[8,16,768]{2,1,0:T(8,128)(2,1)}, bf16[16,2048]{1,0:T(8,128)(2,1)}, f32[8,8,256]{2,1,0:T(8,128)}) custom-call(bf16[8,128,2048]{2,1,0:T(8,128)(2,1)} %bitcast.71, bf16[128,2048]{1,0:T(8,128)(2,1)} %refs_1_.1, f32[128,2048]{1,0:T(8,128)} %get-tuple-element.64.refs_2_, f32[1,2048]{1,0:T(1,128)} %bitcast.87, ...), custom_call_target="tpu_custom_call" | custom-call | tf_op jit(solution)/shard_map/sums/pallas_call | solution.py:1010
  409.0 1.6 fusion.9
  410.8 0.8 fusion.2
  411.6 0.9 convert_bitcast_fusion
  414.6 1.5 convert_element_type.103
  416.9 1.3 reshape.168
  419.1 1.3 reshape.169
  420.4 0.8 slice_convert_fusion.2
  421.2 0.8 copy.47
  422.0 1.0 copy.48
  (63 shorter events, 7.4 us)
Async XLA Ops:
  49.6 8.4 %copy-start.8 = (bf16[16,5632]{1,0:T(8,128)(2,1)S(1)}, bf16[16,5632]{1,0:T(8,128)(2,1)}, u32[]{:S(2)}) copy-start(bf16[16,5632]{1,0:T(8,128)(2,1)} %param.23) | copy-start | bytes 540676
  49.6 10.5 %copy-start.9 = (bf16[16,5632]{1,0:T(8,128)(2,1)S(1)}, bf16[16,5632]{1,0:T(8,128)(2,1)}, u32[]{:S(2)}) copy-start(bf16[16,5632]{1,0:T(8,128)(2,1)} %param.24) | copy-start | bytes 540676
  58.0 5.1 %copy-start.6 = (bf16[44,2048]{1,0:T(8,128)(2,1)S(1)}, bf16[44,2048]{1,0:T(8,128)(2,1)}, u32[]{:S(2)}) copy-start(bf16[44,2048]{1,0:T(8,128)(2,1)} %param.25) | copy-start | bytes 540676
  62.2 50.7 %copy-start.3 = (bf16[2,2,4,16,2048]{4,3,2,1,0:T(8,128)(2,1)S(1)}, bf16[2,2,4,16,2048]{4,3,2,1,0:T(8,128)(2,1)}, u32[]{:S(2)}) copy-start(bf16[2,2,4,16,2048]{4,3,2,1,0:T(8,128)(2,1)} %get-tuple-element.47) | copy-start | bytes 3145732
  179.4 10.5 %copy-start.11 = (bf16[8,128,2048]{2,1,0:T(8,128)(2,1)S(1)}, bf16[8,128,2048]{2,1,0:T(8,128)(2,1)}, u32[]{:S(2)}) copy-start(bf16[8,128,2048]{2,1,0:T(8,128)(2,1)} %get-tuple-element.45) | copy-start | bytes 12582916
  179.4 10.5 %copy-start.15 = (bf16[2,2,4,48,2048]{4,3,2,1,0:T(8,128)(2,1)S(1)}, bf16[2,2,4,48,2048]{4,3,2,1,0:T(8,128)(2,1)}, u32[]{:S(2)}) copy-start(bf16[2,2,4,48,2048]{4,3,2,1,0:T(8,128)(2,1)} %get-tuple-element.50) | copy-start | bytes 9437188
  194.5 4.9 %copy-start.12 = (bf16[8,128,2048]{2,1,0:T(8,128)(2,1)S(1)}, bf16[8,128,2048]{2,1,0:T(8,128)(2,1)}, u32[]{:S(2)}) copy-start(bf16[8,128,2048]{2,1,0:T(8,128)(2,1)} %get-tuple-element.51) | copy-start | bytes 12582916
  194.5 19.7 %slice-start = ((s8[6291456]{0:T(1024)(128)(4,1)}), s8[4194304]{0:T(1024)(128)(4,1)S(1)}, s32[]{:S(2)}) async-start(s8[6291456]{0:T(1024)(128)(4,1)} %bitcast.97), calls=%async_computation | async-start | bytes 8388608
  199.4 14.8 %slice-start.1 = ((s8[6291456]{0:T(1024)(128)(4,1)}), s8[2097152]{0:T(1024)(128)(4,1)S(1)}, s32[]{:S(2)}) async-start(s8[6291456]{0:T(1024)(128)(4,1)} %bitcast.97), calls=%async_computation.1 | async-start | bytes 4194304
  222.5 85.4 %copy-start.1 = (bf16[1024,256]{1,0:T(8,128)(2,1)S(1)}, bf16[1024,256]{1,0:T(8,128)(2,1)}, u32[]{:S(2)}) copy-start(bf16[1024,256]{1,0:T(8,128)(2,1)} %get-tuple-element.46) | copy-start | bytes 1572868
  308.0 4.6 %copy-start.13 = (bf16[8,128,2048]{2,1,0:T(8,128)(2,1)S(1)}, bf16[8,128,2048]{2,1,0:T(8,128)(2,1)}, u32[]{:S(2)}) copy-start(bf16[8,128,2048]{2,1,0:T(8,128)(2,1)} %get-tuple-element.55) | copy-start | bytes 12582916
  314.9 31.3 %copy-start.10 = (bf16[8,128,2048]{2,1,0:T(8,128)(2,1)S(1)}, bf16[8,128,2048]{2,1,0:T(8,128)(2,1)}, u32[]{:S(2)}) copy-start(bf16[8,128,2048]{2,1,0:T(8,128)(2,1)} %get-tuple-element.43) | copy-start | bytes 12582916
  346.2 6.6 %copy-start.14 = (bf16[2,2,4,128,768]{4,3,2,1,0:T(8,128)(2,1)S(1)}, bf16[2,2,4,128,768]{4,3,2,1,0:T(8,128)(2,1)}, u32[]{:S(2)}) copy-start(bf16[2,2,4,128,768]{4,3,2,1,0:T(8,128)(2,1)} %get-tuple-element.44) | copy-start | bytes 9437188
  346.2 6.6 %copy-start.16 = (bf16[1024,768]{1,0:T(8,128)(2,1)S(1)}, bf16[1024,768]{1,0:T(8,128)(2,1)}, u32[]{:S(2)}) copy-start(bf16[1024,768]{1,0:T(8,128)(2,1)} %get-tuple-element.63) | copy-start | bytes 4718596
  357.8 52.8 %copy-start = (f32[24,2048]{1,0:T(8,128)S(1)}, f32[24,2048]{1,0:T(8,128)}, u32[]{:S(2)}) copy-start(f32[24,2048]{1,0:T(8,128)} %param.26) | copy-start | bytes 589828
  357.8 58.3 %copy-start.5 = (bf16[8,16,1536]{2,1,0:T(8,128)(2,1)S(1)}, bf16[8,16,1536]{2,1,0:T(8,128)(2,1)}, u32[]{:S(2)}) copy-start(bf16[8,16,1536]{2,1,0:T(8,128)(2,1)} %get-tuple-element.71) | copy-start | bytes 1179652
  416.9 3.5 copy-start.7
  416.9 4.3 %copy-start.4 = (bf16[128,2048]{1,0:T(8,128)(2,1)S(1)}, bf16[128,2048]{1,0:T(8,128)(2,1)}, u32[]{:S(2)}) copy-start(bf16[128,2048]{1,0:T(8,128)(2,1)} %get-tuple-element.100) | copy-start | bytes 1572868
  418.3 3.7 copy-start.2

commit v3 on v2

v3 whole, which is shorter than its diff:
```python
from types import SimpleNamespace

import jax
import jax.numpy as jnp
from jax import lax
from jax.experimental import pallas as pl
from jax.experimental.pallas import tpu as pltpu
from jax.sharding import Mesh, PartitionSpec as P

EPS = 1e-06
BF = jnp.bfloat16
F32 = jnp.float32
AXES = ("xlo", "xhi", "z", "y", "core")
MESH = pl.DeviceIdType.MESH
ANY = pl.BlockSpec(memory_space=pl.ANY)
VMEM = pl.BlockSpec(memory_space=pltpu.VMEM)
STEPS = (1, 3, 2)
GROUP = [(a, b) for a in range(4) for b in range(2) if a or b]
CHAIN = [(a, b) for a in range(2) for b in range(4) if a or b]
PLANE = [(a, b) for a in range(4) for b in range(4) if a or b]
HIGH = lax.Precision.HIGHEST


def ax(name):
    return lax.axis_index(name)


def ring(axis, s):
    if axis == "x":
        x = lax.rem(ax("xhi") * 2 + ax("xlo") + s, 4)
        return {"xhi": lax.div(x, 2), "xlo": lax.rem(x, 2)}
    return {axis: lax.rem(ax(axis) + s, 4)}


def sibling():
    return {"core": 1 - ax("core")}


def in_group(s, t):
    return {"y": lax.rem(ax("y") + s, 4), "core": lax.rem(ax("core") + t, 2)}


def in_chain(s, t):
    return {"xhi": lax.rem(ax("xhi") + s, 2), "z": lax.rem(ax("z") + t, 4)}


def in_plane(s, t):
    return {**ring("x", s), **ring("z", t)}


def place():
    return ax("xlo") * 8 + ax("xhi") * 4 + ax("z"), ax("y") * 2 + ax("core")


def device(p, g):
    return {
        "xlo": lax.div(p, 8),
        "xhi": lax.rem(lax.div(p, 4), 2),
        "z": lax.rem(p, 4),
        "y": lax.div(g, 2),
        "core": lax.rem(g, 2),
    }


class Copies:
    def __init__(self, send, recv, near):
        self.sems = (send, recv, near)
        self.count = 0
        self.locals = 0
        self.open = []

    def remote(self, src, dst, dev):
        i = self.count
        self.count += 1
        return pltpu.make_async_remote_copy(
            src_ref=src,
            dst_ref=dst,
            send_sem=self.sems[0].at[i],
            recv_sem=self.sems[1].at[i],
            device_id=dev,
            device_id_type=MESH,
        )

    def send(self, src, dst, dev):
        copy = self.remote(src, dst, dev)
        copy.start()
        self.open.append(copy)
        return copy

    def local(self, src, dst):
        copy = pltpu.make_async_copy(src, dst, self.sems[2].at[self.locals])
        self.locals += 1
        copy.start()
        return copy

    def sent(self, copies):
        for copy in copies:
            copy.wait_send()
        gone = {id(copy) for copy in copies}
        self.open = [copy for copy in self.open if id(copy) not in gone]

    def finish(self):
        for copy in self.open:
            copy.wait_send()


def greet(peers, shuffle=None):
    bar = pltpu.get_barrier_semaphore()
    for dev in peers:
        pl.semaphore_signal(bar, inc=1, device_id=dev, device_id_type=MESH)
    count = len(peers)
    if shuffle is not None:
        source, from_me, to_me = shuffle

        @pl.when(jnp.logical_not(from_me))
        def _():
            pl.semaphore_signal(bar, inc=1, device_id=source, device_id_type=MESH)

        count = count + jnp.where(to_me, 0, 1)
    pl.semaphore_wait(bar, count)


def to_group(cp, source, dst):
    g = place()[1]
    there = dst(g)
    copies = []
    for st in GROUP:
        q = in_group(*st)
        copies.append(cp.send(source(q["y"] * 2 + q["core"]), there, q))
    return copies, cp.local(source(g), there)


def settle(copies, home):
    for copy in copies:
        copy.wait_recv()
    home.wait()


class Shuffle:
    def __init__(self, outward):
        p, g = place()
        self.d = p * 8 + g
        row = 16 * g + p
        there = (lax.rem(self.d, 16), lax.div(self.d, 16))
        here = (lax.div(row, 8), lax.rem(row, 8))
        to, come = (there, here) if outward else (here, there)
        self.to = to
        self.target, self.source = device(*to), device(*come)
        self.to_me = to[0] * 8 + to[1] == self.d
        self.from_me = come[0] * 8 + come[1] == self.d
        self.greeting = (self.source, self.from_me, self.to_me)

    def start(self, cp, src, dst):
        copy = cp.remote(src, dst, self.target)
        home = pltpu.make_async_copy(src, dst, cp.sems[2].at[cp.locals])
        cp.locals += 1

        @pl.when(self.to_me)
        def _():
            home.start()

        @pl.when(jnp.logical_not(self.to_me))
        def _():
            copy.start()

        return copy, home

    def wait(self, pair):
        @pl.when(self.to_me)
        def _():
            pair[1].wait()

        @pl.when(jnp.logical_not(self.to_me))
        def _():
            pair[0].wait()


def rings():
    return [ring("x", s) for s in STEPS] + [ring("z", s) for s in STEPS]


def ys():
    return [ring("y", s) for s in STEPS] + [sibling()]


def run(chains, order):
    for i in order:
        next(chains[i], None)
    for chain in chains:
        for _ in chain:
            pass


def rows_of(i, n=16):
    return pl.ds(pl.multiple_of(i * n, n), n)


def block_of(k):
    return rows_of(k, 128)


class GroupGather:
    def __init__(self, cp, src, full):
        self.cp, self.full = cp, full
        self.at = full.at[block_of(place()[1])]
        self.moved = {s: cp.send(src, self.at, ring("y", s)) for s in STEPS}
        self.near = {0: cp.send(src, self.at, sibling())}

    def forward(self, s):
        self.moved[s].wait_recv()
        k = 2 * lax.rem(ax("y") + 4 - s, 4) + ax("core")
        at = self.full.at[block_of(k)]
        self.near[s] = self.cp.send(at, at, sibling())

    def ready(self, s):
        self.near[s].wait_recv()

    def rest(self):
        for s in STEPS:
            if s not in self.near:
                self.forward(s)
        for s in (0, 1, 3, 2):
            self.ready(s)


class GroupSum:
    def __init__(self, cp, near, far):
        self.cp, self.near, self.far = cp, near, far
        self.sent, self.moved = {}, {}

    def chip(self, s):
        return 2 * lax.rem(ax("y") + s, 4)

    def give(self, s, src):
        self.sent[s] = self.cp.send(src, self.near.at[s], sibling())

    def add(self, s, mine, at):
        near = self.near
        self.sent[s].wait_recv()

        def step(i, carry):
            r = rows_of(i)
            to = pl.ds(pl.multiple_of(at + i * 16, 16), 16)
            mine[to, :] = (mine[to, :].astype(F32) + near[s, r, :].astype(F32)).astype(BF)
            return carry

        lax.fori_loop(0, 8, step, 0)
        here = mine.at[pl.ds(pl.multiple_of(at, 128), 128)]
        self.moved[s] = self.cp.send(here, self.far.at[s - 1], ring("y", s))

    def total(self, mine, at):
        self.sent[0].wait_recv()
        for s in STEPS:
            self.moved[s].wait_recv()
        self.cp.sent(list(self.moved.values()))
        near, far = self.near, self.far

        def rows(i):
            r = rows_of(i)
            own = mine[pl.ds(pl.multiple_of(at + i * 16, 16), 16), :]
            acc = own.astype(F32) + near[0, r, :].astype(F32)
            for s in range(3):
                acc = acc + far[s, r, :].astype(F32)
            return acc

        return rows


def sum_of(cp, part, mine, near, far):
    total = GroupSum(cp, near, far)
    c = ax("core")
    own = {}
    for s in (2, 1, 3, 0):
        total.give(s, part.at[block_of(total.chip(s) + 1 - c)])
        own[s] = cp.local(part.at[block_of(total.chip(s) + c)], mine.at[pl.ds(128 * s, 128)])
    yield
    for s in (2, 1, 3):
        own[s].wait()
        total.add(s, mine, 128 * s)
    own[0].wait()
    yield
    yield total.total(mine, 0)


def plane_gather(cp, buf, halves, block=None):
    me = (ax("xlo"), ax("xhi"), ax("z"))
    home = None if block is None else cp.local(block, buf.at[me])

    def view(h, *at):
        return buf.at[at + halves[h]]

    mine = [view(h, *me) if block is None else block.at[halves[h]] for h in range(2)]
    first = []
    for s in STEPS:
        first.append(cp.send(mine[0], view(0, *me), ring("z", s)))
        first.append(cp.send(mine[1], view(1, *me), ring("x", s)))
    yield
    if home is not None:
        home.wait()
    for copy in first:
        copy.wait_recv()
    column = view(0, me[0], me[1], pl.ds(0, 4))
    row = view(1, pl.ds(0, 2), pl.ds(0, 2), me[2])
    wide = {}
    for s in (1, 3):
        wide["x", s] = cp.send(column, column, ring("x", s))
        wide["z", s] = cp.send(row, row, ring("z", s))
    yield
    last = []
    for s in (1, 3):
        back = ring("x", 4 - s)
        wide["x", s].wait_recv()
        v = view(0, back["xlo"], back["xhi"], pl.ds(0 if s == 1 else 2, 2))
        last.append(cp.send(v, v, ring("x", s)))
        back = ring("z", 4 - s)
        wide["z", s].wait_recv()
        v = view(1, 0 if s == 1 else 1, pl.ds(0, 2), back["z"])
        last.append(cp.send(v, v, ring("z", s)))
    yield
    for copy in last:
        copy.wait_recv()


def half_shapes(halves):
    return [tuple(d.size for d in h) for h in halves]


def plane_sum_scratch(halves):
    a, b = half_shapes(halves)
    return [
        pltpu.VMEM((4,) + a, BF),
        pltpu.VMEM((3, 4) + a, BF),
        pltpu.VMEM((3,) + a, BF),
        pltpu.VMEM((2, 2) + b, BF),
        pltpu.VMEM((3, 2, 2) + b, BF),
        pltpu.VMEM((3,) + b, BF),
    ]


def plane_sum(cp, part, halves, own_a, far_a, last_a, own_b, far_b, last_b, out):
    me = (ax("xlo"), ax("xhi"), ax("z"))
    shape_a, shape_b = half_shapes(halves)

    def view(h, *at):
        return part.at[at + halves[h]]

    near_a = cp.local(view(0, me[0], me[1], pl.ds(0, 4)), own_a)
    near_b = cp.local(view(1, pl.ds(0, 2), pl.ds(0, 2), me[2]), own_b)
    first_a, first_b = [], []
    for j, s in enumerate(STEPS):
        d = ring("x", s)
        first_a.append(cp.send(view(0, d["xlo"], d["xhi"], pl.ds(0, 4)), far_a.at[j], d))
        d = ring("z", s)
        first_b.append(cp.send(view(1, pl.ds(0, 2), pl.ds(0, 2), d["z"]), far_b.at[j], d))
    yield
    near_a.wait()
    for copy in first_a:
        copy.wait_recv()
    for k in range(4):

        def add(i, carry, k=k):
            r = rows_of(i)
            acc = own_a[k, r, :].astype(F32)
            for j in range(3):
                acc = acc + far_a[j, k, r, :].astype(F32)
            own_a[k, r, :] = acc.astype(BF)
            return carry

        lax.fori_loop(0, shape_a[0] // 16, add, 0)
    second = []
    for j, s in enumerate(STEPS):
        d = ring("z", s)
        second.append(cp.send(own_a.at[d["z"]], last_a.at[j], d))
    near_b.wait()
    for copy in first_b:
        copy.wait_recv()
    for k in range(4):

        def add(i, carry, k=k):
            r = rows_of(i)
            acc = own_b[k // 2, k % 2, r, :].astype(F32)
            for j in range(3):
                acc = acc + far_b[j, k // 2, k % 2, r, :].astype(F32)
            own_b[k // 2, k % 2, r, :] = acc.astype(BF)
            return carry

        lax.fori_loop(0, shape_b[0] // 16, add, 0)
    for j, s in enumerate(STEPS):
        d = ring("x", s)
        second.append(cp.send(own_b.at[d["xlo"], d["xhi"]], last_b.at[j], d))
    yield
    for copy in second:
        copy.wait_recv()

    def end_a(i, carry):
        r = rows_of(i)
        acc = own_a[me[2], r, :].astype(F32)
        for j in range(3):
            acc = acc + last_a[j, r, :].astype(F32)
        at = rows_of(i) if halves[0][0].start == 0 else pl.ds(halves[0][0].start + i * 16, 16)
        out[at, halves[0][1]] = acc.astype(BF)
        return carry

    lax.fori_loop(0, shape_a[0] // 16, end_a, 0)

    def end_b(i, carry):
        r = rows_of(i)
        acc = own_b[me[0], me[1], r, :].astype(F32)
        for j in range(3):
            acc = acc + last_b[j, r, :].astype(F32)
        at = pl.ds(pl.multiple_of(halves[1][0].start + i * 16, 16), 16)
        out[at, halves[1][1]] = acc.astype(BF)
        return carry

    lax.fori_loop(0, shape_b[0] // 16, end_b, 0)


def by_rows(rows, width):
    h = rows // 2
    return ((pl.ds(0, h), pl.ds(0, width)), (pl.ds(h, h), pl.ds(0, width)))


def by_columns(rows, width):
    h = width // 2
    return ((pl.ds(0, rows), pl.ds(0, h)), (pl.ds(0, rows), pl.ds(h, h)))


def scratch(**kw):
    return {k: pltpu.VMEM(*v) for k, v in kw.items()}


def call(body, name, ident, ins, outs, work, sems, near):
    names = list(ins) + list(outs) + list(work)

    def run_body(*refs):
        body(SimpleNamespace(**dict(zip(names, refs[:-3]))), Copies(*refs[-3:]))

    results = pl.pallas_call(
        run_body,
        name=name,
        out_shape=[jax.ShapeDtypeStruct(*v[:2]) for v in outs.values()],
        in_specs=[v[1] for v in ins.values()],
        out_specs=[v[2] for v in outs.values()],
        scratch_shapes=list(work.values())
        + [
            pltpu.SemaphoreType.DMA((sems,)),
            pltpu.SemaphoreType.DMA((sems,)),
            pltpu.SemaphoreType.DMA((near,)),
        ],
        compiler_params=pltpu.CompilerParams(
            collective_id=ident, has_side_effects=True, vmem_limit_bytes=60 << 20
        ),
    )(*[v[0] for v in ins.values()])
    return SimpleNamespace(**dict(zip(outs, results)))


def drain(*chains):
    for chain in chains:
        for _ in chain:
            pass


NN = ((1,), (0,))
NT = ((1,), (1,))
TN = ((0,), (0,))


def dot(a, b, dims):
    return lax.dot_general(a, b, (dims, ((), ())), preferred_element_type=F32)


def gather_body(R, cp):
    g = place()[1]
    shuffle = Shuffle(True)
    greet(rings() + [in_group(*st) for st in GROUP], shuffle.greeting)
    me = (ax("xlo"), ax("xhi"), ax("z"))
    third = R.w_in.shape[1] // 8
    arrive = []
    for j, w in enumerate((R.w_in, R.w_f, R.w_og)):
        arrive.append(
            to_group(
                cp,
                lambda k, w=w: w.at[:, pl.ds(pl.multiple_of(k * third, 128), third)],
                lambda k, j=j: R.b3.at[me + (rows_of(k), pl.ds(j * third, third))],
            )
        )
    q = shuffle.to[0]
    at = (lax.div(q, 8), lax.rem(lax.div(q, 4), 2), lax.rem(q, 4))
    moved = [shuffle.start(cp, R.w_o, R.bo.at[at]), shuffle.start(cp, R.dn, R.bdn.at[at])]
    arrive_gu = to_group(cp, lambda k: R.gu.at[k], lambda k: R.block_gu.at[rows_of(k), :])

    def norm(i, carry):
        r = rows_of(i)
        x = R.tok[r, :].astype(F32)
        s = lax.rsqrt(jnp.mean(x * x, axis=-1, keepdims=True) + EPS)
        R.first[r, :] = (x * s * R.gain[...]).astype(BF)
        return carry

    lax.fori_loop(0, R.tok.shape[0] // 16, norm, 0)
    own = cp.local(R.first, R.fi.at[block_of(g)])
    chain = GroupGather(cp, R.first, R.fi)
    for pair in arrive:
        settle(*pair)
    b3 = plane_gather(cp, R.b3, by_rows(*R.b3.shape[3:]))
    next(b3)
    for pair in moved:
        shuffle.wait(pair)
    others = [
        plane_gather(cp, R.bo, by_columns(*R.bo.shape[3:])),
        plane_gather(cp, R.bdn, by_columns(*R.bdn.shape[3:])),
    ]
    run([b3] + others, (1, 2, 0, 1, 2, 0, 1))
    chain.rest()
    own.wait()
    settle(*arrive_gu)
    cp.finish()


def silu_slope(v, s):
    return s * (1.0 + v * (1.0 - s))


def row_sums(x):
    ones = jnp.ones((8, x.shape[1]), F32)
    return lax.dot_general(
        ones, x, (((1,), (1,)), ((), ())), precision=HIGH, preferred_element_type=F32
    )[0:1]


def as_column(row, width):
    t = jnp.transpose(jnp.broadcast_to(row, (128, 128)))
    return jnp.concatenate([t] * (width // 128), axis=1)


def chunk_rows(s):
    return pl.ds(pl.multiple_of(s * 128, 128), 128)


def wide(ref, r):
    return jnp.concatenate([ref[j, r, :] for j in range(ref.shape[0])], axis=1)


def put(ref, r, value):
    for j in range(ref.shape[0]):
        ref[j, r, :] = value[:, 128 * j : 128 * (j + 1)]


def share(cp, src, dst, index, peers):
    copies = [cp.send(src, dst.at[index], dev) for dev in peers]
    dst[pl.ds(index, 1)] = src[...][None]
    return copies


def links_before(links, k, w):
    come = jnp.zeros((1, w), F32)
    for j in range(8):
        new = links[j, 0:1, :] * come + links[j, 1:2, :]
        come = jnp.where(j < k, new, come)
    return come


def scan_body(R, cp):
    tiles, rows = R.states.shape[:2]
    w = 128 * tiles
    steps = rows // 8
    peers_chain = [in_chain(*st) for st in CHAIN]
    peers_group = [in_group(*st) for st in GROUP]
    greet(peers_chain + peers_group + [ring("x", s) for s in (1, 3)])
    load = [cp.local(R.b3, R.w3), cp.local(R.fi, R.x)]
    load_out = cp.local(R.bo, R.wo)
    own = cp.local(R.cot, R.gf.at[block_of(place()[1])])
    bulk = plane_gather(cp, R.bgu, by_rows(*R.bgu.shape[3:]), R.block_gu)
    next(bulk)
    chain = GroupGather(cp, R.cot, R.gf)
    low = R.lb[...]
    for copy in load:
        copy.wait()

    def project(j):
        for i in range(2):
            r = pl.ds(i * rows // 2, rows // 2)
            at = pl.ds(j * w, w)
            R.proj[r, at] = dot(R.x[r, :], R.w3[:, at], NN)

    project(0)
    project(1)
    next(bulk)

    def gates(i, c):
        r = rows_of(i, 32)
        f = low + (1.0 - low) * jax.nn.sigmoid(R.proj[r, w : 2 * w])
        v = R.proj[r, 0:w]
        put(R.forget, r, f)
        put(R.states, r, v * jax.nn.sigmoid(v) * (1.0 - f))
        return c

    lax.fori_loop(0, rows // 32, gates, 0)

    def step(t, c):
        at = pl.ds(t, 8, stride=steps)
        new = []
        for j, (h, a) in enumerate(c):
            f = R.forget[j, at, :]
            h = f * h + R.states[j, at, :]
            a = a * f
            R.states[j, at, :] = h
            R.prod[j, at, :] = a
            new.append((h, a))
        return tuple(new)

    start = ((jnp.zeros((8, 128), F32), jnp.ones((8, 128), F32)),) * tiles
    ends = lax.fori_loop(0, steps, step, start, unroll=8)
    h = jnp.concatenate([e[0] for e in ends], axis=1)
    a = jnp.concatenate([e[1] for e in ends], axis=1)
    c = jnp.zeros((1, w), F32)
    q = jnp.ones((1, w), F32)
    cs, qs = [], []
    for s in range(8):
        cs.append(c)
        qs.append(q)
        c = a[s : s + 1] * c + h[s : s + 1]
        q = a[s : s + 1] * q
    R.mine[...] = jnp.concatenate([q, c, jnp.zeros((6, w), F32)], axis=0)
    k = ax("xhi") * 4 + ax("z")
    small = share(cp, R.mine, R.links, k, peers_chain)
    project(2)
    for copy in small:
        copy.wait_recv()
    come = links_before(R.links, k, w)
    R.carry[...] = jnp.broadcast_to(come, (8, w))
    R.entry[...] = jnp.concatenate(qs, axis=0) * come + jnp.concatenate(cs, axis=0)

    def finish(s, c):
        r = chunk_rows(s)
        st = wide(R.states, r) + wide(R.prod, r) * R.entry[pl.ds(s, 1), :]
        put(R.states, r, st)
        R.rowsum[pl.ds(s, 1), :] = row_sums(st * st)
        return c

    lax.fori_loop(0, 8, finish, 0)
    small = share(cp, R.rowsum, R.rows8, place()[1], peers_group)
    next(bulk)
    for copy in small:
        copy.wait_recv()
    total = R.rows8[0]
    for j in range(1, 8):
        total = total + R.rows8[j]
    R.tot[...] = lax.rsqrt(total / (8.0 * w) + EPS)

    def gate(s, c):
        r = chunk_rows(s)
        v = R.proj[r, 2 * w : 3 * w]
        n = wide(R.states, r) * as_column(R.tot[pl.ds(s, 1), :], w)
        R.gated[r, :] = (n * R.gain[...] * (v * jax.nn.sigmoid(v))).astype(BF)
        return c

    lax.fori_loop(0, 8, gate, 0)
    load_out.wait()

    def out(i, c):
        at = rows_of(i, 512)
        R.part[:, at] = dot(R.gated[...], R.wo[:, at], NN).astype(BF)
        return c

    lax.fori_loop(0, R.part.shape[1] // 512, out, 0)
    chain.rest()
    own.wait()
    drain(bulk)
    cp.finish()


def feed_body(R, cp):
    y, c = ax("y"), ax("core")
    g = place()[1]
    unit, width = R.wdn.shape
    greet(ys() + rings())
    load = [cp.local(R.bgu, R.wgu), cp.local(R.gf, R.g), cp.local(R.bdn, R.wdn)]
    mixer = sum_of(cp, R.part, R.ps, R.near, R.far)
    next(mixer)
    next(mixer)
    terms = next(mixer)

    def norm(i, carry):
        r = rows_of(i)
        x = R.tok[r, :].astype(F32) + terms(i)
        R.mid[r, :] = x
        s = lax.rsqrt(jnp.mean(x * x, axis=-1, keepdims=True) + EPS)
        R.si[rows_of(g * 8 + i), :] = (x * s * R.gain[...]).astype(BF)
        return carry

    lax.fori_loop(0, 8, norm, 0)
    gather = GroupGather(cp, R.si.at[block_of(g)], R.si)
    second = GroupSum(cp, R.near, R.far)
    for copy in load:
        copy.wait()
    order = (0, 1, 3, 2)
    stores = []

    def forward(yy):
        r = rows_of(yy, 256)

        def tile(j, carry):
            at = rows_of(j, 256)
            up = pl.ds(pl.multiple_of(unit + j * 256, 256), 256)
            x = R.si[r, :]
            v = dot(x, R.wgu[:, at], NN)
            u = dot(x, R.wgu[:, up], NN)
            gh = dot(R.g[r, :], R.wdn[at, :], NT)
            sig = jax.nn.sigmoid(v)
            act = v * sig
            R.hid[r, at] = (act * u).astype(BF)
            R.ggu[r, at] = (gh * u * silu_slope(v, sig)).astype(BF)
            R.ggu[r, up] = (gh * act).astype(BF)
            return carry

        lax.fori_loop(0, unit // 256, tile, 0)

    def backward(yy):
        r = rows_of(yy, 256)

        def tile(j, carry):
            at = rows_of(j, 512)
            R.ps[r, at] = dot(R.ggu[r, :], R.wgu[at, :], NT).astype(BF)
            return carry

        lax.fori_loop(0, width // 512, tile, 0)

    def result(yy, slot):
        r = rows_of(yy, 256)

        def tile(j, carry):
            at = rows_of(j, 512)
            R.pr[slot, :, at] = dot(R.hid[r, :], R.wdn[:, at], NN).astype(BF)
            return carry

        lax.fori_loop(0, width // 512, tile, 0)
        stores.append(cp.local(R.pr.at[slot], R.part_r.at[r]))

    for i, s in enumerate(order):
        yy = lax.rem(y + 4 - s, 4)
        gather.ready(s)
        forward(yy)
        if i < 3:
            gather.forward(order[i + 1])
        if i > 1:
            back = (4 - order[i - 1]) % 4
            second.add(back, R.ps, 128 * (second.chip(back) + c))
        backward(yy)
        second.give((4 - s) % 4, R.ps.at[block_of(2 * yy + 1 - c)])
        if i > 1:
            stores[i - 2].wait()
        result(yy, i % 2)
    second.add(2, R.ps, 128 * (second.chip(2) + c))

    def grad_down(j, carry):
        at = rows_of(j, 512)
        for i in range(2):
            h = unit // 2
            v = dot(R.hid[:, h * i : h * (i + 1)], R.g[:, at], TN)
            R.ddn[i, :, :, :, at] = v.astype(BF).reshape(R.ddn.shape[1:4] + (512,))
        return carry

    lax.fori_loop(0, width // 512, grad_down, 0)
    planes = [plane_sum(cp, R.ddn, by_columns(*R.ddn.shape[3:]), *plane_refs(R, "a"), R.block_ddn)]
    next(planes[0])

    def grad_gate(i, carry):
        at = rows_of(i, 256)
        v = dot(R.si[:, at], R.ggu[:, 0:unit], TN).astype(BF)
        to = (lax.div(i, 4), lax.rem(lax.div(i, 2), 2), pl.ds(2 * lax.rem(i, 2), 2))
        R.dgate[to] = v.reshape(2, 128, unit)
        return carry

    lax.fori_loop(0, width // 256, grad_gate, 0)
    planes.append(plane_sum(cp, R.dgate, by_rows(*R.dgate.shape[3:]), *plane_refs(R, "b"), R.block_dgate))
    next(planes[1])
    terms = second.total(R.ps, 128 * g)
    R.sums[...] = jnp.zeros_like(R.sums)

    def back(i, carry):
        r = rows_of(i)
        x = R.mid[r, :]
        s = lax.rsqrt(jnp.mean(x * x, axis=-1, keepdims=True) + EPS)
        n = x * s
        dy = terms(i)
        R.sums[0:1, :] = R.sums[0:1, :] + jnp.sum(dy * n, axis=0, keepdims=True)
        dy = dy * R.gain[...]
        v = R.cot[r, :].astype(F32) + s * (dy - n * jnp.mean(dy * n, axis=-1, keepdims=True))
        R.mixed[r, :] = v
        R.block[r, :] = v.astype(BF)
        return carry

    lax.fori_loop(0, 8, back, 0)
    own = cp.local(R.block, R.gb.at[block_of(g)])
    branch = GroupGather(cp, R.block, R.gb)
    ups = []
    for copy in stores[2:]:
        copy.wait()

    def grad_up(i):
        at = pl.ds(i * 256, 256)
        v = dot(R.si[:, at], R.ggu[:, unit : 2 * unit], TN).astype(BF)
        if i > 1:
            ups[i - 2].wait()
        R.pu[i % 2] = v
        ups.append(cp.local(R.pu.at[i % 2], R.dup.at[at]))

    for i in range(width // 256):
        grad_up(i)
    for copy in ups[-2:]:
        copy.wait()
    next(planes[0])
    branch.forward(1)
    branch.forward(3)
    next(planes[1])
    branch.rest()
    own.wait()
    drain(*planes)
    cp.finish()


def plane_refs(R, key):
    return [getattr(R, "plane_" + key + str(i)) for i in range(6)]


def plane_work(key, halves):
    return {"plane_" + key + str(i): v for i, v in enumerate(plane_sum_scratch(halves))}


def back_body(R, cp):
    c = ax("core")
    p, g = place()
    tiles, rows = R.states.shape[:2]
    w = 128 * tiles
    steps = rows // 8
    width = R.tok.shape[1]
    shuffle = Shuffle(False)
    peers_chain = [in_chain(*st) for st in CHAIN]
    peers_group = [in_group(*st) for st in GROUP]
    peers_plane = [in_plane(*st) for st in PLANE]
    greet(peers_plane + peers_group, shuffle.greeting)
    load = [cp.local(R.gb, R.gbv), cp.local(R.bo, R.wo)]
    load_last = [cp.local(R.b3, R.w3), cp.local(R.fi, R.x)]
    res = sum_of(cp, R.part_r, R.pr, R.pr_near, R.pr_far)
    next(res)
    up = plane_sum(cp, R.dup, by_rows(*R.dup.shape[3:]), *plane_refs(R, "a"), R.block_dup)
    next(up)
    low = R.lb[...]
    R.sums[...] = jnp.zeros_like(R.sums)
    for copy in load:
        copy.wait()
    for i in range(2):
        r = pl.ds(i * rows // 2, rows // 2)
        R.gg[r, :] = dot(R.gbv[r, :], R.wo[...], NT)

    def through(s, carry):
        r = chunk_rows(s)
        v = R.proj[r, 2 * w : 3 * w]
        sig = jax.nn.sigmoid(v)
        n = wide(R.states, r) * as_column(R.tot[pl.ds(s, 1), :], w)
        dy = R.gg[r, :]
        R.sums[0:1, :] = R.sums[0:1, :] + jnp.sum(dy * n * (v * sig), axis=0, keepdims=True)
        R.grads[r, 2 * w : 3 * w] = (dy * n * R.gain[...] * silu_slope(v, sig)).astype(BF)
        dy = dy * R.gain[...] * (v * sig)
        put(R.gs, r, dy)
        R.rowsum[pl.ds(s, 1), :] = row_sums(dy * n)
        return carry

    lax.fori_loop(0, 8, through, 0)
    small = share(cp, R.rowsum, R.rows8, g, peers_group)
    def grad_out(j, carry):
        at = rows_of(j, 512)
        v = dot(R.gated[...], R.gbv[:, at], TN).astype(BF)
        R.do[:, :, :, :, at] = v.reshape(R.do.shape[:4] + (512,))
        return carry

    lax.fori_loop(0, width // 512, grad_out, 0)
    outs = plane_sum(cp, R.do, by_columns(*R.do.shape[3:]), *plane_refs(R, "b"), R.oo)
    next(outs)
    for copy in small:
        copy.wait_recv()
    total = R.rows8[0]
    for j in range(1, 8):
        total = total + R.rows8[j]
    cp.sent(small)
    R.rowsum[...] = total / (8.0 * w)

    def norm(s, carry):
        r = chunk_rows(s)
        t = as_column(R.tot[pl.ds(s, 1), :], w)
        m = as_column(R.rowsum[pl.ds(s, 1), :], w)
        put(R.gs, r, t * (wide(R.gs, r) - wide(R.states, r) * t * m))
        return carry

    lax.fori_loop(0, 8, norm, 0)

    def step(i, carry):
        at = pl.ds(steps - 1 - i, 8, stride=steps)
        new = []
        for j, (h, a) in enumerate(carry):
            f = R.forget[j, at, :]
            v = R.gs[j, at, :] + h
            R.gs[j, at, :] = v
            R.prod[j, at, :] = a
            new.append((f * v, a * f))
        return tuple(new)

    start = ((jnp.zeros((8, 128), F32), jnp.ones((8, 128), F32)),) * tiles
    ends = lax.fori_loop(0, steps, step, start, unroll=8)
    h = jnp.concatenate([e[0] for e in ends], axis=1)
    a = jnp.concatenate([e[1] for e in ends], axis=1)
    e = jnp.zeros((1, w), F32)
    q = jnp.ones((1, w), F32)
    cs, qs = [None] * 8, [None] * 8
    for s in range(7, -1, -1):
        cs[s] = e
        qs[s] = q
        e = a[s : s + 1] * e + h[s : s + 1]
        q = a[s : s + 1] * q
    R.mine[...] = jnp.broadcast_to(e, (8, w))
    k = ax("xhi") * 4 + ax("z")
    small = share(cp, R.mine, R.chain, k, peers_chain)
    next(res)
    for copy in small:
        copy.wait_recv()
    come = jnp.zeros((1, w), F32)
    for j in range(7, -1, -1):
        new = R.links[j, 0:1, :] * come + R.chain[j, 0:1, :]
        come = jnp.where(j > k, new, come)
    R.entry[...] = jnp.concatenate(qs, axis=0) * come + jnp.concatenate(cs, axis=0)

    def last(s, carry):
        r = chunk_rows(s)
        v = wide(R.gs, r) + wide(R.prod, r) * R.entry[pl.ds(s, 1), :]
        st = wide(R.states, r)
        above = pl.ds(jnp.maximum(s * 128 - 1, 0), 1)
        before = jnp.where(s == 0, R.carry[0:1, :], wide(R.states, above))
        top = lax.broadcasted_iota(jnp.int32, (128, w), 0) == 0
        prev = jnp.where(top, before, pltpu.roll(st, 1, 0))
        x = R.proj[r, 0:w]
        sx = jax.nn.sigmoid(x)
        f = wide(R.forget, r)
        sf = jax.nn.sigmoid(R.proj[r, w : 2 * w])
        gf = v * (prev - x * sx)
        R.grads[r, 0:w] = (v * (1.0 - f) * silu_slope(x, sx)).astype(BF)
        R.grads[r, w : 2 * w] = (gf * (1.0 - low) * sf * (1.0 - sf)).astype(BF)
        R.sums[1:2, :] = R.sums[1:2, :] + jnp.sum(gf * (1.0 - sf), axis=0, keepdims=True)
        return carry

    lax.fori_loop(0, 8, last, 0)
    for copy in load_last:
        copy.wait()
    first = GroupSum(cp, R.near, R.far)
    order = (2, 1, 3, 0)
    for i, s in enumerate(order):
        chip = first.chip(s)
        r = pl.ds(pl.multiple_of(chip * 128, 256), 256)

        def tile(j, carry, r=r):
            at = rows_of(j, 512)
            R.fp[r, at] = dot(R.grads[r, :], R.w3[at, :], NT).astype(BF)
            return carry

        lax.fori_loop(0, width // 512, tile, 0)
        first.give(s, R.fp.at[block_of(chip + 1 - c)])
        if i > 0:
            back = order[i - 1]
            first.add(back, R.fp, 128 * (first.chip(back) + c))

    def grad_three(i, carry):
        at = rows_of(i, 256)
        v = dot(R.x[:, at], R.grads[...], TN).astype(BF)
        to = (lax.div(i, 4), lax.rem(lax.div(i, 2), 2), pl.ds(2 * lax.rem(i, 2), 2))
        R.d3[to] = v.reshape(2, 128, 3 * w)
        return carry

    lax.fori_loop(0, width // 256, grad_three, 0)
    three = plane_sum(cp, R.d3, by_rows(*R.d3.shape[3:]), *plane_refs(R, "c"), R.o3)
    next(three)
    next(up)
    next(outs)
    drain(up, outs)
    arrive = [
        to_group(cp, lambda k: R.block_dgate.at[rows_of(k), :], lambda k: R.rgate.at[k]),
        to_group(cp, lambda k: R.block_dup.at[rows_of(k), :], lambda k: R.rup.at[k]),
    ]
    moved = [shuffle.start(cp, R.block_ddn, R.rdn), shuffle.start(cp, R.oo, R.ro)]
    terms = next(res)

    def finish_result(i, carry):
        r = rows_of(i)
        R.result[r, :] = (R.mid[r, :] + terms(i)).astype(BF)
        return carry

    lax.fori_loop(0, 8, finish_result, 0)
    terms_first = first.total(R.fp, 128 * g)
    R.va[...] = jnp.zeros_like(R.va)

    def back(i, carry):
        r = rows_of(i)
        x = R.tok[r, :].astype(F32)
        s = lax.rsqrt(jnp.mean(x * x, axis=-1, keepdims=True) + EPS)
        n = x * s
        dy = terms_first(i)
        R.va[0:1, :] = R.va[0:1, :] + jnp.sum(dy * n, axis=0, keepdims=True)
        dy = dy * R.attn_gain[...]
        R.gtok[r, :] = R.mixed[r, :] + s * (dy - n * jnp.mean(dy * n, axis=-1, keepdims=True))
        return carry

    lax.fori_loop(0, 8, back, 0)
    R.va[1:2, :] = R.ffn_sums[0:1, :]
    small = []
    for st in GROUP:
        dev = in_group(*st)
        k = dev["y"] * 2 + dev["core"]
        small.append(cp.send(R.va.at[:, rows_of(k, w)], R.ga.at[g], dev))
    R.ga[pl.ds(g, 1)] = R.va[:, rows_of(g, w)][None]
    next(three)
    for copy in small:
        copy.wait_recv()
    acc = R.ga[0]
    for j in range(1, 8):
        acc = acc + R.ga[j]
    R.ta[...] = acc
    R.ta[2:4, :] = R.sums[0:2, :]
    for copy in share(cp, R.ta, R.gather, p, peers_plane):
        copy.wait_recv()
    acc = R.gather[0]
    for j in range(1, 16):
        acc = acc + R.gather[j]
    R.tb[...] = acc
    small = share(cp, R.tb, R.totals, g, peers_group)
    drain(three)
    arrive.append(to_group(cp, lambda k: R.o3.at[rows_of(k), :], lambda k: R.r3.at[k]))
    for copy in small:
        copy.wait_recv()
    for pair in arrive:
        settle(*pair)
    for pair in moved:
        shuffle.wait(pair)
    cp.finish()


def bound_value(bound_table, layer_idx):
    probabilities = jax.nn.softmax(bound_table, axis=0)
    levels = jnp.arange(bound_table.shape[0], dtype=jnp.int32)[:, None]
    keep = jnp.where((levels >= 1) & (levels <= layer_idx[0]), 1.0, 0.0).astype(F32)
    return jnp.sum(probabilities * keep, axis=0)


def on_device(
    tokens, cotangent, attn_gain, w_input, w_forget, w_outgate, w_out, norm_gain, mlp_gain, w_gate, w_up, w_down, bound_table, layer_idx
):
    n, width = tokens.shape
    rows = w_input.shape[0]
    hidden_width = w_gate.shape[1]
    down = w_down.shape[0]
    padded = -(-down // 16) * 16
    unit = 16 * padded
    w = width // 8

    def spread(m):
        m = jnp.pad(m.reshape(rows, 128, down), ((0, 0), (0, 0), (0, padded - down)))
        return m.reshape(rows, 8, unit).transpose(1, 0, 2)

    gu = jnp.concatenate([spread(w_gate), spread(w_up)], axis=2)
    dn = jnp.pad(w_down, ((0, padded - down), (0, 0)))
    gains = attn_gain[None, :]
    full = (8 * n, width)
    block = (n, width)
    gate_blocks = (2, 2, 4, 8 * rows, unit)
    A = call(
        gather_body,
        "gather",
        0,
        dict(
            tok=(tokens, VMEM),
            gain=(gains, VMEM),
            w_in=(w_input, ANY),
            w_f=(w_forget, ANY),
            w_og=(w_outgate, ANY),
            w_o=(w_out, ANY),
            dn=(dn, ANY),
            gu=(gu, ANY),
        ),
        dict(
            b3=((2, 2, 4, 8 * rows, 3 * w), BF, ANY),
            bo=((2, 2, 4, rows, width), BF, ANY),
            bdn=((2, 2, 4, padded, width), BF, ANY),
            fi=(full, BF, ANY),
            block_gu=((8 * rows, 2 * unit), BF, ANY),
        ),
        scratch(first=(block, BF)),
        96,
        10,
    )
    big3 = A.b3.reshape(width, 3 * w)
    big_out = A.bo.reshape(w, width)
    group = ax("y") * 2 + ax("core")
    lower = bound_value(lax.dynamic_slice_in_dim(bound_table, group * w, w, 1), layer_idx)[None, :]
    mixer_gain = lax.dynamic_slice_in_dim(norm_gain, group * w, w, 0)[None, :]
    column = (w // 128, 8 * n, 128)
    B = call(
        scan_body,
        "scan",
        1,
        dict(
            lb=(lower, VMEM),
            gain=(mixer_gain, VMEM),
            b3=(big3, ANY),
            bo=(big_out, ANY),
            fi=(A.fi, ANY),
            block_gu=(A.block_gu, ANY),
            cot=(cotangent, ANY),
        ),
        dict(
            gated=((8 * n, w), BF, VMEM),
            states=(column, F32, VMEM),
            forget=(column, F32, VMEM),
            proj=((8 * n, 3 * w), F32, VMEM),
            tot=((8, n), F32, VMEM),
            links=((8, 8, w), F32, VMEM),
            carry=((8, w), F32, VMEM),
            part=(full, BF, VMEM),
            gf=(full, BF, ANY),
            bgu=((2, 2, 4, 8 * rows, 2 * unit), BF, ANY),
        ),
        scratch(
            w3=((width, 3 * w), BF),
            x=(full, BF),
            wo=((w, width), BF),
            prod=(column, F32),
            entry=((8, w), F32),
            mine=((8, w), F32),
            rowsum=((8, n), F32),
            rows8=((8, 8, n), F32),
        ),
        48,
        8,
    )
    gains_two = mlp_gain[None, :]
    C = call(
        feed_body,
        "feed",
        2,
        dict(
            tok=(tokens, VMEM),
            cot=(cotangent, VMEM),
            gain=(gains_two, VMEM),
            part=(B.part, ANY),
            bgu=(B.bgu.reshape(width, 2 * unit), ANY),
            bdn=(A.bdn.reshape(unit, width), ANY),
            gf=(B.gf, ANY),
        ),
        dict(
            mid=(block, F32, VMEM),
            mixed=(block, F32, VMEM),
            gb=(full, BF, ANY),
            part_r=(full, BF, ANY),
            sums=((8, width), F32, VMEM),
            block_ddn=((padded, width), BF, VMEM),
            block_dgate=((8 * rows, unit), BF, VMEM),
            dup=((width, unit), BF, ANY),
        ),
        scratch(
            wgu=((width, 2 * unit), BF),
            wdn=((unit, width), BF),
            g=(full, BF),
            si=(full, BF),
            hid=((8 * n, unit), BF),
            ggu=((8 * n, 2 * unit), BF),
            ps=(full, BF),
            pr=((2, 2 * n, width), BF),
            near=((4,) + block, BF),
            far=((3,) + block, BF),
            block=(block, BF),
            ddn=((2, 2, 4, padded, width), BF),
            dgate=(gate_blocks, BF),
            pu=((2, 256, unit), BF),
        )
        | plane_work("a", by_columns(padded, width))
        | plane_work("b", by_rows(8 * rows, unit)),
        56,
        30,
    )
    D = call(
        back_body,
        "back",
        3,
        dict(
            tok=(tokens, VMEM),
            mid=(C.mid, VMEM),
            mixed=(C.mixed, VMEM),
            attn_gain=(gains, VMEM),
            lb=(lower, VMEM),
            gain=(mixer_gain, VMEM),
            ffn_sums=(C.sums, VMEM),
            states=(B.states, VMEM),
            forget=(B.forget, VMEM),
            proj=(B.proj, VMEM),
            gated=(B.gated, VMEM),
            tot=(B.tot, VMEM),
            links=(B.links, VMEM),
            carry=(B.carry, VMEM),
            b3=(big3, ANY),
            bo=(big_out, ANY),
            fi=(A.fi, ANY),
            gb=(C.gb, ANY),
            part_r=(C.part_r, ANY),
            dup=(C.dup.reshape(gate_blocks), ANY),
            block_dgate=(C.block_dgate, ANY),
            block_ddn=(C.block_ddn, ANY),
        ),
        dict(
            result=(block, BF, VMEM),
            gtok=(block, F32, VMEM),
            rgate=((8, rows, unit), BF, VMEM),
            rup=((8, rows, unit), BF, VMEM),
            r3=((8, rows, 3 * w), BF, VMEM),
            ro=((rows, width), BF, VMEM),
            rdn=((padded, width), BF, VMEM),
            totals=((8, 8, w), F32, VMEM),
        ),
        scratch(
            gbv=(full, BF),
            wo=((w, width), BF),
            w3=((width, 3 * w), BF),
            x=(full, BF),
            gg=((8 * n, w), F32),
            gs=(column, F32),
            prod=(column, F32),
            grads=((8 * n, 3 * w), BF),
            sums=((8, w), F32),
            entry=((8, w), F32),
            mine=((8, w), F32),
            rowsum=((8, n), F32),
            rows8=((8, 8, n), F32),
            chain=((8, 8, w), F32),
            pr=((4 * n, width), BF),
            pr_near=((4,) + block, BF),
            pr_far=((3,) + block, BF),
            fp=(full, BF),
            near=((4,) + block, BF),
            far=((3,) + block, BF),
            do=((2, 2, 4, rows, width), BF),
            d3=((2, 2, 4, 8 * rows, 3 * w), BF),
            block_dup=((8 * rows, unit), BF),
            o3=((8 * rows, 3 * w), BF),
            oo=((rows, width), BF),
            va=((8, width), F32),
            ga=((8, 8, w), F32),
            ta=((8, w), F32),
            gather=((16, 8, w), F32),
            tb=((8, w), F32),
        )
        | plane_work("a", by_rows(8 * rows, unit))
        | plane_work("b", by_columns(rows, width))
        | plane_work("c", by_rows(8 * rows, 3 * w)),
        150,
        30,
    )

    def join(m):
        m = m.transpose(1, 0, 2)
        return m.reshape(rows, 8 * m.shape[2]).astype(F32)

    def unspread(m):
        m = m.transpose(1, 0, 2).reshape(rows, 128, padded)[:, :, :down]
        return m.reshape(rows, hidden_width).astype(F32)

    sums = D.totals.transpose(1, 0, 2).reshape(8, width)
    pullback = jax.vjp(lambda table: bound_value(table, layer_idx), bound_table)[1]
    return (
        D.result,
        D.gtok,
        sums[0],
        join(D.r3[:, :, :w]),
        join(D.r3[:, :, w : 2 * w]),
        join(D.r3[:, :, 2 * w :]),
        D.ro.astype(F32),
        sums[2],
        sums[1],
        unspread(D.rgate),
        unspread(D.rup),
        D.rdn[:down].astype(F32),
        pullback(sums[3])[0],
    )


def solution(mesh):
    split = Mesh(mesh.devices.reshape(2, 2, 4, 4, 2), AXES)
    cut = P(AXES, None)
    return jax.shard_map(
        on_device,
        mesh=split,
        in_specs=(cut, cut, P(), cut, cut, cut, cut, P(), P(), cut, cut, cut, P(), P()),
        out_specs=(cut, cut, P(), cut, cut, cut, cut, P(), P(), cut, cut, cut, P()),
        check_vma=False,
    )
```

time: 431 us -> 419 us (0.972); the launches traced: 423 us -> 419 us
  matrix products: 74.2 us -> 0 us
  Pallas kernels: 323 us -> 392 us
    dot_general x12 -> x0, matrix products: 74.2 us -> none  [dot(): return lax.dot_general(a, b, (dims, ((), ())), preferred_element_type=F32)]
    pallas_call x6 -> x4, Pallas kernels: 323 us -> 392 us  [call(): pl.pallas_call(run_body, name=name, out_shape=[jax.ShapeDtypeStruct(*v[:2...]
where the time goes in v3:
time: 419 us
  Pallas kernels  392 us (94%)
  local copies, waits for them, and re-layouts  18.5 us (4%)
  other arithmetic  7.22 us (2%)
    pallas_call x4, Pallas kernels, call(): pl.pallas_call(run_body, name=name, out_shape=[jax.ShapeDtypeStruct(*v[:2...  392 us

profile of v3, /device:TPU:1, one launch (start us, length us, event | category | flops | bytes accessed | tf_op | source)
XLA Modules:
  0.0 419.0 jit_solution(168646963821454936)
XLA Ops:
  0.7 0.8 dynamic-slice_reduce_fusion
  1.5 0.8 fusion.5
  2.9 1.4 multiply_reduce_fusion
  4.3 1.3 dynamic_slice.7
  5.6 2.4 reshape.110
  8.0 0.1 pad.12
  8.2 0.5 reshape.111
  8.6 2.4 reshape.112
  11.0 0.1 pad.13
  11.2 0.5 reshape.113
  11.7 0.8 pad_maximum_fusion.refs_7_
  12.5 0.7 pad.11.refs_6_
  13.2 74.7 %gather.1 = (bf16[2,2,4,128,768]{4,3,2,1,0:T(8,128)(2,1)}, bf16[2,2,4,16,2048]{4,3,2,1,0:T(8,128)(2,1)}, bf16[2,2,4,48,2048]{4,3,2,1,0:T(8,128)(2,1)}, bf16[1024,2048]{1,0:T(8,128)(2,1)}, bf16[128,1536]{1,0:T(8,128)(2,1)}) custom-call(bf16[128,2048]{1,0:T(8,128)(2,1)} %refs_0_.5, f32[1,2048]{1,0:T(1,128)} %bitcast.48, bf16[16,2048]{1,0:T(8,128)(2,1)} %refs_2_.1, ...), custom_call_target="tpu_custom_call" | custom-call | tf_op jit(solution)/shard_map/gather/pallas_call | solution.py:438
  87.9 71.4 %scan.1 = (bf16[1024,256]{1,0:T(8,128)(2,1)}, f32[2,1024,128]{2,1,0:T(8,128)}, f32[2,1024,128]{2,1,0:T(8,128)}, f32[1024,768]{1,0:T(8,128)}, f32[8,128]{1,0:T(8,...) custom-call(f32[1,256]{1,0:T(1,128)} %bitcast.51, ...), custom_call_target="tpu_custom_call" | custom-call | tf_op jit(solution)/shard_map/scan/pallas_call | solution.py:438
  159.4 137.7 %feed.1 = (f32[128,2048]{1,0:T(8,128)}, f32[128,2048]{1,0:T(8,128)}, bf16[1024,2048]{1,0:T(8,128)(2,1)}, bf16[1024,2048]{1,0:T(8,128)(2,1)}, f32[8,2048]{1,0:T(8...) custom-call(bf16[128,2048]{1,0:T(8,128)(2,1)} %refs_0_.5, ...), custom_call_target="tpu_custom_call" | custom-call | tf_op jit(solution)/shard_map/feed/pallas_call | solution.py:438
  297.1 107.9 %back.1 = (bf16[128,2048]{1,0:T(8,128)(2,1)}, f32[128,2048]{1,0:T(8,128)}, bf16[8,16,768]{2,1,0:T(8,128)(2,1)}, bf16[8,16,768]{2,1,0:T(8,128)(2,1)}, bf16[8,16,7...) custom-call(bf16[128,2048]{1,0:T(8,128)(2,1)} %refs_0_.5, ...), custom_call_target="tpu_custom_call" | custom-call | tf_op jit(solution)/shard_map/back/pallas_call | solution.py:438
  405.0 1.6 fusion.6
  406.7 0.1 fusion.3
  406.8 0.8 fusion.1
  407.6 1.0 copy.32
  408.6 0.6 reshape.119
  409.3 0.1 slice_convert_fusion.1
  409.4 1.3 reshape.124
  410.8 0.6 reshape.120
  411.6 1.3 reshape.125
  412.9 0.7 copy.34
  413.6 0.7 copy.35
  414.3 0.7 copy.36
  414.9 0.8 slice_convert_fusion.2
  415.7 1.5 convert_element_type.59
  417.2 0.8 copy.42
  418.0 1.0 copy.43
  (23 shorter events, 0.4 us)
Async XLA Ops:
  0.6 11.8 %copy-start.3 = (bf16[44,2048]{1,0:T(8,128)(2,1)S(1)}, bf16[44,2048]{1,0:T(8,128)(2,1)}, u32[]{:S(2)}) copy-start(bf16[44,2048]{1,0:T(8,128)(2,1)} %param.25) | copy-start | bytes 540676
  297.0 109.6 %copy-start = (f32[24,2048]{1,0:T(8,128)S(1)}, f32[24,2048]{1,0:T(8,128)}, u32[]{:S(2)}) copy-start(f32[24,2048]{1,0:T(8,128)} %param.26) | copy-start | bytes 589828
  405.0 5.8 %copy-start.4 = (bf16[8,16,768]{2,1,0:T(8,128)(2,1)S(1)}, bf16[8,16,768]{2,1,0:T(8,128)(2,1)}, u32[]{:S(2)}) copy-start(bf16[8,16,768]{2,1,0:T(8,128)(2,1)} %get-tuple-element.73) | copy-start | bytes 589828
  407.6 5.3 %copy-start.6 = (bf16[8,16,768]{2,1,0:T(8,128)(2,1)S(1)}, bf16[8,16,768]{2,1,0:T(8,128)(2,1)}, u32[]{:S(2)}) copy-start(bf16[8,16,768]{2,1,0:T(8,128)(2,1)} %get-tuple-element.70) | copy-start | bytes 589828
  409.3 5.7 %copy-start.5 = (bf16[48,2048]{1,0:T(8,128)(2,1)S(1)}, bf16[48,2048]{1,0:T(8,128)(2,1)}, u32[]{:S(2)}) copy-start(bf16[48,2048]{1,0:T(8,128)(2,1)} %get-tuple-element.74) | copy-start | bytes 589828
  409.4 7.8 %copy-start.2 = (bf16[128,2048]{1,0:T(8,128)(2,1)S(1)}, bf16[128,2048]{1,0:T(8,128)(2,1)}, u32[]{:S(2)}) copy-start(bf16[128,2048]{1,0:T(8,128)(2,1)} %get-tuple-element.97) | copy-start | bytes 1572868
  409.4 8.6 %copy-start.1 = (f32[128,2048]{1,0:T(8,128)S(1)}, f32[128,2048]{1,0:T(8,128)}, u32[]{:S(2)}) copy-start(f32[128,2048]{1,0:T(8,128)} %get-tuple-element.98) | copy-start | bytes 3145732

commit v4 on v3

--- a/solution.py
+++ b/solution.py
@@ -72,6 +72,7 @@
     def remote(self, src, dst, dev):
         i = self.count
         self.count += 1
+        assert i < self.sems[0].shape[0]
         return pltpu.make_async_remote_copy(
             src_ref=src,
             dst_ref=dst,
@@ -87,9 +88,14 @@
         self.open.append(copy)
         return copy
 
+    def near(self, src, dst):
+        i = self.locals
+        self.locals += 1
+        assert i < self.sems[2].shape[0]
+        return pltpu.make_async_copy(src, dst, self.sems[2].at[i])
+
     def local(self, src, dst):
-        copy = pltpu.make_async_copy(src, dst, self.sems[2].at[self.locals])
-        self.locals += 1
+        copy = self.near(src, dst)
         copy.start()
         return copy
 
@@ -152,8 +158,7 @@
 
     def start(self, cp, src, dst):
         copy = cp.remote(src, dst, self.target)
-        home = pltpu.make_async_copy(src, dst, cp.sems[2].at[cp.locals])
-        cp.locals += 1
+        home = cp.near(src, dst)
 
         @pl.when(self.to_me)
         def _():
@@ -321,6 +326,52 @@
         copy.wait_recv()
 
 
+def plane_first(cp, block, column, row, halves):
+    me = (ax("xlo"), ax("xhi"), ax("z"))
+    top, bottom = block.at[halves[0]], block.at[halves[1]]
+    home = [cp.local(top, column.at[me[2]]), cp.local(bottom, row.at[me[0], me[1]])]
+    first = []
+    for s in STEPS:
+        first.append(cp.send(top, column.at[me[2]], ring("z", s)))
+        first.append(cp.send(bottom, row.at[me[0], me[1]], ring("x", s)))
+    yield
+    for copy in first:
+        copy.wait_recv()
+    for copy in home:
+        copy.wait()
+
+
+def plane_second(cp, column, row, buf, halves):
+    me = (ax("xlo"), ax("xhi"), ax("z"))
+
+    def view(h, *at):
+        return buf.at[at + halves[h]]
+
+    here = view(0, me[0], me[1], pl.ds(0, 4))
+    across = view(1, pl.ds(0, 2), pl.ds(0, 2), me[2])
+    home = [cp.local(column, here), cp.local(row, across)]
+    wide = {}
+    for s in (1, 3):
+        wide["x", s] = cp.send(column, here, ring("x", s))
+        wide["z", s] = cp.send(row, across, ring("z", s))
+    yield
+    last = []
+    for s in (1, 3):
+        back = ring("x", 4 - s)
+        wide["x", s].wait_recv()
+        v = view(0, back["xlo"], back["xhi"], pl.ds(0 if s == 1 else 2, 2))
+        last.append(cp.send(v, v, ring("x", s)))
+        back = ring("z", 4 - s)
+        wide["z", s].wait_recv()
+        v = view(1, 0 if s == 1 else 1, pl.ds(0, 2), back["z"])
+        last.append(cp.send(v, v, ring("z", s)))
+    yield
+    for copy in last:
+        copy.wait_recv()
+    for copy in home:
+        copy.wait()
+
+
 def half_shapes(halves):
     return [tuple(d.size for d in h) for h in halves]
 
@@ -486,7 +537,7 @@
         )
     q = shuffle.to[0]
     at = (lax.div(q, 8), lax.rem(lax.div(q, 4), 2), lax.rem(q, 4))
-    moved = [shuffle.start(cp, R.w_o, R.bo.at[at]), shuffle.start(cp, R.dn, R.bdn.at[at])]
+    moved = shuffle.start(cp, R.w_o, R.bo.at[at])
     arrive_gu = to_group(cp, lambda k: R.gu.at[k], lambda k: R.block_gu.at[rows_of(k), :])
 
     def norm(i, carry):
@@ -503,16 +554,15 @@
         settle(*pair)
     b3 = plane_gather(cp, R.b3, by_rows(*R.b3.shape[3:]))
     next(b3)
-    for pair in moved:
-        shuffle.wait(pair)
-    others = [
-        plane_gather(cp, R.bo, by_columns(*R.bo.shape[3:])),
-        plane_gather(cp, R.bdn, by_columns(*R.bdn.shape[3:])),
-    ]
-    run([b3] + others, (1, 2, 0, 1, 2, 0, 1))
+    shuffle.wait(moved)
+    bo = plane_gather(cp, R.bo, by_columns(*R.bo.shape[3:]))
+    next(bo)
+    settle(*arrive_gu)
+    gu = plane_first(cp, R.block_gu, R.gu_column, R.gu_row, by_rows(*R.block_gu.shape))
+    next(gu)
+    run([b3, bo, gu], (0, 1, 0, 1, 2))
     chain.rest()
     own.wait()
-    settle(*arrive_gu)
     cp.finish()
 
 
@@ -569,7 +619,7 @@
     load = [cp.local(R.b3, R.w3), cp.local(R.fi, R.x)]
     load_out = cp.local(R.bo, R.wo)
     own = cp.local(R.cot, R.gf.at[block_of(place()[1])])
-    bulk = plane_gather(cp, R.bgu, by_rows(*R.bgu.shape[3:]), R.block_gu)
+    bulk = plane_gather(cp, R.bdn, by_columns(*R.bdn.shape[3:]), R.dn)
     next(bulk)
     chain = GroupGather(cp, R.cot, R.gf)
     low = R.lb[...]
@@ -674,10 +724,13 @@
     g = place()[1]
     unit, width = R.wdn.shape
     greet(ys() + rings())
-    load = [cp.local(R.bgu, R.wgu), cp.local(R.gf, R.g), cp.local(R.bdn, R.wdn)]
+    weights = plane_second(cp, R.gu_column, R.gu_row, R.wgu, by_rows(*R.wgu.shape[3:]))
+    next(weights)
     mixer = sum_of(cp, R.part, R.ps, R.near, R.far)
     next(mixer)
+    load = [cp.local(R.gf, R.g), cp.local(R.bdn, R.wdn)]
     next(mixer)
+    next(weights)
     terms = next(mixer)
 
     def norm(i, carry):
@@ -693,6 +746,7 @@
     second = GroupSum(cp, R.near, R.far)
     for copy in load:
         copy.wait()
+    drain(weights)
     order = (0, 1, 3, 2)
     stores = []
 
@@ -703,8 +757,8 @@
             at = rows_of(j, 256)
             up = pl.ds(pl.multiple_of(unit + j * 256, 256), 256)
             x = R.si[r, :]
-            v = dot(x, R.wgu[:, at], NN)
-            u = dot(x, R.wgu[:, up], NN)
+            v = dot(x, R.wgu[:, :, :, :, at].reshape(width, 256), NN)
+            u = dot(x, R.wgu[:, :, :, :, up].reshape(width, 256), NN)
             gh = dot(R.g[r, :], R.wdn[at, :], NT)
             sig = jax.nn.sigmoid(v)
             act = v * sig
@@ -720,7 +774,8 @@
 
         def tile(j, carry):
             at = rows_of(j, 512)
-            R.ps[r, at] = dot(R.ggu[r, :], R.wgu[at, :], NT).astype(BF)
+            w = R.wgu[lax.div(j, 2), lax.rem(j, 2)].reshape(512, 2 * unit)
+            R.ps[r, at] = dot(R.ggu[r, :], w, NT).astype(BF)
             return carry
 
         lax.fori_loop(0, width // 512, tile, 0)
@@ -847,11 +902,13 @@
     next(up)
     low = R.lb[...]
     R.sums[...] = jnp.zeros_like(R.sums)
+    gate_home = to_group(cp, lambda k: R.block_dgate.at[rows_of(k), :], lambda k: R.rgate.at[k])
     for copy in load:
         copy.wait()
     for i in range(2):
         r = pl.ds(i * rows // 2, rows // 2)
         R.gg[r, :] = dot(R.gbv[r, :], R.wo[...], NT)
+    next(res)
 
     def through(s, carry):
         r = chunk_rows(s)
@@ -920,7 +977,8 @@
     R.mine[...] = jnp.broadcast_to(e, (8, w))
     k = ax("xhi") * 4 + ax("z")
     small = share(cp, R.mine, R.chain, k, peers_chain)
-    next(res)
+    next(up)
+    next(outs)
     for copy in small:
         copy.wait_recv()
     come = jnp.zeros((1, w), F32)
@@ -950,6 +1008,8 @@
     lax.fori_loop(0, 8, last, 0)
     for copy in load_last:
         copy.wait()
+    R.va[...] = jnp.zeros_like(R.va)
+    R.va[1:2, :] = R.ffn_sums[0:1, :]
     first = GroupSum(cp, R.near, R.far)
     order = (2, 1, 3, 0)
     for i, s in enumerate(order):
@@ -958,7 +1018,11 @@
 
         def tile(j, carry, r=r):
             at = rows_of(j, 512)
-            R.fp[r, at] = dot(R.grads[r, :], R.w3[at, :], NT).astype(BF)
+            v = dot(R.grads[r, :], R.w3[at, :], NT)
+            R.va[0:1, at] = R.va[0:1, at] + jnp.sum(
+                v * (R.x[r, at].astype(F32) / R.attn_gain[:, at]), axis=0, keepdims=True
+            )
+            R.fp[r, at] = v.astype(BF)
             return carry
 
         lax.fori_loop(0, width // 512, tile, 0)
@@ -966,6 +1030,13 @@
         if i > 0:
             back = order[i - 1]
             first.add(back, R.fp, 128 * (first.chip(back) + c))
+
+    gains = []
+    for st in GROUP:
+        dev = in_group(*st)
+        k = dev["y"] * 2 + dev["core"]
+        gains.append(cp.send(R.va.at[:, rows_of(k, w)], R.ga.at[g], dev))
+    R.ga[pl.ds(g, 1)] = R.va[:, rows_of(g, w)][None]
 
     def grad_three(i, carry):
         at = rows_of(i, 256)
@@ -977,14 +1048,25 @@
     lax.fori_loop(0, width // 256, grad_three, 0)
     three = plane_sum(cp, R.d3, by_rows(*R.d3.shape[3:]), *plane_refs(R, "c"), R.o3)
     next(three)
-    next(up)
-    next(outs)
     drain(up, outs)
     arrive = [
-        to_group(cp, lambda k: R.block_dgate.at[rows_of(k), :], lambda k: R.rgate.at[k]),
+        gate_home,
         to_group(cp, lambda k: R.block_dup.at[rows_of(k), :], lambda k: R.rup.at[k]),
     ]
-    moved = [shuffle.start(cp, R.block_ddn, R.rdn), shuffle.start(cp, R.oo, R.ro)]
+    moved = shuffle.start(cp, R.oo, R.ro)
+    for copy in gains:
+        copy.wait_recv()
+    acc = R.ga[0]
+    for j in range(1, 8):
+        acc = acc + R.ga[j]
+    R.ta[...] = acc
+    R.ta[2:4, :] = R.sums[0:2, :]
+    for copy in share(cp, R.ta, R.gather, p, peers_plane):
+        copy.wait_recv()
+    acc = R.gather[0]
+    for j in range(1, 16):
+        acc = acc + R.gather[j]
+    R.tb[...] = acc
     terms = next(res)
 
     def finish_result(i, carry):
@@ -993,8 +1075,9 @@
         return carry
 
     lax.fori_loop(0, 8, finish_result, 0)
+    small = share(cp, R.tb, R.totals, g, peers_group)
+    next(three)
     terms_first = first.total(R.fp, 128 * g)
-    R.va[...] = jnp.zeros_like(R.va)
 
     def back(i, carry):
         r = rows_of(i)
@@ -1002,42 +1085,18 @@
         s = lax.rsqrt(jnp.mean(x * x, axis=-1, keepdims=True) + EPS)
         n = x * s
         dy = terms_first(i)
-        R.va[0:1, :] = R.va[0:1, :] + jnp.sum(dy * n, axis=0, keepdims=True)
         dy = dy * R.attn_gain[...]
         R.gtok[r, :] = R.mixed[r, :] + s * (dy - n * jnp.mean(dy * n, axis=-1, keepdims=True))
         return carry
 
     lax.fori_loop(0, 8, back, 0)
-    R.va[1:2, :] = R.ffn_sums[0:1, :]
-    small = []
-    for st in GROUP:
-        dev = in_group(*st)
-        k = dev["y"] * 2 + dev["core"]
-        small.append(cp.send(R.va.at[:, rows_of(k, w)], R.ga.at[g], dev))
-    R.ga[pl.ds(g, 1)] = R.va[:, rows_of(g, w)][None]
-    next(three)
-    for copy in small:
-        copy.wait_recv()
-    acc = R.ga[0]
-    for j in range(1, 8):
-        acc = acc + R.ga[j]
-    R.ta[...] = acc
-    R.ta[2:4, :] = R.sums[0:2, :]
-    for copy in share(cp, R.ta, R.gather, p, peers_plane):
-        copy.wait_recv()
-    acc = R.gather[0]
-    for j in range(1, 16):
-        acc = acc + R.gather[j]
-    R.tb[...] = acc
-    small = share(cp, R.tb, R.totals, g, peers_group)
     drain(three)
     arrive.append(to_group(cp, lambda k: R.o3.at[rows_of(k), :], lambda k: R.r3.at[k]))
     for copy in small:
         copy.wait_recv()
     for pair in arrive:
         settle(*pair)
-    for pair in moved:
-        shuffle.wait(pair)
+    shuffle.wait(moved)
     cp.finish()
 
 
@@ -1060,8 +1119,9 @@
     w = width // 8
 
     def spread(m):
-        m = jnp.pad(m.reshape(rows, 128, down), ((0, 0), (0, 0), (0, padded - down)))
-        return m.reshape(rows, 8, unit).transpose(1, 0, 2)
+        m = m.reshape(rows, 16, 8, down)
+        m = jnp.pad(m, ((0, 0), (0, 0), (0, 0), (0, padded - down)))
+        return m.transpose(2, 0, 1, 3).reshape(8, rows, unit)
 
     gu = jnp.concatenate([spread(w_gate), spread(w_up)], axis=2)
     dn = jnp.pad(w_down, ((0, padded - down), (0, 0)))
@@ -1076,21 +1136,20 @@
         dict(
             tok=(tokens, VMEM),
             gain=(gains, VMEM),
-            w_in=(w_input, ANY),
-            w_f=(w_forget, ANY),
-            w_og=(w_outgate, ANY),
-            w_o=(w_out, ANY),
-            dn=(dn, ANY),
-            gu=(gu, ANY),
+            w_in=(w_input, VMEM),
+            w_f=(w_forget, VMEM),
+            w_og=(w_outgate, VMEM),
+            w_o=(w_out, VMEM),
+            gu=(gu, VMEM),
         ),
         dict(
             b3=((2, 2, 4, 8 * rows, 3 * w), BF, ANY),
             bo=((2, 2, 4, rows, width), BF, ANY),
-            bdn=((2, 2, 4, padded, width), BF, ANY),
             fi=(full, BF, ANY),
-            block_gu=((8 * rows, 2 * unit), BF, ANY),
+            gu_column=((4, 4 * rows, 2 * unit), BF, ANY),
+            gu_row=((2, 2, 4 * rows, 2 * unit), BF, ANY),
         ),
-        scratch(first=(block, BF)),
+        scratch(first=(block, BF), block_gu=((8 * rows, 2 * unit), BF)),
         96,
         10,
     )
@@ -1110,8 +1169,8 @@
             b3=(big3, ANY),
             bo=(big_out, ANY),
             fi=(A.fi, ANY),
-            block_gu=(A.block_gu, ANY),
-            cot=(cotangent, ANY),
+            dn=(dn, VMEM),
+            cot=(cotangent, VMEM),
         ),
         dict(
             gated=((8 * n, w), BF, VMEM),
@@ -1123,7 +1182,7 @@
             carry=((8, w), F32, VMEM),
             part=(full, BF, VMEM),
             gf=(full, BF, ANY),
-            bgu=((2, 2, 4, 8 * rows, 2 * unit), BF, ANY),
+            bdn=((2, 2, 4, padded, width), BF, ANY),
         ),
         scratch(
             w3=((width, 3 * w), BF),
@@ -1148,8 +1207,9 @@
             cot=(cotangent, VMEM),
             gain=(gains_two, VMEM),
             part=(B.part, ANY),
-            bgu=(B.bgu.reshape(width, 2 * unit), ANY),
-            bdn=(A.bdn.reshape(unit, width), ANY),
+            gu_column=(A.gu_column, ANY),
+            gu_row=(A.gu_row, ANY),
+            bdn=(B.bdn.reshape(unit, width), ANY),
             gf=(B.gf, ANY),
         ),
         dict(
@@ -1163,7 +1223,7 @@
             dup=((width, unit), BF, ANY),
         ),
         scratch(
-            wgu=((width, 2 * unit), BF),
+            wgu=((2, 2, 4, 8 * rows, 2 * unit), BF),
             wdn=((unit, width), BF),
             g=(full, BF),
             si=(full, BF),
@@ -1180,7 +1240,7 @@
         )
         | plane_work("a", by_columns(padded, width))
         | plane_work("b", by_rows(8 * rows, unit)),
-        56,
+        72,
         30,
     )
     D = call(
@@ -1209,7 +1269,6 @@
             part_r=(C.part_r, ANY),
             dup=(C.dup.reshape(gate_blocks), ANY),
             block_dgate=(C.block_dgate, ANY),
-            block_ddn=(C.block_ddn, ANY),
         ),
         dict(
             result=(block, BF, VMEM),
@@ -1218,7 +1277,6 @@
             rup=((8, rows, unit), BF, VMEM),
             r3=((8, rows, 3 * w), BF, VMEM),
             ro=((rows, width), BF, VMEM),
-            rdn=((padded, width), BF, VMEM),
             totals=((8, 8, w), F32, VMEM),
         ),
         scratch(
@@ -1265,7 +1323,7 @@
         return m.reshape(rows, 8 * m.shape[2]).astype(F32)
 
     def unspread(m):
-        m = m.transpose(1, 0, 2).reshape(rows, 128, padded)[:, :, :down]
+        m = m.reshape(8, rows, 16, padded)[:, :, :, :down].transpose(1, 2, 0, 3)
         return m.reshape(rows, hidden_width).astype(F32)
 
     sums = D.totals.transpose(1, 0, 2).reshape(8, width)
@@ -1282,7 +1340,7 @@
         sums[1],
         unspread(D.rgate),
         unspread(D.rup),
-        D.rdn[:down].astype(F32),
+        C.block_ddn[:down].astype(F32),
         pullback(sums[3])[0],
     )
 

time: 419 us -> 349 us (0.83)
  Pallas kernels: 392 us -> 321 us
    pallas_call x4, Pallas kernels: 392 us -> 321 us  [call(): pl.pallas_call(run_body, name=name, out_shape=[jax.ShapeDtypeStruct(*v[:2...]
where the time goes in v4:
time: 349 us
  Pallas kernels  321 us (92%)
  local copies, waits for them, and re-layouts  19.6 us (6%)
  other arithmetic  6.32 us (2%)
    pallas_call x4, Pallas kernels, call(): pl.pallas_call(run_body, name=name, out_shape=[jax.ShapeDtypeStruct(*v[:2...  321 us

profile of v4, /device:TPU:1, one launch (start us, length us, event | category | flops | bytes accessed | tf_op | source)
XLA Modules:
  0.0 348.6 jit_solution(16838377574763458826)
XLA Ops:
  0.7 0.8 dynamic-slice_reduce_fusion
  1.4 0.8 fusion.5
  2.8 1.4 multiply_reduce_fusion
  4.2 1.3 dynamic_slice.7
  5.6 2.4 reshape.107
  8.1 0.1 pad_bitcast_fusion.1
  8.2 0.5 reshape.108
  8.6 2.4 reshape.109
  11.1 0.1 pad_bitcast_fusion
  11.2 0.5 reshape.110
  11.7 0.8 pad_maximum_fusion.refs_6_
  12.5 55.5 %gather.1 = (bf16[2,2,4,128,768]{4,3,2,1,0:T(8,128)(2,1)}, bf16[2,2,4,16,2048]{4,3,2,1,0:T(8,128)(2,1)}, bf16[1024,2048]{1,0:T(8,128)(2,1)}, bf16[4,64,1536]{2,1,0:T(8,128)(2,1)}, bf16[2,2,64,1536]{3,2,1,0:T(8,128)(2,1)}) custom-call(bf16[128,2048]{1,0:T(8,128)(2,1)} %refs_0_.5, f32[1,2048]{1,0:T(1,128)} %bitcast.54, bf16[16,2048]{1,0:T(8,128)(2,1)} %refs_2_.1, ...), custom_call_target="tpu_custom_call" | custom-call | tf_op jit(solution)/shard_map/gather/pallas_call | solution.py:489
  68.0 0.7 pad.13.refs_5_
  68.7 40.4 %scan.1 = (bf16[1024,256]{1,0:T(8,128)(2,1)}, f32[2,1024,128]{2,1,0:T(8,128)}, f32[2,1024,128]{2,1,0:T(8,128)}, f32[1024,768]{1,0:T(8,128)}, f32[8,128]{1,0:T(8,...) custom-call(f32[1,256]{1,0:T(1,128)} %bitcast.57, ...), custom_call_target="tpu_custom_call" | custom-call | tf_op jit(solution)/shard_map/scan/pallas_call | solution.py:489
  109.2 124.0 %feed.1 = (f32[128,2048]{1,0:T(8,128)}, f32[128,2048]{1,0:T(8,128)}, bf16[1024,2048]{1,0:T(8,128)(2,1)}, bf16[1024,2048]{1,0:T(8,128)(2,1)}, f32[8,2048]{1,0:T(8...) custom-call(bf16[128,2048]{1,0:T(8,128)(2,1)} %refs_0_.5, ...), custom_call_target="tpu_custom_call" | custom-call | tf_op jit(solution)/shard_map/feed/pallas_call | solution.py:489
  233.2 101.2 %back.1 = (bf16[128,2048]{1,0:T(8,128)(2,1)}, f32[128,2048]{1,0:T(8,128)}, bf16[8,16,768]{2,1,0:T(8,128)(2,1)}, bf16[8,16,768]{2,1,0:T(8,128)(2,1)}, bf16[8,16,7...) custom-call(bf16[128,2048]{1,0:T(8,128)(2,1)} %refs_0_.5, ...), custom_call_target="tpu_custom_call" | custom-call | tf_op jit(solution)/shard_map/back/pallas_call | solution.py:489
  334.4 1.6 fusion.6
  336.1 0.1 fusion.3
  336.2 0.8 fusion.1
  337.0 1.5 reshape.115
  338.7 0.6 copy.36
  339.3 1.3 reshape.120
  340.7 0.6 reshape.116
  341.4 0.6 copy.37
  342.0 1.3 reshape.121
  343.4 0.7 copy.38
  344.1 0.7 copy.39
  344.7 0.7 copy.40
  345.4 0.7 convert_element_type.65
  346.1 0.8 slice_convert_fusion
  346.9 0.8 copy.44
  347.7 1.0 copy.45
  (26 shorter events, 0.5 us)
Async XLA Ops:
  8.0 60.1 %copy-start.3 = (bf16[44,2048]{1,0:T(8,128)(2,1)S(1)}, bf16[44,2048]{1,0:T(8,128)(2,1)}, u32[]{:S(2)}) copy-start(bf16[44,2048]{1,0:T(8,128)(2,1)} %param.25) | copy-start | bytes 540676
  233.2 102.9 %copy-start = (f32[24,2048]{1,0:T(8,128)S(1)}, f32[24,2048]{1,0:T(8,128)}, u32[]{:S(2)}) copy-start(f32[24,2048]{1,0:T(8,128)} %param.26) | copy-start | bytes 589828
  334.4 6.3 %copy-start.6 = (bf16[8,16,768]{2,1,0:T(8,128)(2,1)S(1)}, bf16[8,16,768]{2,1,0:T(8,128)(2,1)}, u32[]{:S(2)}) copy-start(bf16[8,16,768]{2,1,0:T(8,128)(2,1)} %get-tuple-element.71) | copy-start | bytes 589828
  338.7 4.7 %copy-start.5 = (bf16[8,16,768]{2,1,0:T(8,128)(2,1)S(1)}, bf16[8,16,768]{2,1,0:T(8,128)(2,1)}, u32[]{:S(2)}) copy-start(bf16[8,16,768]{2,1,0:T(8,128)(2,1)} %get-tuple-element.68) | copy-start | bytes 589828
  339.3 6.1 %copy-start.7 = (bf16[16,2048]{1,0:T(8,128)(2,1)S(1)}, bf16[16,2048]{1,0:T(8,128)(2,1)}, u32[]{:S(2)}) copy-start(bf16[16,2048]{1,0:T(8,128)(2,1)} %get-tuple-element.69) | copy-start | bytes 196612
  339.3 6.8 %copy-start.4 = (bf16[48,2048]{1,0:T(8,128)(2,1)S(1)}, bf16[48,2048]{1,0:T(8,128)(2,1)}, u32[]{:S(2)}) copy-start(bf16[48,2048]{1,0:T(8,128)(2,1)} %get-tuple-element.72) | copy-start | bytes 589828
  340.7 6.2 %copy-start.2 = (bf16[128,2048]{1,0:T(8,128)(2,1)S(1)}, bf16[128,2048]{1,0:T(8,128)(2,1)}, u32[]{:S(2)}) copy-start(bf16[128,2048]{1,0:T(8,128)(2,1)} %get-tuple-element.93) | copy-start | bytes 1572868
  341.3 6.3 %copy-start.1 = (f32[128,2048]{1,0:T(8,128)S(1)}, f32[128,2048]{1,0:T(8,128)}, u32[]{:S(2)}) copy-start(f32[128,2048]{1,0:T(8,128)} %get-tuple-element.94) | copy-start | bytes 3145732

commit v5 on v4

--- a/solution.py
+++ b/solution.py
@@ -207,14 +207,40 @@
 class GroupGather:
     def __init__(self, cp, src, full):
         self.cp, self.full = cp, full
-        self.at = full.at[block_of(place()[1])]
-        self.moved = {s: cp.send(src, self.at, ring("y", s)) for s in STEPS}
-        self.near = {0: cp.send(src, self.at, sibling())}
+        k = place()[1]
+        self.half = {}
+        for first in (0, 1):
+            for s in (1, 3):
+                h = first if s == 1 else 1 - first
+                self.half[s, h] = cp.send(
+                    src.at[pl.ds(64 * h, 64)], full.at[self.rows(k, h)], ring("y", s)
+                )
+        self.near = {0: cp.send(src, full.at[block_of(k)], sibling())}
+        self.done = set()
+
+    def rows(self, k, h):
+        return pl.ds(pl.multiple_of(k * 128 + 64 * h, 64), 64)
+
+    def chip(self, s):
+        return 2 * lax.rem(ax("y") + 4 - s, 4) + ax("core")
+
+    def arrived(self, s, h):
+        if (s, h) not in self.done:
+            self.done.add((s, h))
+            self.half[s, h].wait_recv()
+
+    def relay(self):
+        for s, h in ((1, 0), (3, 1)):
+            self.arrived(s, h)
+            at = self.full.at[self.rows(self.chip(s), h)]
+            self.half[2, h] = self.cp.send(at, at, ring("y", s))
 
     def forward(self, s):
-        self.moved[s].wait_recv()
-        k = 2 * lax.rem(ax("y") + 4 - s, 4) + ax("core")
-        at = self.full.at[block_of(k)]
+        if (2, 0) not in self.half:
+            self.relay()
+        self.arrived(s, 0)
+        self.arrived(s, 1)
+        at = self.full.at[block_of(self.chip(s))]
         self.near[s] = self.cp.send(at, at, sibling())
 
     def ready(self, s):
@@ -271,8 +297,62 @@
         return rows
 
 
+class RelaySum(GroupSum):
+    def piece(self, mine, at, h):
+        return mine.at[pl.ds(pl.multiple_of(at + 64 * h, 64), 64)]
+
+    def plus(self, mine, at, term, n):
+        def step(i, carry):
+            to = pl.ds(pl.multiple_of(at + i * 16, 16), 16)
+            mine[to, :] = (mine[to, :].astype(F32) + term(rows_of(i)).astype(F32)).astype(BF)
+            return carry
+
+        lax.fori_loop(0, n // 16, step, 0)
+
+    def to(self, s, slot, h, mine, at):
+        return self.cp.send(
+            self.piece(mine, at, h), self.far.at[slot, pl.ds(64 * h, 64)], ring("y", s)
+        )
+
+    def add(self, s, mine, at):
+        near = self.near
+        self.sent[s].wait_recv()
+        self.plus(mine, at, lambda r: near[s, r, :], 128)
+        if s == 2:
+            self.hop = [self.to(1, 2, 0, mine, at), self.to(3, 2, 1, mine, at)]
+        elif s == 1:
+            self.moved[1, 1] = self.to(1, 0, 1, mine, at)
+        else:
+            self.moved[3, 0] = self.to(3, 1, 0, mine, at)
+
+    def relay(self, mine, at_next, at_last):
+        far = self.far
+        self.hop[0].wait_recv()
+        self.plus(mine, at_next, lambda r: far[2, r, :], 64)
+        self.moved[1, 0] = self.to(1, 0, 0, mine, at_next)
+        self.hop[1].wait_recv()
+        up = lambda r: far[2, pl.ds(pl.multiple_of(64 + r.start, 16), 16), :]
+        self.plus(mine, at_last + 64, up, 64)
+        self.moved[3, 1] = self.to(3, 1, 1, mine, at_last)
+
+    def total(self, mine, at):
+        self.sent[0].wait_recv()
+        for key in ((1, 1), (3, 0), (1, 0), (3, 1)):
+            self.moved[key].wait_recv()
+        self.cp.sent(self.hop + list(self.moved.values()))
+        near, far = self.near, self.far
+
+        def rows(i):
+            r = rows_of(i)
+            own = mine[pl.ds(pl.multiple_of(at + i * 16, 16), 16), :]
+            acc = own.astype(F32) + near[0, r, :].astype(F32)
+            return acc + (far[0, r, :].astype(F32) + far[1, r, :].astype(F32))
+
+        return rows
+
+
 def sum_of(cp, part, mine, near, far):
-    total = GroupSum(cp, near, far)
+    total = RelaySum(cp, near, far)
     c = ax("core")
     own = {}
     for s in (2, 1, 3, 0):
@@ -283,6 +363,8 @@
         own[s].wait()
         total.add(s, mine, 128 * s)
     own[0].wait()
+    yield
+    total.relay(mine, 128, 384)
     yield
     yield total.total(mine, 0)
 
@@ -557,10 +639,13 @@
     shuffle.wait(moved)
     bo = plane_gather(cp, R.bo, by_columns(*R.bo.shape[3:]))
     next(bo)
+    next(b3)
+    next(bo)
     settle(*arrive_gu)
     gu = plane_first(cp, R.block_gu, R.gu_column, R.gu_row, by_rows(*R.block_gu.shape))
     next(gu)
-    run([b3, bo, gu], (0, 1, 0, 1, 2))
+    chain.relay()
+    run([b3, bo, gu], (0, 1, 2))
     chain.rest()
     own.wait()
     cp.finish()
@@ -635,6 +720,7 @@
     project(0)
     project(1)
     next(bulk)
+    chain.relay()
 
     def gates(i, c):
         r = rows_of(i, 32)
@@ -645,6 +731,7 @@
         return c
 
     lax.fori_loop(0, rows // 32, gates, 0)
+    keep = [cp.local(R.forget, R.forget_out)]
 
     def step(t, c):
         at = pl.ds(t, 8, stride=steps)
@@ -674,6 +761,7 @@
     k = ax("xhi") * 4 + ax("z")
     small = share(cp, R.mine, R.links, k, peers_chain)
     project(2)
+    keep.append(cp.local(R.proj, R.proj_out))
     for copy in small:
         copy.wait_recv()
     come = links_before(R.links, k, w)
@@ -688,6 +776,7 @@
         return c
 
     lax.fori_loop(0, 8, finish, 0)
+    keep.append(cp.local(R.states, R.states_out))
     small = share(cp, R.rowsum, R.rows8, place()[1], peers_group)
     next(bulk)
     for copy in small:
@@ -705,15 +794,21 @@
         return c
 
     lax.fori_loop(0, 8, gate, 0)
+    keep.append(cp.local(R.gated, R.gated_out))
     load_out.wait()
-
-    def out(i, c):
-        at = rows_of(i, 512)
-        R.part[:, at] = dot(R.gated[...], R.wo[:, at], NN).astype(BF)
-        return c
-
-    lax.fori_loop(0, R.part.shape[1] // 512, out, 0)
+    for i in range(4):
+        r = pl.ds(i * rows // 4, rows // 4)
+
+        def out(j, c, r=r):
+            at = rows_of(j, 512)
+            R.part[r, at] = dot(R.gated[r, :], R.wo[:, at], NN).astype(BF)
+            return c
+
+        lax.fori_loop(0, R.part.shape[1] // 512, out, 0)
+        keep.append(cp.local(R.part.at[r], R.part_out.at[r]))
     chain.rest()
+    for copy in keep:
+        copy.wait()
     own.wait()
     drain(bulk)
     cp.finish()
@@ -729,6 +824,7 @@
     mixer = sum_of(cp, R.part, R.ps, R.near, R.far)
     next(mixer)
     load = [cp.local(R.gf, R.g), cp.local(R.bdn, R.wdn)]
+    next(mixer)
     next(mixer)
     next(weights)
     terms = next(mixer)
@@ -862,6 +958,7 @@
 
     for i in range(width // 256):
         grad_up(i)
+    branch.relay()
     for copy in ups[-2:]:
         copy.wait()
     next(planes[0])
@@ -880,6 +977,19 @@
 
 def plane_work(key, halves):
     return {"plane_" + key + str(i): v for i, v in enumerate(plane_sum_scratch(halves))}
+
+
+def grad_weights(R, start, dst):
+    n = dst.shape[4]
+
+    def tile(i, carry):
+        at = rows_of(i, 256)
+        v = dot(R.x[:, at], R.grads[:, start : start + n], TN).astype(BF)
+        to = (lax.div(i, 4), lax.rem(lax.div(i, 2), 2), pl.ds(2 * lax.rem(i, 2), 2))
+        dst[to] = v.reshape(2, 128, n)
+        return carry
+
+    lax.fori_loop(0, R.x.shape[1] // 256, tile, 0)
 
 
 def back_body(R, cp):
@@ -893,9 +1003,16 @@
     peers_chain = [in_chain(*st) for st in CHAIN]
     peers_group = [in_group(*st) for st in GROUP]
     peers_plane = [in_plane(*st) for st in PLANE]
+    load = [cp.local(R.gb, R.gbv), cp.local(R.bo, R.wo)]
+    load_scan = [
+        cp.local(R.states_in, R.states),
+        cp.local(R.proj_in, R.proj),
+        cp.local(R.forget_in, R.forget),
+        cp.local(R.gated_in, R.gated),
+    ]
+    load_x = cp.local(R.fi, R.x)
+    load_last = [cp.local(R.b3, R.w3), cp.local(R.mid_in, R.mid), cp.local(R.mixed_in, R.mixed)]
     greet(peers_plane + peers_group, shuffle.greeting)
-    load = [cp.local(R.gb, R.gbv), cp.local(R.bo, R.wo)]
-    load_last = [cp.local(R.b3, R.w3), cp.local(R.fi, R.x)]
     res = sum_of(cp, R.part_r, R.pr, R.pr_near, R.pr_far)
     next(res)
     up = plane_sum(cp, R.dup, by_rows(*R.dup.shape[3:]), *plane_refs(R, "a"), R.block_dup)
@@ -909,6 +1026,8 @@
         r = pl.ds(i * rows // 2, rows // 2)
         R.gg[r, :] = dot(R.gbv[r, :], R.wo[...], NT)
     next(res)
+    for copy in load_scan:
+        copy.wait()
 
     def through(s, carry):
         r = chunk_rows(s)
@@ -925,6 +1044,7 @@
 
     lax.fori_loop(0, 8, through, 0)
     small = share(cp, R.rowsum, R.rows8, g, peers_group)
+    next(res)
     def grad_out(j, carry):
         at = rows_of(j, 512)
         v = dot(R.gated[...], R.gbv[:, at], TN).astype(BF)
@@ -934,6 +1054,10 @@
     lax.fori_loop(0, width // 512, grad_out, 0)
     outs = plane_sum(cp, R.do, by_columns(*R.do.shape[3:]), *plane_refs(R, "b"), R.oo)
     next(outs)
+    load_x.wait()
+    grad_weights(R, 2 * w, R.d1)
+    one = plane_sum(cp, R.d1, by_rows(*R.d1.shape[3:]), *plane_refs(R, "d"), R.o1)
+    next(one)
     for copy in small:
         copy.wait_recv()
     total = R.rows8[0]
@@ -1008,9 +1132,13 @@
     lax.fori_loop(0, 8, last, 0)
     for copy in load_last:
         copy.wait()
+    grad_weights(R, 0, R.d2)
+    two = plane_sum(cp, R.d2, by_rows(*R.d2.shape[3:]), *plane_refs(R, "c"), R.o2)
+    next(two)
+    next(one)
     R.va[...] = jnp.zeros_like(R.va)
     R.va[1:2, :] = R.ffn_sums[0:1, :]
-    first = GroupSum(cp, R.near, R.far)
+    first = RelaySum(cp, R.near, R.far)
     order = (2, 1, 3, 0)
     for i, s in enumerate(order):
         chip = first.chip(s)
@@ -1030,6 +1158,7 @@
         if i > 0:
             back = order[i - 1]
             first.add(back, R.fp, 128 * (first.chip(back) + c))
+    first.relay(R.fp, 128 * (first.chip(1) + c), 128 * (first.chip(3) + c))
 
     gains = []
     for st in GROUP:
@@ -1038,19 +1167,10 @@
         gains.append(cp.send(R.va.at[:, rows_of(k, w)], R.ga.at[g], dev))
     R.ga[pl.ds(g, 1)] = R.va[:, rows_of(g, w)][None]
 
-    def grad_three(i, carry):
-        at = rows_of(i, 256)
-        v = dot(R.x[:, at], R.grads[...], TN).astype(BF)
-        to = (lax.div(i, 4), lax.rem(lax.div(i, 2), 2), pl.ds(2 * lax.rem(i, 2), 2))
-        R.d3[to] = v.reshape(2, 128, 3 * w)
-        return carry
-
-    lax.fori_loop(0, width // 256, grad_three, 0)
-    three = plane_sum(cp, R.d3, by_rows(*R.d3.shape[3:]), *plane_refs(R, "c"), R.o3)
-    next(three)
-    drain(up, outs)
+    drain(up, outs, one)
     arrive = [
         gate_home,
+        to_group(cp, lambda k: R.o1.at[rows_of(k), :], lambda k: R.r1.at[k]),
         to_group(cp, lambda k: R.block_dup.at[rows_of(k), :], lambda k: R.rup.at[k]),
     ]
     moved = shuffle.start(cp, R.oo, R.ro)
@@ -1076,7 +1196,7 @@
 
     lax.fori_loop(0, 8, finish_result, 0)
     small = share(cp, R.tb, R.totals, g, peers_group)
-    next(three)
+    next(two)
     terms_first = first.total(R.fp, 128 * g)
 
     def back(i, carry):
@@ -1090,8 +1210,8 @@
         return carry
 
     lax.fori_loop(0, 8, back, 0)
-    drain(three)
-    arrive.append(to_group(cp, lambda k: R.o3.at[rows_of(k), :], lambda k: R.r3.at[k]))
+    drain(two)
+    arrive.append(to_group(cp, lambda k: R.o2.at[rows_of(k), :], lambda k: R.r2.at[k]))
     for copy in small:
         copy.wait_recv()
     for pair in arrive:
@@ -1173,18 +1293,23 @@
             cot=(cotangent, VMEM),
         ),
         dict(
-            gated=((8 * n, w), BF, VMEM),
-            states=(column, F32, VMEM),
-            forget=(column, F32, VMEM),
-            proj=((8 * n, 3 * w), F32, VMEM),
+            gated_out=((8 * n, w), BF, ANY),
+            states_out=(column, F32, ANY),
+            forget_out=(column, F32, ANY),
+            proj_out=((8 * n, 3 * w), F32, ANY),
             tot=((8, n), F32, VMEM),
             links=((8, 8, w), F32, VMEM),
             carry=((8, w), F32, VMEM),
-            part=(full, BF, VMEM),
+            part_out=(full, BF, ANY),
             gf=(full, BF, ANY),
             bdn=((2, 2, 4, padded, width), BF, ANY),
         ),
         scratch(
+            gated=((8 * n, w), BF),
+            states=(column, F32),
+            forget=(column, F32),
+            proj=((8 * n, 3 * w), F32),
+            part=(full, BF),
             w3=((width, 3 * w), BF),
             x=(full, BF),
             wo=((w, width), BF),
@@ -1195,7 +1320,7 @@
             rows8=((8, 8, n), F32),
         ),
         48,
-        8,
+        16,
     )
     gains_two = mlp_gain[None, :]
     C = call(
@@ -1206,7 +1331,7 @@
             tok=(tokens, VMEM),
             cot=(cotangent, VMEM),
             gain=(gains_two, VMEM),
-            part=(B.part, ANY),
+            part=(B.part_out, ANY),
             gu_column=(A.gu_column, ANY),
             gu_row=(A.gu_row, ANY),
             bdn=(B.bdn.reshape(unit, width), ANY),
@@ -1249,16 +1374,16 @@
         3,
         dict(
             tok=(tokens, VMEM),
-            mid=(C.mid, VMEM),
-            mixed=(C.mixed, VMEM),
+            mid_in=(C.mid, ANY),
+            mixed_in=(C.mixed, ANY),
             attn_gain=(gains, VMEM),
             lb=(lower, VMEM),
             gain=(mixer_gain, VMEM),
             ffn_sums=(C.sums, VMEM),
-            states=(B.states, VMEM),
-            forget=(B.forget, VMEM),
-            proj=(B.proj, VMEM),
-            gated=(B.gated, VMEM),
+            states_in=(B.states_out, ANY),
+            forget_in=(B.forget_out, ANY),
+            proj_in=(B.proj_out, ANY),
+            gated_in=(B.gated_out, ANY),
             tot=(B.tot, VMEM),
             links=(B.links, VMEM),
             carry=(B.carry, VMEM),
@@ -1275,11 +1400,18 @@
             gtok=(block, F32, VMEM),
             rgate=((8, rows, unit), BF, VMEM),
             rup=((8, rows, unit), BF, VMEM),
-            r3=((8, rows, 3 * w), BF, VMEM),
+            r1=((8, rows, w), BF, VMEM),
+            r2=((8, rows, 2 * w), BF, VMEM),
             ro=((rows, width), BF, VMEM),
             totals=((8, 8, w), F32, VMEM),
         ),
         scratch(
+            states=(column, F32),
+            forget=(column, F32),
+            proj=((8 * n, 3 * w), F32),
+            gated=((8 * n, w), BF),
+            mid=(block, F32),
+            mixed=(block, F32),
             gbv=(full, BF),
             wo=((w, width), BF),
             w3=((width, 3 * w), BF),
@@ -1301,9 +1433,11 @@
             near=((4,) + block, BF),
             far=((3,) + block, BF),
             do=((2, 2, 4, rows, width), BF),
-            d3=((2, 2, 4, 8 * rows, 3 * w), BF),
+            d1=((2, 2, 4, 8 * rows, w), BF),
+            d2=((2, 2, 4, 8 * rows, 2 * w), BF),
             block_dup=((8 * rows, unit), BF),
-            o3=((8 * rows, 3 * w), BF),
+            o1=((8 * rows, w), BF),
+            o2=((8 * rows, 2 * w), BF),
             oo=((rows, width), BF),
             va=((8, width), F32),
             ga=((8, 8, w), F32),
@@ -1313,8 +1447,9 @@
         )
         | plane_work("a", by_rows(8 * rows, unit))
         | plane_work("b", by_columns(rows, width))
-        | plane_work("c", by_rows(8 * rows, 3 * w)),
-        150,
+        | plane_work("c", by_rows(8 * rows, 2 * w))
+        | plane_work("d", by_rows(8 * rows, w)),
+        160,
         30,
     )
 
@@ -1332,9 +1467,9 @@
         D.result,
         D.gtok,
         sums[0],
-        join(D.r3[:, :, :w]),
-        join(D.r3[:, :, w : 2 * w]),
-        join(D.r3[:, :, 2 * w :]),
+        join(D.r2[:, :, :w]),
+        join(D.r2[:, :, w:]),
+        join(D.r1),
         D.ro.astype(F32),
         sums[2],
         sums[1],

time: 349 us -> 334 us (0.957)
  Pallas kernels: 321 us -> 306 us
    pallas_call x4, Pallas kernels: 321 us -> 306 us  [call(): pl.pallas_call(run_body, name=name, out_shape=[jax.ShapeDtypeStruct(*v[:2...]
where the time goes in v5:
time: 334 us; the launch traced here: 333 us
  Pallas kernels  306 us (92%)
  local copies, waits for them, and re-layouts  19.6 us (6%)
  other arithmetic  6.32 us (2%)
    pallas_call x4, Pallas kernels, call(): pl.pallas_call(run_body, name=name, out_shape=[jax.ShapeDtypeStruct(*v[:2...  306 us

profile of v5, /device:TPU:1, one launch (start us, length us, event | category | flops | bytes accessed | tf_op | source)
XLA Modules:
  0.0 333.5 jit_solution(8089621906084439259)
XLA Ops:
  0.7 0.8 dynamic-slice_reduce_fusion
  1.4 0.8 fusion.5
  2.8 1.4 multiply_reduce_fusion
  4.2 1.3 dynamic_slice.7
  5.6 2.4 reshape.107
  8.1 0.1 pad_bitcast_fusion.1
  8.2 0.5 reshape.108
  8.6 2.4 reshape.109
  11.1 0.1 pad_bitcast_fusion
  11.2 0.5 reshape.110
  11.7 0.8 pad_maximum_fusion.refs_6_
  12.5 57.9 %gather.1 = (bf16[2,2,4,128,768]{4,3,2,1,0:T(8,128)(2,1)}, bf16[2,2,4,16,2048]{4,3,2,1,0:T(8,128)(2,1)}, bf16[1024,2048]{1,0:T(8,128)(2,1)}, bf16[4,64,1536]{2,1,0:T(8,128)(2,1)}, bf16[2,2,64,1536]{3,2,1,0:T(8,128)(2,1)}) custom-call(bf16[128,2048]{1,0:T(8,128)(2,1)} %refs_0_.5, f32[1,2048]{1,0:T(1,128)} %bitcast.54, bf16[16,2048]{1,0:T(8,128)(2,1)} %refs_2_.1, ...), custom_call_target="tpu_custom_call" | custom-call | tf_op jit(solution)/shard_map/gather/pallas_call | solution.py:571
  70.4 0.7 pad.13.refs_5_
  71.1 38.6 %scan.1 = (bf16[1024,256]{1,0:T(8,128)(2,1)}, f32[2,1024,128]{2,1,0:T(8,128)}, f32[2,1024,128]{2,1,0:T(8,128)}, f32[1024,768]{1,0:T(8,128)}, f32[8,128]{1,0:T(8,...) custom-call(f32[1,256]{1,0:T(1,128)} %bitcast.57, ...), custom_call_target="tpu_custom_call" | custom-call | tf_op jit(solution)/shard_map/scan/pallas_call | solution.py:571
  109.7 118.3 %feed.1 = (f32[128,2048]{1,0:T(8,128)}, f32[128,2048]{1,0:T(8,128)}, bf16[1024,2048]{1,0:T(8,128)(2,1)}, bf16[1024,2048]{1,0:T(8,128)(2,1)}, f32[8,2048]{1,0:T(8...) custom-call(bf16[128,2048]{1,0:T(8,128)(2,1)} %refs_0_.5, ...), custom_call_target="tpu_custom_call" | custom-call | tf_op jit(solution)/shard_map/feed/pallas_call | solution.py:571
  228.0 91.2 %back.1 = (bf16[128,2048]{1,0:T(8,128)(2,1)}, f32[128,2048]{1,0:T(8,128)}, bf16[8,16,768]{2,1,0:T(8,128)(2,1)}, bf16[8,16,768]{2,1,0:T(8,128)(2,1)}, bf16[8,16,2...) custom-call(bf16[128,2048]{1,0:T(8,128)(2,1)} %refs_0_.5, ...), custom_call_target="tpu_custom_call" | custom-call | tf_op jit(solution)/shard_map/back/pallas_call | solution.py:571
  319.2 1.6 fusion.6
  321.0 0.1 fusion.3
  321.1 0.8 fusion.1
  321.9 1.5 reshape.115
  323.5 0.6 copy.36
  324.2 1.3 reshape.120
  325.5 0.6 reshape.116
  326.3 0.6 copy.37
  326.9 1.3 reshape.121
  328.3 0.7 copy.38
  328.9 0.7 copy.39
  329.6 0.7 copy.40
  330.3 0.7 convert_element_type.65
  330.9 0.8 slice_convert_fusion
  331.7 0.8 copy.44
  332.5 1.0 copy.45
  (28 shorter events, 0.5 us)
Async XLA Ops:
  8.0 62.4 %copy-start.3 = (bf16[44,2048]{1,0:T(8,128)(2,1)S(1)}, bf16[44,2048]{1,0:T(8,128)(2,1)}, u32[]{:S(2)}) copy-start(bf16[44,2048]{1,0:T(8,128)(2,1)} %param.25) | copy-start | bytes 540676
  228.0 92.9 %copy-start = (f32[24,2048]{1,0:T(8,128)S(1)}, f32[24,2048]{1,0:T(8,128)}, u32[]{:S(2)}) copy-start(f32[24,2048]{1,0:T(8,128)} %param.26) | copy-start | bytes 589828
  319.2 6.3 %copy-start.5 = (bf16[8,16,768]{2,1,0:T(8,128)(2,1)S(1)}, bf16[8,16,768]{2,1,0:T(8,128)(2,1)}, u32[]{:S(2)}) copy-start(bf16[8,16,768]{2,1,0:T(8,128)(2,1)} %get-tuple-element.73) | copy-start | bytes 589828
  323.5 4.7 %copy-start.6 = (bf16[8,16,512]{2,1,0:T(8,128)(2,1)S(1)}, bf16[8,16,512]{2,1,0:T(8,128)(2,1)}, u32[]{:S(2)}) copy-start(bf16[8,16,512]{2,1,0:T(8,128)(2,1)} %get-tuple-element.69) | copy-start | bytes 393220
  323.5 4.7 %copy-start.8 = (bf16[8,16,256]{2,1,0:T(8,128)(2,1)S(1)}, bf16[8,16,256]{2,1,0:T(8,128)(2,1)}, u32[]{:S(2)}) copy-start(bf16[8,16,256]{2,1,0:T(8,128)(2,1)} %get-tuple-element.70) | copy-start | bytes 196612
  324.1 6.1 %copy-start.7 = (bf16[16,2048]{1,0:T(8,128)(2,1)S(1)}, bf16[16,2048]{1,0:T(8,128)(2,1)}, u32[]{:S(2)}) copy-start(bf16[16,2048]{1,0:T(8,128)(2,1)} %get-tuple-element.71) | copy-start | bytes 196612
  324.2 6.8 %copy-start.4 = (bf16[48,2048]{1,0:T(8,128)(2,1)S(1)}, bf16[48,2048]{1,0:T(8,128)(2,1)}, u32[]{:S(2)}) copy-start(bf16[48,2048]{1,0:T(8,128)(2,1)} %get-tuple-element.74) | copy-start | bytes 589828
  325.5 6.2 %copy-start.2 = (bf16[128,2048]{1,0:T(8,128)(2,1)S(1)}, bf16[128,2048]{1,0:T(8,128)(2,1)}, u32[]{:S(2)}) copy-start(bf16[128,2048]{1,0:T(8,128)(2,1)} %get-tuple-element.95) | copy-start | bytes 1572868
  326.1 6.3 %copy-start.1 = (f32[128,2048]{1,0:T(8,128)S(1)}, f32[128,2048]{1,0:T(8,128)}, u32[]{:S(2)}) copy-start(f32[128,2048]{1,0:T(8,128)} %get-tuple-element.96) | copy-start | bytes 3145732

commit v6 on v5

--- a/solution.py
+++ b/solution.py
@@ -110,7 +110,7 @@
             copy.wait_send()
 
 
-def greet(peers, shuffle=None):
+def hail(peers, shuffle=None):
     bar = pltpu.get_barrier_semaphore()
     for dev in peers:
         pl.semaphore_signal(bar, inc=1, device_id=dev, device_id_type=MESH)
@@ -123,7 +123,11 @@
             pl.semaphore_signal(bar, inc=1, device_id=source, device_id_type=MESH)
 
         count = count + jnp.where(to_me, 0, 1)
-    pl.semaphore_wait(bar, count)
+    return lambda: pl.semaphore_wait(bar, count)
+
+
+def greet(peers):
+    hail(peers)()
 
 
 def to_group(cp, source, dst):
@@ -410,7 +414,7 @@
 
 def plane_first(cp, block, column, row, halves):
     me = (ax("xlo"), ax("xhi"), ax("z"))
-    top, bottom = block.at[halves[0]], block.at[halves[1]]
+    top, bottom = [block.at[h] for h in halves]
     home = [cp.local(top, column.at[me[2]]), cp.local(bottom, row.at[me[0], me[1]])]
     first = []
     for s in STEPS:
@@ -602,10 +606,38 @@
     return lax.dot_general(a, b, (dims, ((), ())), preferred_element_type=F32)
 
 
+def spread(m, out, start, down, padded):
+    x = m[...].astype(F32)
+    none = jnp.zeros((m.shape[0], padded - down), F32)
+    for k in range(8):
+        runs = []
+        for p in range(16):
+            at = (8 * p + k) * down
+            runs += [x[:, at : at + down], none]
+        out[k, :, start : start + 16 * padded] = jnp.concatenate(runs, axis=1).astype(BF)
+
+
+def unspread(m, out, down, padded):
+    for k in range(8):
+        for p in range(16):
+            at = (8 * p + k) * down
+            out[:, at : at + down] = m[k, :, padded * p : padded * p + down].astype(F32)
+
+
 def gather_body(R, cp):
     g = place()[1]
     shuffle = Shuffle(True)
-    greet(rings() + [in_group(*st) for st in GROUP], shuffle.greeting)
+    meet = hail(rings() + [in_group(*st) for st in GROUP], shuffle.greeting)
+
+    def norm(i, carry):
+        r = rows_of(i)
+        x = R.tok[r, :].astype(F32)
+        s = lax.rsqrt(jnp.mean(x * x, axis=-1, keepdims=True) + EPS)
+        R.first[r, :] = (x * s * R.gain[...]).astype(BF)
+        return carry
+
+    lax.fori_loop(0, R.tok.shape[0] // 16, norm, 0)
+    meet()
     me = (ax("xlo"), ax("xhi"), ax("z"))
     third = R.w_in.shape[1] // 8
     arrive = []
@@ -620,16 +652,8 @@
     q = shuffle.to[0]
     at = (lax.div(q, 8), lax.rem(lax.div(q, 4), 2), lax.rem(q, 4))
     moved = shuffle.start(cp, R.w_o, R.bo.at[at])
-    arrive_gu = to_group(cp, lambda k: R.gu.at[k], lambda k: R.block_gu.at[rows_of(k), :])
-
-    def norm(i, carry):
-        r = rows_of(i)
-        x = R.tok[r, :].astype(F32)
-        s = lax.rsqrt(jnp.mean(x * x, axis=-1, keepdims=True) + EPS)
-        R.first[r, :] = (x * s * R.gain[...]).astype(BF)
-        return carry
-
-    lax.fori_loop(0, R.tok.shape[0] // 16, norm, 0)
+    dn = plane_first(cp, R.dn, R.dn_column, R.dn_row, by_columns(*R.dn.shape))
+    next(dn)
     own = cp.local(R.first, R.fi.at[block_of(g)])
     chain = GroupGather(cp, R.first, R.fi)
     for pair in arrive:
@@ -641,11 +665,8 @@
     next(bo)
     next(b3)
     next(bo)
-    settle(*arrive_gu)
-    gu = plane_first(cp, R.block_gu, R.gu_column, R.gu_row, by_rows(*R.block_gu.shape))
-    next(gu)
     chain.relay()
-    run([b3, bo, gu], (0, 1, 2))
+    run([b3, bo, dn], (2, 0, 1))
     chain.rest()
     own.wait()
     cp.finish()
@@ -684,6 +705,13 @@
     copies = [cp.send(src, dst.at[index], dev) for dev in peers]
     dst[pl.ds(index, 1)] = src[...][None]
     return copies
+
+
+def levels(table, layer):
+    e = jnp.exp(table - jnp.max(table, axis=0, keepdims=True))
+    level = lax.broadcasted_iota(jnp.int32, table.shape, 0)
+    counts = jnp.where((level >= 1) & (level <= layer), 1.0, 0.0)
+    return e / jnp.sum(e, axis=0, keepdims=True), counts
 
 
 def links_before(links, k, w):
@@ -700,14 +728,24 @@
     steps = rows // 8
     peers_chain = [in_chain(*st) for st in CHAIN]
     peers_group = [in_group(*st) for st in GROUP]
-    greet(peers_chain + peers_group + [ring("x", s) for s in (1, 3)])
     load = [cp.local(R.b3, R.w3), cp.local(R.fi, R.x)]
     load_out = cp.local(R.bo, R.wo)
+    meet = hail(peers_chain + peers_group + [ring("x", s) for s in (1, 3)])
+    mine = rows_of(place()[1], w)
+    prob, keep_mask = levels(R.table[:, mine], R.layer[...])
+    low = jnp.sum(prob * keep_mask, axis=0, keepdims=True)
+    R.lb[...] = jnp.broadcast_to(low, (8, w))
+    gain = R.gain[:, mine]
+    unit = R.gu.shape[2] // 2
+    down = R.w_gate.shape[1] // 128
+    spread(R.w_gate, R.gu, 0, down, unit // 16)
+    spread(R.w_up, R.gu, unit, down, unit // 16)
+    meet()
+    arrive_gu = to_group(cp, lambda k: R.gu.at[k], lambda k: R.block_gu.at[rows_of(k), :])
     own = cp.local(R.cot, R.gf.at[block_of(place()[1])])
-    bulk = plane_gather(cp, R.bdn, by_columns(*R.bdn.shape[3:]), R.dn)
+    bulk = plane_second(cp, R.dn_column, R.dn_row, R.bdn, by_columns(*R.bdn.shape[3:]))
     next(bulk)
     chain = GroupGather(cp, R.cot, R.gf)
-    low = R.lb[...]
     for copy in load:
         copy.wait()
 
@@ -719,6 +757,9 @@
 
     project(0)
     project(1)
+    settle(*arrive_gu)
+    gate_up = plane_first(cp, R.block_gu, R.gu_column, R.gu_row, by_rows(*R.block_gu.shape))
+    next(gate_up)
     next(bulk)
     chain.relay()
 
@@ -778,7 +819,6 @@
     lax.fori_loop(0, 8, finish, 0)
     keep.append(cp.local(R.states, R.states_out))
     small = share(cp, R.rowsum, R.rows8, place()[1], peers_group)
-    next(bulk)
     for copy in small:
         copy.wait_recv()
     total = R.rows8[0]
@@ -790,7 +830,7 @@
         r = chunk_rows(s)
         v = R.proj[r, 2 * w : 3 * w]
         n = wide(R.states, r) * as_column(R.tot[pl.ds(s, 1), :], w)
-        R.gated[r, :] = (n * R.gain[...] * (v * jax.nn.sigmoid(v))).astype(BF)
+        R.gated[r, :] = (n * gain * (v * jax.nn.sigmoid(v))).astype(BF)
         return c
 
     lax.fori_loop(0, 8, gate, 0)
@@ -810,7 +850,7 @@
     for copy in keep:
         copy.wait()
     own.wait()
-    drain(bulk)
+    drain(bulk, gate_up)
     cp.finish()
 
 
@@ -1012,12 +1052,13 @@
     ]
     load_x = cp.local(R.fi, R.x)
     load_last = [cp.local(R.b3, R.w3), cp.local(R.mid_in, R.mid), cp.local(R.mixed_in, R.mixed)]
-    greet(peers_plane + peers_group, shuffle.greeting)
+    hail(peers_plane + peers_group, shuffle.greeting)()
+    gain = R.gain[:, rows_of(g, w)]
     res = sum_of(cp, R.part_r, R.pr, R.pr_near, R.pr_far)
     next(res)
     up = plane_sum(cp, R.dup, by_rows(*R.dup.shape[3:]), *plane_refs(R, "a"), R.block_dup)
     next(up)
-    low = R.lb[...]
+    low = R.lb[0:1, :]
     R.sums[...] = jnp.zeros_like(R.sums)
     gate_home = to_group(cp, lambda k: R.block_dgate.at[rows_of(k), :], lambda k: R.rgate.at[k])
     for copy in load:
@@ -1036,8 +1077,8 @@
         n = wide(R.states, r) * as_column(R.tot[pl.ds(s, 1), :], w)
         dy = R.gg[r, :]
         R.sums[0:1, :] = R.sums[0:1, :] + jnp.sum(dy * n * (v * sig), axis=0, keepdims=True)
-        R.grads[r, 2 * w : 3 * w] = (dy * n * R.gain[...] * silu_slope(v, sig)).astype(BF)
-        dy = dy * R.gain[...] * (v * sig)
+        R.grads[r, 2 * w : 3 * w] = (dy * n * gain * silu_slope(v, sig)).astype(BF)
+        dy = dy * gain * (v * sig)
         put(R.gs, r, dy)
         R.rowsum[pl.ds(s, 1), :] = row_sums(dy * n)
         return carry
@@ -1210,21 +1251,44 @@
         return carry
 
     lax.fori_loop(0, 8, back, 0)
-    drain(two)
-    arrive.append(to_group(cp, lambda k: R.o2.at[rows_of(k), :], lambda k: R.r2.at[k]))
+    for pair in arrive:
+        settle(*pair)
+    unit = R.rgate.shape[2]
+    down = R.g_gate.shape[1] // 128
+    unspread(R.rgate, R.g_gate, down, unit // 16)
+    unspread(R.rup, R.g_up, down, unit // 16)
     for copy in small:
         copy.wait_recv()
-    for pair in arrive:
-        settle(*pair)
+    for j in range(8):
+        at = pl.ds(j * w, w)
+        R.gains[:, at] = R.totals[j]
+        R.g_og[:, at] = R.r1[j].astype(F32)
+    prob, counts = levels(R.table[...], R.layer[...])
+    bound = jnp.sum(prob * counts, axis=0, keepdims=True)
+    R.g_table[...] = R.gains[3:4, :] * prob * (counts - bound)
     shuffle.wait(moved)
+    R.g_out[...] = R.ro[...].astype(F32)
+    drain(two)
+    settle(*to_group(cp, lambda k: R.o2.at[rows_of(k), :], lambda k: R.r2.at[k]))
+    for j in range(8):
+        at = pl.ds(j * w, w)
+        R.g_in[:, at] = R.r2[j, :, 0:w].astype(F32)
+        R.g_forget[:, at] = R.r2[j, :, w : 2 * w].astype(F32)
     cp.finish()
 
 
-def bound_value(bound_table, layer_idx):
-    probabilities = jax.nn.softmax(bound_table, axis=0)
-    levels = jnp.arange(bound_table.shape[0], dtype=jnp.int32)[:, None]
-    keep = jnp.where((levels >= 1) & (levels <= layer_idx[0]), 1.0, 0.0).astype(F32)
-    return jnp.sum(probabilities * keep, axis=0)
+def write_body(*refs):
+    count = (len(refs) - 3) // 2
+    ins, outs, sem = refs[:count], refs[count:-1], refs[-1]
+    copies = []
+    for i in range(count - 2):
+        copies.append(pltpu.make_async_copy(ins[i], outs[i], sem.at[i]))
+        copies[-1].start()
+    for i, row in enumerate((0, 2, 1)):
+        outs[count - 1 + i][...] = ins[count - 2][row : row + 1, :]
+    outs[count - 2][...] = ins[count - 1][...].astype(F32)[0 : outs[count - 2].shape[0]]
+    for copy in copies:
+        copy.wait()
 
 
 def on_device(
@@ -1238,12 +1302,6 @@
     unit = 16 * padded
     w = width // 8
 
-    def spread(m):
-        m = m.reshape(rows, 16, 8, down)
-        m = jnp.pad(m, ((0, 0), (0, 0), (0, 0), (0, padded - down)))
-        return m.transpose(2, 0, 1, 3).reshape(8, rows, unit)
-
-    gu = jnp.concatenate([spread(w_gate), spread(w_up)], axis=2)
     dn = jnp.pad(w_down, ((0, padded - down), (0, 0)))
     gains = attn_gain[None, :]
     full = (8 * n, width)
@@ -1260,36 +1318,37 @@
             w_f=(w_forget, VMEM),
             w_og=(w_outgate, VMEM),
             w_o=(w_out, VMEM),
-            gu=(gu, VMEM),
+            dn=(dn, VMEM),
         ),
         dict(
             b3=((2, 2, 4, 8 * rows, 3 * w), BF, ANY),
             bo=((2, 2, 4, rows, width), BF, ANY),
             fi=(full, BF, ANY),
-            gu_column=((4, 4 * rows, 2 * unit), BF, ANY),
-            gu_row=((2, 2, 4 * rows, 2 * unit), BF, ANY),
+            dn_column=((4, padded, width // 2), BF, ANY),
+            dn_row=((2, 2, padded, width // 2), BF, ANY),
         ),
-        scratch(first=(block, BF), block_gu=((8 * rows, 2 * unit), BF)),
+        scratch(first=(block, BF)),
         96,
         10,
     )
     big3 = A.b3.reshape(width, 3 * w)
     big_out = A.bo.reshape(w, width)
-    group = ax("y") * 2 + ax("core")
-    lower = bound_value(lax.dynamic_slice_in_dim(bound_table, group * w, w, 1), layer_idx)[None, :]
-    mixer_gain = lax.dynamic_slice_in_dim(norm_gain, group * w, w, 0)[None, :]
     column = (w // 128, 8 * n, 128)
     B = call(
         scan_body,
         "scan",
         1,
         dict(
-            lb=(lower, VMEM),
-            gain=(mixer_gain, VMEM),
+            table=(bound_table, VMEM),
+            layer=(layer_idx[None, :], VMEM),
+            gain=(norm_gain[None, :], VMEM),
             b3=(big3, ANY),
             bo=(big_out, ANY),
             fi=(A.fi, ANY),
-            dn=(dn, VMEM),
+            dn_column=(A.dn_column, VMEM),
+            dn_row=(A.dn_row, VMEM),
+            w_gate=(w_gate, VMEM),
+            w_up=(w_up, VMEM),
             cot=(cotangent, VMEM),
         ),
         dict(
@@ -1300,11 +1359,16 @@
             tot=((8, n), F32, VMEM),
             links=((8, 8, w), F32, VMEM),
             carry=((8, w), F32, VMEM),
+            lb=((8, w), F32, VMEM),
             part_out=(full, BF, ANY),
             gf=(full, BF, ANY),
             bdn=((2, 2, 4, padded, width), BF, ANY),
+            gu_column=((4, 4 * rows, 2 * unit), BF, ANY),
+            gu_row=((2, 2, 4 * rows, 2 * unit), BF, ANY),
         ),
         scratch(
+            gu=((8, rows, 2 * unit), BF),
+            block_gu=((8 * rows, 2 * unit), BF),
             gated=((8 * n, w), BF),
             states=(column, F32),
             forget=(column, F32),
@@ -1319,8 +1383,8 @@
             rowsum=((8, n), F32),
             rows8=((8, 8, n), F32),
         ),
-        48,
-        16,
+        64,
+        24,
     )
     gains_two = mlp_gain[None, :]
     C = call(
@@ -1332,8 +1396,8 @@
             cot=(cotangent, VMEM),
             gain=(gains_two, VMEM),
             part=(B.part_out, ANY),
-            gu_column=(A.gu_column, ANY),
-            gu_row=(A.gu_row, ANY),
+            gu_column=(B.gu_column, ANY),
+            gu_row=(B.gu_row, ANY),
             bdn=(B.bdn.reshape(unit, width), ANY),
             gf=(B.gf, ANY),
         ),
@@ -1377,8 +1441,10 @@
             mid_in=(C.mid, ANY),
             mixed_in=(C.mixed, ANY),
             attn_gain=(gains, VMEM),
-            lb=(lower, VMEM),
-            gain=(mixer_gain, VMEM),
+            lb=(B.lb, VMEM),
+            table=(bound_table, VMEM),
+            layer=(layer_idx[None, :], VMEM),
+            gain=(norm_gain[None, :], VMEM),
             ffn_sums=(C.sums, VMEM),
             states_in=(B.states_out, ANY),
             forget_in=(B.forget_out, ANY),
@@ -1398,14 +1464,22 @@
         dict(
             result=(block, BF, VMEM),
             gtok=(block, F32, VMEM),
-            rgate=((8, rows, unit), BF, VMEM),
-            rup=((8, rows, unit), BF, VMEM),
-            r1=((8, rows, w), BF, VMEM),
-            r2=((8, rows, 2 * w), BF, VMEM),
-            ro=((rows, width), BF, VMEM),
-            totals=((8, 8, w), F32, VMEM),
+            g_in=((rows, width), F32, VMEM),
+            g_forget=((rows, width), F32, VMEM),
+            g_og=((rows, width), F32, VMEM),
+            g_out=((rows, width), F32, VMEM),
+            g_gate=((rows, hidden_width), F32, VMEM),
+            g_up=((rows, hidden_width), F32, VMEM),
+            g_table=(bound_table.shape, F32, VMEM),
+            gains=((8, width), F32, VMEM),
         ),
         scratch(
+            rgate=((8, rows, unit), BF),
+            rup=((8, rows, unit), BF),
+            r1=((8, rows, w), BF),
+            r2=((8, rows, 2 * w), BF),
+            ro=((rows, width), BF),
+            totals=((8, 8, w), F32),
             states=(column, F32),
             forget=(column, F32),
             proj=((8 * n, 3 * w), F32),
@@ -1453,30 +1527,34 @@
         30,
     )
 
-    def join(m):
-        m = m.transpose(1, 0, 2)
-        return m.reshape(rows, 8 * m.shape[2]).astype(F32)
-
-    def unspread(m):
-        m = m.reshape(8, rows, 16, padded)[:, :, :, :down].transpose(1, 2, 0, 3)
-        return m.reshape(rows, hidden_width).astype(F32)
-
-    sums = D.totals.transpose(1, 0, 2).reshape(8, width)
-    pullback = jax.vjp(lambda table: bound_value(table, layer_idx), bound_table)[1]
+    moved = (D.result, D.gtok, D.g_in, D.g_forget, D.g_og, D.g_out, D.g_gate, D.g_up, D.g_table)
+    like = [jax.ShapeDtypeStruct(m.shape, m.dtype) for m in moved]
+    row = jax.ShapeDtypeStruct((1, width), F32)
+    last = pl.pallas_call(
+        write_body,
+        name="write",
+        out_shape=like + [jax.ShapeDtypeStruct((down, width), F32), row, row, row],
+        in_specs=[ANY] * len(moved) + [VMEM] * 2,
+        out_specs=[VMEM] * (len(moved) + 4),
+        scratch_shapes=[pltpu.SemaphoreType.DMA((len(moved),))],
+        compiler_params=pltpu.CompilerParams(vmem_limit_bytes=60 << 20),
+    )(*moved, D.gains, C.block_ddn)
+    result, grad_tokens, g_in, g_forget, g_og, g_out, g_gate, g_up, g_table, g_down = last[:10]
+    attn, norm, mlp = [m[0] for m in last[10:]]
     return (
-        D.result,
-        D.gtok,
-        sums[0],
-        join(D.r2[:, :, :w]),
-        join(D.r2[:, :, w:]),
-        join(D.r1),
-        D.ro.astype(F32),
-        sums[2],
-        sums[1],
-        unspread(D.rgate),
-        unspread(D.rup),
-        C.block_ddn[:down].astype(F32),
-        pullback(sums[3])[0],
+        result,
+        grad_tokens,
+        attn,
+        g_in,
+        g_forget,
+        g_og,
+        g_out,
+        norm,
+        mlp,
+        g_gate,
+        g_up,
+        g_down,
+        g_table,
     )
 
 

time: 334 us -> 312 us (0.934)
  local copies, waits for them, and re-layouts: 19.6 us -> 1.62 us
  other arithmetic: 6.32 us -> 0 us
    reshape x8 -> x0, local copies, waits for them, and re-layouts: 8.04 us -> none  [the longest x4 4.95 us: spread(): m = m.reshape(rows, 16, 8, down)]
    convert_element_type x7 -> x0, local copies, waits for them, and re-layouts: 5.88 us -> none  [the longest x4 3.89 us: unspread(): return m.reshape(rows, hidden_width).astype(F32)]
    pallas_call x0 -> x1, Pallas kernels: none -> 4.57 us  [on_device(): pl.pallas_call(write_body, name='write', out_shape=like + [jax.ShapeDtype...]
where the time goes in v6:
time: 312 us
  Pallas kernels  309 us (99%)
    pallas_call x4, Pallas kernels, call(): pl.pallas_call(run_body, name=name, out_shape=[jax.ShapeDtypeStruct(*v[:2...  304 us

profile of v6, /device:TPU:1, one launch (start us, length us, event | category | flops | bytes accessed | tf_op | source)
XLA Modules:
  0.0 312.1 jit_solution(2592376372461944325)
XLA Ops:
  1.3 1.6 pad.4.refs_6_
  2.9 49.3 %gather.1 = (bf16[2,2,4,128,768]{4,3,2,1,0:T(8,128)(2,1)}, bf16[2,2,4,16,2048]{4,3,2,1,0:T(8,128)(2,1)}, bf16[1024,2048]{1,0:T(8,128)(2,1)}, bf16[4,48,1024]{2,1,0:T(8,128)(2,1)}, bf16[2,2,48,1024]{3,2,1,0:T(8,128)(2,1)}) custom-call(bf16[128,2048]{1,0:T(8,128)(2,1)} %refs_0_.7, f32[1,2048]{1,0:T(1,128)} %bitcast.19, bf16[16,2048]{1,0:T(8,128)(2,1)} %refs_2_.1, ...), custom_call_target="tpu_custom_call" | custom-call | tf_op jit(solution)/shard_map/gather/pallas_call | solution.py:575
  52.3 45.5 %scan.1 = (bf16[1024,256]{1,0:T(8,128)(2,1)}, f32[2,1024,128]{2,1,0:T(8,128)}, f32[2,1024,128]{2,1,0:T(8,128)}, f32[1024,768]{1,0:T(8,128)}, f32[8,128]{1,0:T(8,...) custom-call(f32[24,2048]{1,0:T(8,128)} %refs_5_.3, ...), custom_call_target="tpu_custom_call" | custom-call | tf_op jit(solution)/shard_map/scan/pallas_call | solution.py:575
  97.8 118.4 %feed.1 = (f32[128,2048]{1,0:T(8,128)}, f32[128,2048]{1,0:T(8,128)}, bf16[1024,2048]{1,0:T(8,128)(2,1)}, bf16[1024,2048]{1,0:T(8,128)(2,1)}, f32[8,2048]{1,0:T(8...) custom-call(bf16[128,2048]{1,0:T(8,128)(2,1)} %refs_0_.7, ...), custom_call_target="tpu_custom_call" | custom-call | tf_op jit(solution)/shard_map/feed/pallas_call | solution.py:575
  216.2 91.2 %back.1 = (bf16[128,2048]{1,0:T(8,128)(2,1)}, f32[128,2048]{1,0:T(8,128)}, f32[16,2048]{1,0:T(8,128)}, f32[16,2048]{1,0:T(8,128)}, f32[16,2048]{1,0:T(8,128)}, /...) custom-call(bf16[128,2048]{1,0:T(8,128)(2,1)} %refs_0_.7, ...), custom_call_target="tpu_custom_call" | custom-call | tf_op jit(solution)/shard_map/back/pallas_call | solution.py:575
  307.4 4.6 %write.1 = (bf16[128,2048]{1,0:T(8,128)(2,1)}, f32[128,2048]{1,0:T(8,128)}, f32[16,2048]{1,0:T(8,128)}, f32[16,2048]{1,0:T(8,128)}, f32[16,2048]{1,0:T(8,128)}, ...) custom-call(bf16[128,2048]{1,0:T(8,128)(2,1)} %get-tuple-element.87., ...), custom_call_target="tpu_custom_call" | custom-call | tf_op jit(solution)/shard_map/write/pallas_call | solution.py:1533

commit v7 on v6

--- a/solution.py
+++ b/solution.py
@@ -931,8 +931,6 @@
         yy = lax.rem(y + 4 - s, 4)
         gather.ready(s)
         forward(yy)
-        if i < 3:
-            gather.forward(order[i + 1])
         if i > 1:
             back = (4 - order[i - 1]) % 4
             second.add(back, R.ps, 128 * (second.chip(back) + c))
@@ -941,6 +939,8 @@
         if i > 1:
             stores[i - 2].wait()
         result(yy, i % 2)
+        for ahead in ((1, 3), (2,), (), ())[i]:
+            gather.forward(ahead)
     second.add(2, R.ps, 128 * (second.chip(2) + c))
 
     def grad_down(j, carry):
@@ -1095,10 +1095,6 @@
     lax.fori_loop(0, width // 512, grad_out, 0)
     outs = plane_sum(cp, R.do, by_columns(*R.do.shape[3:]), *plane_refs(R, "b"), R.oo)
     next(outs)
-    load_x.wait()
-    grad_weights(R, 2 * w, R.d1)
-    one = plane_sum(cp, R.d1, by_rows(*R.d1.shape[3:]), *plane_refs(R, "d"), R.o1)
-    next(one)
     for copy in small:
         copy.wait_recv()
     total = R.rows8[0]
@@ -1142,6 +1138,10 @@
     R.mine[...] = jnp.broadcast_to(e, (8, w))
     k = ax("xhi") * 4 + ax("z")
     small = share(cp, R.mine, R.chain, k, peers_chain)
+    load_x.wait()
+    grad_weights(R, 2 * w, R.d1)
+    one = plane_sum(cp, R.d1, by_rows(*R.d1.shape[3:]), *plane_refs(R, "d"), R.o1)
+    next(one)
     next(up)
     next(outs)
     for copy in small:
@@ -1173,10 +1173,6 @@
     lax.fori_loop(0, 8, last, 0)
     for copy in load_last:
         copy.wait()
-    grad_weights(R, 0, R.d2)
-    two = plane_sum(cp, R.d2, by_rows(*R.d2.shape[3:]), *plane_refs(R, "c"), R.o2)
-    next(two)
-    next(one)
     R.va[...] = jnp.zeros_like(R.va)
     R.va[1:2, :] = R.ffn_sums[0:1, :]
     first = RelaySum(cp, R.near, R.far)
@@ -1199,6 +1195,10 @@
         if i > 0:
             back = order[i - 1]
             first.add(back, R.fp, 128 * (first.chip(back) + c))
+    grad_weights(R, 0, R.d2)
+    two = plane_sum(cp, R.d2, by_rows(*R.d2.shape[3:]), *plane_refs(R, "c"), R.o2)
+    next(two)
+    next(one)
     first.relay(R.fp, 128 * (first.chip(1) + c), 128 * (first.chip(3) + c))
 
     gains = []

time: 312 us -> 300 us (0.962)
  Pallas kernels: 309 us -> 297 us
    pallas_call x4, Pallas kernels: 304 us -> 292 us  [call(): pl.pallas_call(run_body, name=name, out_shape=[jax.ShapeDtypeStruct(*v[:2...]
where the time goes in v7:
time: 300 us
  Pallas kernels  297 us (99%)
    pallas_call x4, Pallas kernels, call(): pl.pallas_call(run_body, name=name, out_shape=[jax.ShapeDtypeStruct(*v[:2...  292 us

profile of v7, /device:TPU:1, one launch (start us, length us, event | category | flops | bytes accessed | tf_op | source)
XLA Modules:
  0.0 300.0 jit_solution(14646262996353330424)
XLA Ops:
  1.3 1.6 pad.4.refs_6_
  2.9 49.3 %gather.1 = (bf16[2,2,4,128,768]{4,3,2,1,0:T(8,128)(2,1)}, bf16[2,2,4,16,2048]{4,3,2,1,0:T(8,128)(2,1)}, bf16[1024,2048]{1,0:T(8,128)(2,1)}, bf16[4,48,1024]{2,1,0:T(8,128)(2,1)}, bf16[2,2,48,1024]{3,2,1,0:T(8,128)(2,1)}) custom-call(bf16[128,2048]{1,0:T(8,128)(2,1)} %refs_0_.7, f32[1,2048]{1,0:T(1,128)} %bitcast.19, bf16[16,2048]{1,0:T(8,128)(2,1)} %refs_2_.1, ...), custom_call_target="tpu_custom_call" | custom-call | tf_op jit(solution)/shard_map/gather/pallas_call | solution.py:575
  52.3 45.5 %scan.1 = (bf16[1024,256]{1,0:T(8,128)(2,1)}, f32[2,1024,128]{2,1,0:T(8,128)}, f32[2,1024,128]{2,1,0:T(8,128)}, f32[1024,768]{1,0:T(8,128)}, f32[8,128]{1,0:T(8,...) custom-call(f32[24,2048]{1,0:T(8,128)} %refs_5_.3, ...), custom_call_target="tpu_custom_call" | custom-call | tf_op jit(solution)/shard_map/scan/pallas_call | solution.py:575
  97.8 115.6 %feed.1 = (f32[128,2048]{1,0:T(8,128)}, f32[128,2048]{1,0:T(8,128)}, bf16[1024,2048]{1,0:T(8,128)(2,1)}, bf16[1024,2048]{1,0:T(8,128)(2,1)}, f32[8,2048]{1,0:T(8...) custom-call(bf16[128,2048]{1,0:T(8,128)(2,1)} %refs_0_.7, ...), custom_call_target="tpu_custom_call" | custom-call | tf_op jit(solution)/shard_map/feed/pallas_call | solution.py:575
  213.4 81.8 %back.1 = (bf16[128,2048]{1,0:T(8,128)(2,1)}, f32[128,2048]{1,0:T(8,128)}, f32[16,2048]{1,0:T(8,128)}, f32[16,2048]{1,0:T(8,128)}, f32[16,2048]{1,0:T(8,128)}, /...) custom-call(bf16[128,2048]{1,0:T(8,128)(2,1)} %refs_0_.7, ...), custom_call_target="tpu_custom_call" | custom-call | tf_op jit(solution)/shard_map/back/pallas_call | solution.py:575
  295.3 4.6 %write.1 = (bf16[128,2048]{1,0:T(8,128)(2,1)}, f32[128,2048]{1,0:T(8,128)}, f32[16,2048]{1,0:T(8,128)}, f32[16,2048]{1,0:T(8,128)}, f32[16,2048]{1,0:T(8,128)}, ...) custom-call(bf16[128,2048]{1,0:T(8,128)(2,1)} %get-tuple-element.87., ...), custom_call_target="tpu_custom_call" | custom-call | tf_op jit(solution)/shard_map/write/pallas_call | solution.py:1533

commit v8 on v7

--- a/solution.py
+++ b/solution.py
@@ -637,6 +637,8 @@
         return carry
 
     lax.fori_loop(0, R.tok.shape[0] // 16, norm, 0)
+    last = jnp.zeros((R.dn_pad.shape[0] - R.dn.shape[0], R.dn.shape[1]), F32)
+    R.dn_pad[...] = jnp.concatenate([R.dn[...].astype(F32), last], axis=0).astype(BF)
     meet()
     me = (ax("xlo"), ax("xhi"), ax("z"))
     third = R.w_in.shape[1] // 8
@@ -652,7 +654,7 @@
     q = shuffle.to[0]
     at = (lax.div(q, 8), lax.rem(lax.div(q, 4), 2), lax.rem(q, 4))
     moved = shuffle.start(cp, R.w_o, R.bo.at[at])
-    dn = plane_first(cp, R.dn, R.dn_column, R.dn_row, by_columns(*R.dn.shape))
+    dn = plane_first(cp, R.dn_pad, R.dn_column, R.dn_row, by_columns(*R.dn_pad.shape))
     next(dn)
     own = cp.local(R.first, R.fi.at[block_of(g)])
     chain = GroupGather(cp, R.first, R.fi)
@@ -1302,7 +1304,6 @@
     unit = 16 * padded
     w = width // 8
 
-    dn = jnp.pad(w_down, ((0, padded - down), (0, 0)))
     gains = attn_gain[None, :]
     full = (8 * n, width)
     block = (n, width)
@@ -1318,7 +1319,7 @@
             w_f=(w_forget, VMEM),
             w_og=(w_outgate, VMEM),
             w_o=(w_out, VMEM),
-            dn=(dn, VMEM),
+            dn=(w_down, VMEM),
         ),
         dict(
             b3=((2, 2, 4, 8 * rows, 3 * w), BF, ANY),
@@ -1327,7 +1328,7 @@
             dn_column=((4, padded, width // 2), BF, ANY),
             dn_row=((2, 2, padded, width // 2), BF, ANY),
         ),
-        scratch(first=(block, BF)),
+        scratch(first=(block, BF), dn_pad=((padded, width), BF)),
         96,
         10,
     )

time: 300 us -> 299 us (level)
  no operation moved by 1% of the time
where the time goes in v8:
time: 299 us; the launch traced here: 298 us
  Pallas kernels  297 us (99%)
    pallas_call x4, Pallas kernels, call(): pl.pallas_call(run_body, name=name, out_shape=[jax.ShapeDtypeStruct(*v[:2...  292 us

profile of v8, /device:TPU:1, one launch (start us, length us, event | category | flops | bytes accessed | tf_op | source)
XLA Modules:
  0.0 298.3 jit_solution(10444399586395533628)
XLA Ops:
  1.3 49.4 %gather.1 = (bf16[2,2,4,128,768]{4,3,2,1,0:T(8,128)(2,1)}, bf16[2,2,4,16,2048]{4,3,2,1,0:T(8,128)(2,1)}, bf16[1024,2048]{1,0:T(8,128)(2,1)}, bf16[4,48,1024]{2,1,0:T(8,128)(2,1)}, bf16[2,2,48,1024]{3,2,1,0:T(8,128)(2,1)}) custom-call(bf16[128,2048]{1,0:T(8,128)(2,1)} %refs_0_.7, f32[1,2048]{1,0:T(1,128)} %bitcast.19, bf16[16,2048]{1,0:T(8,128)(2,1)} %refs_2_.1, ...), custom_call_target="tpu_custom_call" | custom-call | tf_op jit(solution)/shard_map/gather/pallas_call | solution.py:575
  50.7 45.5 %scan.1 = (bf16[1024,256]{1,0:T(8,128)(2,1)}, f32[2,1024,128]{2,1,0:T(8,128)}, f32[2,1024,128]{2,1,0:T(8,128)}, f32[1024,768]{1,0:T(8,128)}, f32[8,128]{1,0:T(8,...) custom-call(f32[24,2048]{1,0:T(8,128)} %refs_5_.3, ...), custom_call_target="tpu_custom_call" | custom-call | tf_op jit(solution)/shard_map/scan/pallas_call | solution.py:575
  96.2 115.6 %feed.1 = (f32[128,2048]{1,0:T(8,128)}, f32[128,2048]{1,0:T(8,128)}, bf16[1024,2048]{1,0:T(8,128)(2,1)}, bf16[1024,2048]{1,0:T(8,128)(2,1)}, f32[8,2048]{1,0:T(8...) custom-call(bf16[128,2048]{1,0:T(8,128)(2,1)} %refs_0_.7, ...), custom_call_target="tpu_custom_call" | custom-call | tf_op jit(solution)/shard_map/feed/pallas_call | solution.py:575
  211.9 81.7 %back.1 = (bf16[128,2048]{1,0:T(8,128)(2,1)}, f32[128,2048]{1,0:T(8,128)}, f32[16,2048]{1,0:T(8,128)}, f32[16,2048]{1,0:T(8,128)}, f32[16,2048]{1,0:T(8,128)}, /...) custom-call(bf16[128,2048]{1,0:T(8,128)(2,1)} %refs_0_.7, ...), custom_call_target="tpu_custom_call" | custom-call | tf_op jit(solution)/shard_map/back/pallas_call | solution.py:575
  293.6 4.6 %write.1 = (bf16[128,2048]{1,0:T(8,128)(2,1)}, f32[128,2048]{1,0:T(8,128)}, f32[16,2048]{1,0:T(8,128)}, f32[16,2048]{1,0:T(8,128)}, f32[16,2048]{1,0:T(8,128)}, ...) custom-call(bf16[128,2048]{1,0:T(8,128)(2,1)} %get-tuple-element.87., ...), custom_call_target="tpu_custom_call" | custom-call | tf_op jit(solution)/shard_map/write/pallas_call | solution.py:1534
